TPU v7x, 32 devices: a whole 2x2x4 slice. The times are simulated.
32 devices in a mesh: rep: 4 (over x, core), shard: 8 (over z, y).
Axes of the slice: x: 2, y: 2, z: 4, core: 2. Of those that a mesh axis runs over, the one named last changes fastest.
Arguments:
- token_ids: int32 [4096], P(('rep', 'shard')), may hold values from 0 to 49151
- target_ids: int32 [4096], P(('rep', 'shard')), may hold values from 0 to 49151
- loss_mask: int32 [4096], P(('rep', 'shard')), may hold values from 0 to 1
- table_master: float32 [49152, 960], P('shard'), may hold values from -1 to 1
- attn_in_master: float32 [1, 960, 1600], P(None, 'shard'), may hold values from -0.1875 to 0.1875
- attn_out_master: float32 [1, 960, 960], P(None, 'shard'), may hold values from -1.5 to 1.5
- mlp_in_master: float32 [1, 960, 5120], P(None, 'shard'), may hold values from -0.1875 to 0.1875
- mlp_out_master: float32 [1, 2560, 960], P(None, 'shard'), may hold values from -0.125 to 0.125
- gain_master: float32 [3, 960], P(None, 'shard'), may hold values from 0.5 to 2.1
- table_first: float32 [49152, 960], P('shard'), may hold values from -1 to 1
- attn_in_first: float32 [1, 960, 1600], P(None, 'shard'), may hold values from -1 to 1
- attn_out_first: float32 [1, 960, 960], P(None, 'shard'), may hold values from -1 to 1
- mlp_in_first: float32 [1, 960, 5120], P(None, 'shard'), may hold values from -1 to 1
- mlp_out_first: float32 [1, 2560, 960], P(None, 'shard'), may hold values from -1 to 1
- gain_first: float32 [3, 960], P(None, 'shard'), may hold values from -1 to 1
- table_second: float32 [49152, 960], P('shard'), may hold values from 0 to 1
- attn_in_second: float32 [1, 960, 1600], P(None, 'shard'), may hold values from 0 to 1
- attn_out_second: float32 [1, 960, 960], P(None, 'shard'), may hold values from 0 to 1
- mlp_in_second: float32 [1, 960, 5120], P(None, 'shard'), may hold values from 0 to 1
- mlp_out_second: float32 [1, 2560, 960], P(None, 'shard'), may hold values from 0 to 1
- gain_second: float32 [3, 960], P(None, 'shard'), may hold values from 0 to 1
Outputs:
- loss_sum: float32 [], replicated
- valid_count: float32 [], replicated
- grad_norm: float32 [], replicated
- table_new: float32 [49152, 960], P('shard')
- table_first_new: float32 [49152, 960], P('shard')
- table_second_new: float32 [49152, 960], P('shard')
- table_copy: bfloat16 [49152, 960], P('shard')
- attn_in_new: float32 [1, 960, 1600], P(None, 'shard')
- attn_in_first_new: float32 [1, 960, 1600], P(None, 'shard')
- attn_in_second_new: float32 [1, 960, 1600], P(None, 'shard')
- attn_in_copy: bfloat16 [1, 960, 1600], P(None, 'shard')
- attn_out_new: float32 [1, 960, 960], P(None, 'shard')
- attn_out_first_new: float32 [1, 960, 960], P(None, 'shard')
- attn_out_second_new: float32 [1, 960, 960], P(None, 'shard')
- attn_out_copy: bfloat16 [1, 960, 960], P(None, 'shard')
- mlp_in_new: float32 [1, 960, 5120], P(None, 'shard')
- mlp_in_first_new: float32 [1, 960, 5120], P(None, 'shard')
- mlp_in_second_new: float32 [1, 960, 5120], P(None, 'shard')
- mlp_in_copy: bfloat16 [1, 960, 5120], P(None, 'shard')
- mlp_out_new: float32 [1, 2560, 960], P(None, 'shard')
- mlp_out_first_new: float32 [1, 2560, 960], P(None, 'shard')
- mlp_out_second_new: float32 [1, 2560, 960], P(None, 'shard')
- mlp_out_copy: bfloat16 [1, 2560, 960], P(None, 'shard')
- gain_new: float32 [3, 960], P(None, 'shard')
- gain_first_new: float32 [3, 960], P(None, 'shard')
- gain_second_new: float32 [3, 960], P(None, 'shard')
- gain_copy: bfloat16 [3, 960], P(None, 'shard')
All inputs are finite; a program needn't handle non-finite values.
Results may differ from a plain program's by a relative error of at most 0.01.
The roundings to bfloat16 on the way count: a program that leaves them out, or rounds other values in their place, can miss the bound.
Values may be sent and summed in bfloat16 or wider, within the bound.
No kernel may reach another device: no remote copies, remote signals or barrier semaphores. Data moves between devices by JAX's collectives and lax.ppermute only.
A program may use at most 576 MiB of HBM per device.

v0:
```python
import jax
import jax.numpy as jnp
from jax import lax
from jax.sharding import PartitionSpec as P

D = 960
HEADS = 15
KV_HEADS = 5
HEAD_DIM = 64
FF = 2560
LAYERS = 1
BLOCK = 256
STEP = 5


EPS_NORM = 1e-05
ROPE_BASE = 100000.0
BETA_ONE = 0.5
BETA_TWO = 0.5
DECAY = 0.1
CLIP_AT = 0.01
ADAM_EPS = 1e-08


def merged(value, axis, join):
    pieces = jax.tree.map(lambda part: lax.all_gather(part, axis), value)
    head = jax.tree.map(lambda part: part[0], pieces)
    tail = jax.tree.map(lambda part: part[1:], pieces)
    total, _ = lax.scan(lambda total, piece: (join(total, piece), None), head, tail)
    return total


def rms_norm(values, gain):
    return values * lax.rsqrt(jnp.mean(values * values, axis=-1, keepdims=True) + EPS_NORM) * gain


def rotate(values, positions):
    half_dim = values.shape[-1] // 2
    freqs = ROPE_BASE ** (-2.0 * jnp.arange(half_dim).astype(jnp.float32) / values.shape[-1])
    angles = positions.astype(jnp.float32)[:, None] * freqs[None, :]
    cosine = jnp.cos(angles)[:, None, :]
    sine = jnp.sin(angles)[:, None, :]
    first_half = values[..., :half_dim]
    second_half = values[..., half_dim:]
    return jnp.concatenate(
        [first_half * cosine - second_half * sine, second_half * cosine + first_half * sine],
        axis=-1,
    )


def swiglu(gate_up):
    half_width = gate_up.shape[-1] // 2
    return jax.nn.silu(gate_up[:, :half_width]) * gate_up[:, half_width:]


def rates(seq_len):
    out_fan = max(1, HEADS * HEAD_DIM * 16 // seq_len)
    return (
        0.8 * D ** (-0.5),
        0.5 * D ** (-0.5),
        0.5 * out_fan ** (-0.5),
        0.5 * D ** (-0.5),
        0.5 * FF ** (-0.5),
        0.2,
    )


def adam_update(master, first, second, gradient, rate):
    first_new = BETA_ONE * first + (1.0 - BETA_ONE) * gradient
    second_new = BETA_TWO * second + (1.0 - BETA_TWO) * gradient * gradient
    step_size = (
        first_new
        / (1.0 - BETA_ONE**STEP)
        / (jnp.sqrt(second_new / (1.0 - BETA_TWO**STEP)) + ADAM_EPS)
    )
    master_new = master - rate * (step_size + DECAY * master)
    return (master_new, first_new, second_new, master_new.astype(jnp.bfloat16))


def gather_layer(copies, layer_index):
    return (
        lax.all_gather(copies[1][layer_index], "shard", axis=0, tiled=True),
        lax.all_gather(copies[2][layer_index], "shard", axis=0, tiled=True),
        lax.all_gather(copies[3][layer_index], "shard", axis=0, tiled=True),
        lax.all_gather(copies[4][layer_index], "shard", axis=0, tiled=True),
        lax.all_gather(copies[5], "shard", axis=1, tiled=True),
    )


def gather_again(copies, layer_index):
    return (
        lax.all_gather(copies[1][layer_index], "shard", axis=0, tiled=True),
        lax.all_gather(copies[2][layer_index], "shard", axis=0, tiled=True),
        lax.all_gather(copies[3][layer_index], "shard", axis=0, tiled=True),
        lax.all_gather(copies[4][layer_index], "shard", axis=0, tiled=True),
        lax.all_gather(copies[5], "shard", axis=1, tiled=True),
    )


def head_scores(head_rows, key_rows, query_blocks, key_blocks):
    scores = jnp.einsum(
        "tgd,sd->gts", head_rows, key_rows, preferred_element_type=jnp.float32
    ) * HEAD_DIM ** (-0.5)
    allowed = key_blocks[None, :] <= query_blocks[:, None]
    return (scores, allowed)


def attend_forward(head_rows, key_heads, value_heads, query_blocks, key_blocks):

    def one_head(operands):
        query_part, key_part, value_part = operands
        scores, allowed = head_scores(query_part, key_part, query_blocks, key_blocks)
        scores = jnp.where(allowed[None], scores, -1e30)
        highest = jnp.max(scores, axis=-1, keepdims=True)
        weights = jnp.exp(scores - highest)
        totals = jnp.sum(weights, axis=-1, keepdims=True)
        chances = (weights / totals).astype(jnp.bfloat16)
        output = jnp.einsum("gts,sd->tgd", chances, value_part, preferred_element_type=jnp.float32)
        return (output, (highest + jnp.log(totals))[..., 0])

    return lax.map(one_head, (head_rows, key_heads, value_heads))


def attend_backward(
    head_rows, key_heads, value_heads, query_blocks, key_blocks, log_totals, grad_heads, deltas
):

    def one_head(operands):
        query_part, key_part, value_part, log_part, grad_part, delta_part = operands
        scores, allowed = head_scores(query_part, key_part, query_blocks, key_blocks)
        chances = jnp.where(allowed[None], jnp.exp(scores - log_part[..., None]), 0.0)
        grad_chances = jnp.einsum(
            "tgd,sd->gts", grad_part, value_part, preferred_element_type=jnp.float32
        )
        grad_scores = (chances * (grad_chances - delta_part[..., None])).astype(jnp.bfloat16)
        scale = HEAD_DIM ** (-0.5)
        grad_queries = (
            jnp.einsum("gts,sd->tgd", grad_scores, key_part, preferred_element_type=jnp.float32)
            * scale
        )
        grad_keys = (
            jnp.einsum("gts,tgd->sd", grad_scores, query_part, preferred_element_type=jnp.float32)
            * scale
        )
        grad_values = jnp.einsum(
            "gts,tgd->sd",
            chances.astype(jnp.bfloat16),
            grad_part,
            preferred_element_type=jnp.float32,
        )
        return (grad_queries, grad_keys, grad_values)

    return lax.map(one_head, (head_rows, key_heads, value_heads, log_totals, grad_heads, deltas))


def project_in(values, weights, gain_one, positions):
    query_width = HEADS * HEAD_DIM
    key_width = KV_HEADS * HEAD_DIM
    tokens_here = values.shape[0]
    normed, norm_back = jax.vjp(rms_norm, values, gain_one)
    normed_low = normed.astype(jnp.bfloat16)
    mixed = jnp.dot(normed_low, weights[0], preferred_element_type=jnp.float32)
    query_raw = mixed[:, :query_width].reshape(tokens_here, HEADS, HEAD_DIM)
    key_raw = mixed[:, query_width : query_width + key_width].reshape(
        tokens_here, KV_HEADS, HEAD_DIM
    )
    rotated, rope_back = jax.vjp(
        lambda first_part, second_part: (
            rotate(first_part, positions),
            rotate(second_part, positions),
        ),
        query_raw,
        key_raw,
    )
    query_low = rotated[0].astype(jnp.bfloat16)
    key_low = rotated[1].reshape(tokens_here, key_width).astype(jnp.bfloat16)
    value_low = mixed[:, query_width + key_width :].astype(jnp.bfloat16)
    return (normed_low, norm_back, rope_back, query_low, key_low, value_low)


def attend_rest(
    values, sectioned, weights, gain_two, keys_all, values_all, query_blocks, key_blocks
):
    tokens_here = values.shape[0]
    group = HEADS // KV_HEADS
    head_rows = sectioned[3].reshape(tokens_here, KV_HEADS, group, HEAD_DIM).transpose(1, 0, 2, 3)
    key_heads = keys_all.reshape(-1, KV_HEADS, HEAD_DIM).transpose(1, 0, 2)
    value_heads = values_all.reshape(-1, KV_HEADS, HEAD_DIM).transpose(1, 0, 2)
    outputs, log_totals = attend_forward(
        head_rows, key_heads, value_heads, query_blocks, key_blocks
    )
    attended_low = (
        outputs.transpose(1, 0, 2, 3).reshape(tokens_here, HEADS * HEAD_DIM).astype(jnp.bfloat16)
    )
    middle = values + jnp.dot(attended_low, weights[1], preferred_element_type=jnp.float32)
    normed, norm_back = jax.vjp(rms_norm, middle, gain_two)
    normed_low = normed.astype(jnp.bfloat16)
    gate_up = jnp.dot(normed_low, weights[2], preferred_element_type=jnp.float32)
    hidden, glu_back = jax.vjp(swiglu, gate_up)
    hidden_low = hidden.astype(jnp.bfloat16)
    result = middle + jnp.dot(hidden_low, weights[3], preferred_element_type=jnp.float32)
    return (
        result,
        (
            head_rows,
            key_heads,
            value_heads,
            outputs,
            log_totals,
            attended_low,
            norm_back,
            normed_low,
            glu_back,
            hidden_low,
        ),
    )


def layer_back(grad_output, sectioned, saved, weights, query_blocks, key_blocks):
    normed_one, norm_one_back, rope_back = (sectioned[0], sectioned[1], sectioned[2])
    (
        head_rows,
        key_heads,
        value_heads,
        outputs,
        log_totals,
        attended_low,
        norm_two_back,
        normed_two,
        glu_back,
        hidden_low,
    ) = saved
    tokens_here = grad_output.shape[0]
    group = HEADS // KV_HEADS
    grad_branch = grad_output.astype(jnp.bfloat16)
    grad_down = jnp.einsum("tf,td->fd", hidden_low, grad_branch, preferred_element_type=jnp.float32)
    grad_hidden = jnp.einsum(
        "td,fd->tf", grad_branch, weights[3], preferred_element_type=jnp.float32
    )
    grad_gate_up = glu_back(grad_hidden)[0].astype(jnp.bfloat16)
    grad_up_in = jnp.einsum(
        "td,tf->df", normed_two, grad_gate_up, preferred_element_type=jnp.float32
    )
    grad_normed_two = jnp.einsum(
        "tf,df->td", grad_gate_up, weights[2], preferred_element_type=jnp.float32
    )
    grad_middle_part, grad_gain_two = norm_two_back(grad_normed_two)
    grad_middle = grad_output + grad_middle_part
    grad_attn_branch = grad_middle.astype(jnp.bfloat16)
    grad_out_proj = jnp.einsum(
        "tq,td->qd", attended_low, grad_attn_branch, preferred_element_type=jnp.float32
    )
    grad_attended = jnp.einsum(
        "td,qd->tq", grad_attn_branch, weights[1], preferred_element_type=jnp.float32
    ).astype(jnp.bfloat16)
    grad_heads = grad_attended.reshape(tokens_here, KV_HEADS, group, HEAD_DIM).transpose(1, 0, 2, 3)
    deltas = jnp.einsum("ktgd,ktgd->kgt", grad_heads.astype(jnp.float32), outputs)
    grad_rows, grad_key_heads, grad_value_heads = attend_backward(
        head_rows, key_heads, value_heads, query_blocks, key_blocks, log_totals, grad_heads, deltas
    )
    seq_len = key_heads.shape[1]
    grad_keys, grad_values = (
        lax.psum_scatter(
            grad_key_heads.transpose(1, 0, 2).reshape(seq_len, -1),
            "shard",
            scatter_dimension=0,
            tiled=True,
        ),
        lax.psum_scatter(
            grad_value_heads.transpose(1, 0, 2).reshape(seq_len, -1),
            "shard",
            scatter_dimension=0,
            tiled=True,
        ),
    )
    grad_queries = grad_rows.transpose(1, 0, 2, 3).reshape(tokens_here, HEADS, HEAD_DIM)
    grad_query_raw, grad_key_raw = rope_back(
        (grad_queries, grad_keys.reshape(tokens_here, KV_HEADS, HEAD_DIM))
    )
    grad_mixed = jnp.concatenate(
        [
            grad_query_raw.reshape(tokens_here, -1),
            grad_key_raw.reshape(tokens_here, -1),
            grad_values,
        ],
        axis=1,
    ).astype(jnp.bfloat16)
    grad_attn_in = jnp.einsum(
        "td,tf->df", normed_one, grad_mixed, preferred_element_type=jnp.float32
    )
    grad_normed_one = jnp.einsum(
        "tf,df->td", grad_mixed, weights[0], preferred_element_type=jnp.float32
    )
    grad_values_part, grad_gain_one = norm_one_back(grad_normed_one)
    return (
        grad_middle + grad_values_part,
        (grad_attn_in, grad_out_proj, grad_up_in, grad_down),
        grad_gain_one,
        grad_gain_two,
    )


def local(
    token_ids,
    target_ids,
    loss_mask,
    table_master,
    attn_in_master,
    attn_out_master,
    mlp_in_master,
    mlp_out_master,
    gain_master,
    table_first,
    attn_in_first,
    attn_out_first,
    mlp_in_first,
    mlp_out_first,
    gain_first,
    table_second,
    attn_in_second,
    attn_out_second,
    mlp_in_second,
    mlp_out_second,
    gain_second,
):
    masters = (
        table_master,
        attn_in_master,
        attn_out_master,
        mlp_in_master,
        mlp_out_master,
        gain_master,
    )
    firsts = (table_first, attn_in_first, attn_out_first, mlp_in_first, mlp_out_first, gain_first)
    seconds = (
        table_second,
        attn_in_second,
        attn_out_second,
        mlp_in_second,
        mlp_out_second,
        gain_second,
    )
    copies = tuple((master.astype(jnp.bfloat16) for master in masters))
    tok_rows = token_ids.shape[0]
    my_shard = lax.axis_index("shard")
    positions = my_shard * tok_rows + jnp.arange(tok_rows, dtype=jnp.int32)
    group_ids, group_targets, group_mask = (
        lax.all_gather(token_ids, "shard", axis=0, tiled=True),
        lax.all_gather(target_ids, "shard", axis=0, tiled=True),
        lax.all_gather(loss_mask, "shard", axis=0, tiled=True),
    )
    seq_len = group_ids.shape[0]
    key_blocks = jnp.arange(seq_len, dtype=jnp.int32) // BLOCK
    query_blocks = positions // BLOCK
    table_low = copies[0]
    vocab_rows = table_low.shape[0]
    vocab_start = my_shard * vocab_rows
    local_ids = group_ids - vocab_start
    inside = (local_ids >= 0) & (local_ids < vocab_rows)
    clipped_ids = jnp.clip(local_ids, 0, vocab_rows - 1)
    looked = jnp.where(inside[:, None], table_low[clipped_ids], jnp.zeros((), jnp.bfloat16))
    values = lax.psum_scatter(looked, "shard", scatter_dimension=0, tiled=True).astype(jnp.float32)
    gains_full = None
    layer_index = 0
    weights = gather_layer(copies, layer_index)
    gains_full = weights[4].astype(jnp.float32)
    sectioned = project_in(values, weights, gains_full[2 * layer_index], positions)
    keys_all = lax.all_gather(sectioned[4], "shard", axis=0, tiled=True)
    values_all = lax.all_gather(sectioned[5], "shard", axis=0, tiled=True)
    result, _ = attend_rest(
        values,
        sectioned,
        weights,
        gains_full[2 * layer_index + 1],
        keys_all,
        values_all,
        query_blocks,
        key_blocks,
    )
    kept = [(values, keys_all, values_all, None)]
    final, final_back = jax.vjp(rms_norm, result, gains_full[2 * LAYERS])
    states = lax.all_gather(final.astype(jnp.bfloat16), "shard", axis=0, tiled=True)
    row_block = min(512, seq_len)
    block_count = seq_len // row_block
    state_blocks = states.reshape(block_count, row_block, -1)
    target_blocks = (group_targets - vocab_start).reshape(block_count, row_block)
    vocab_iota = jnp.arange(vocab_rows, dtype=jnp.int32)

    def block_stats(operands):
        state_rows, target_rows = operands
        logits = jnp.einsum("td,vd->tv", state_rows, table_low, preferred_element_type=jnp.float32)
        highest = jnp.max(logits, axis=-1)
        totals = jnp.sum(jnp.exp(logits - highest[:, None]), axis=-1)
        picked = jnp.sum(
            jnp.where(vocab_iota[None, :] == target_rows[:, None], logits, 0.0), axis=-1
        )
        return (highest, totals, picked)

    highs, totals, picks = lax.map(block_stats, (state_blocks, target_blocks))

    def combine(first_part, second_part):
        highest = jnp.maximum(first_part[0], second_part[0])
        summed = first_part[1] * jnp.exp(first_part[0] - highest) + second_part[1] * jnp.exp(
            second_part[0] - highest
        )
        return (highest, summed, first_part[2] + second_part[2])

    highs, totals, picks = merged(
        (highs.reshape(-1), totals.reshape(-1), picks.reshape(-1)), "shard", combine
    )
    log_totals = highs + jnp.log(totals)
    own_log = lax.dynamic_slice_in_dim(log_totals, my_shard * tok_rows, tok_rows)
    own_picks = lax.dynamic_slice_in_dim(picks, my_shard * tok_rows, tok_rows)
    own_mask = loss_mask.astype(jnp.float32)
    loss_sum, valid_count = lax.psum(
        (jnp.sum((own_log - own_picks) * own_mask), jnp.sum(own_mask)), ("rep", "shard")
    )
    weight_blocks = (group_mask.astype(jnp.float32) / valid_count).reshape(block_count, row_block)
    log_blocks = log_totals.reshape(block_count, row_block)

    def block_back(table_grad, operands):
        state_rows, target_rows, log_rows, weight_rows = operands
        logits = jnp.einsum("td,vd->tv", state_rows, table_low, preferred_element_type=jnp.float32)
        chances = jnp.exp(logits - log_rows[:, None])
        onehot = jnp.where(vocab_iota[None, :] == target_rows[:, None], 1.0, 0.0)
        grad_logits = ((chances - onehot) * weight_rows[:, None]).astype(jnp.bfloat16)
        grad_rows = jnp.einsum(
            "tv,vd->td", grad_logits, table_low, preferred_element_type=jnp.float32
        )
        table_grad = table_grad + jnp.einsum(
            "tv,td->vd", grad_logits, state_rows, preferred_element_type=jnp.float32
        )
        return (table_grad, grad_rows)

    table_grad, grad_states = lax.scan(
        block_back,
        jnp.zeros(table_low.shape, jnp.float32),
        (state_blocks, target_blocks, log_blocks, weight_blocks),
    )
    grad_final = lax.psum_scatter(
        grad_states.reshape(seq_len, -1), "shard", scatter_dimension=0, tiled=True
    )
    grad_values, grad_final_gain = final_back(grad_final)
    gain_rows = jnp.arange(2 * LAYERS + 1, dtype=jnp.int32)[:, None]
    pending = jnp.where(gain_rows == 2 * LAYERS, grad_final_gain[None, :], 0.0)
    owned_layers = [None] * LAYERS
    owned_gains = jnp.zeros(gain_master.shape, jnp.float32)
    for layer_index in reversed(range(LAYERS)):
        values_in, keys_all, values_all, weights = kept[layer_index]
        weights = gather_again(copies, layer_index)
        gains_full = weights[4].astype(jnp.float32)
        sectioned = project_in(values_in, weights, gains_full[2 * layer_index], positions)
        _, saved = attend_rest(
            values_in,
            sectioned,
            weights,
            gains_full[2 * layer_index + 1],
            keys_all,
            values_all,
            query_blocks,
            key_blocks,
        )
        grad_values, matrix_grads, grad_gain_one, grad_gain_two = layer_back(
            grad_values, sectioned, saved, weights, query_blocks, key_blocks
        )
        pending = (
            pending
            + jnp.where(gain_rows == 2 * layer_index, grad_gain_one[None, :], 0.0)
            + jnp.where(gain_rows == 2 * layer_index + 1, grad_gain_two[None, :], 0.0)
        )
        reduced = (
            lax.psum_scatter(matrix_grads[0], "shard", scatter_dimension=0, tiled=True),
            lax.psum_scatter(matrix_grads[1], "shard", scatter_dimension=0, tiled=True),
            lax.psum_scatter(matrix_grads[2], "shard", scatter_dimension=0, tiled=True),
            lax.psum_scatter(matrix_grads[3], "shard", scatter_dimension=0, tiled=True),
            lax.psum_scatter(pending, "shard", scatter_dimension=1, tiled=True),
        )
        owned_layers[layer_index] = reduced[:4]
        owned_gains = reduced[4]
        pending = jnp.zeros_like(pending)
    grad_embedded = lax.all_gather(grad_values.astype(jnp.bfloat16), "shard", axis=0, tiled=True)
    table_grad = table_grad.at[clipped_ids].add(
        jnp.where(inside[:, None], grad_embedded.astype(jnp.float32), 0.0)
    )
    stacked = tuple((jnp.stack([owned_layers[0][member]]) for member in range(4)))
    summed = lax.psum(
        (table_grad, stacked[0], stacked[1], stacked[2], stacked[3], owned_gains), "rep"
    )
    squares = jnp.zeros((), jnp.float32)
    for gradient in summed:
        squares = squares + jnp.sum(gradient * gradient)
    grad_norm = jnp.sqrt(lax.psum(squares, "shard"))
    clip_scale = CLIP_AT / jnp.maximum(grad_norm, CLIP_AT)
    results = [loss_sum, valid_count, grad_norm]
    rate_list = rates(seq_len)
    for member in range(6):
        results.extend(
            adam_update(
                masters[member],
                firsts[member],
                seconds[member],
                summed[member] * clip_scale,
                rate_list[member],
            )
        )
    return tuple(results)


def solution(mesh):
    placed = (
        P(("rep", "shard")),
        P(("rep", "shard")),
        P(("rep", "shard")),
        P("shard", None),
        P(None, "shard", None),
        P(None, "shard", None),
        P(None, "shard", None),
        P(None, "shard", None),
        P(None, "shard"),
        P("shard", None),
        P(None, "shard", None),
        P(None, "shard", None),
        P(None, "shard", None),
        P(None, "shard", None),
        P(None, "shard"),
        P("shard", None),
        P(None, "shard", None),
        P(None, "shard", None),
        P(None, "shard", None),
        P(None, "shard", None),
        P(None, "shard"),
    )
    return jax.shard_map(
        local,
        mesh=mesh,
        in_specs=placed,
        out_specs=(
            P(),
            P(),
            P(),
            P("shard", None),
            P("shard", None),
            P("shard", None),
            P("shard", None),
            P(None, "shard", None),
            P(None, "shard", None),
            P(None, "shard", None),
            P(None, "shard", None),
            P(None, "shard", None),
            P(None, "shard", None),
            P(None, "shard", None),
            P(None, "shard", None),
            P(None, "shard", None),
            P(None, "shard", None),
            P(None, "shard", None),
            P(None, "shard", None),
            P(None, "shard", None),
            P(None, "shard", None),
            P(None, "shard", None),
            P(None, "shard", None),
            P(None, "shard"),
            P(None, "shard"),
            P(None, "shard"),
            P(None, "shard"),
        ),
        check_vma=False,
    )
```

profile of v0, /device:TPU:0, one launch (start us, length us, event | category | flops | bytes accessed | tf_op | source)
XLA Modules:
  0.0 2710.4 jit_solution(2323490512694790921)
XLA Ops:
  30.2 24.2 copy.114
  108.6 41.9 %reduce-scatter.26.cloned.1.call-done = bf16[128,960]{1,0:T(8,128)(2,1)} async-done(((bf16[1024,960]{1,0:T(8,128)(2,1)}), bf16[128,960]{1,0:T(8,128)(2,1)}) %reduce-scatter.26.cloned.1.call-update) | async-done | bytes 245776
  151.9 61.3 %all-gather.22.cloned.1.call-done = bf16[1,960,1600]{2,1,0:T(8,128)(2,1)} async-done(((bf16[1,120,1600]{2,1,0:T(8,128)(2,1)}), bf16[1,960,1600]{2,1,0:T(8,128)(2,1)}) %all-gather.22.cloned.1.call-update) | async-done | bytes 3072016 | tf_op jit(solution)/shard_map/all_gather | solution.py:82
  217.0 30.5 %all_gather.53 = bf16[1024,320]{0,1:T(8,128)(2,1)S(1)} all-gather(bf16[128,320]{0,1:T(8,128)(2,1)S(1)} %slice.139), channel_id=1, replica_groups=mesh['rep'=4,'shard'=8] {'shard'}, dimensions={0}, use_global_device_ids=true | all-gather | bytes 737280 | tf_op jit(solution)/shard_map/all_gather | solution.py:369
  247.5 32.4 %all_gather.54 = bf16[1024,320]{0,1:T(8,128)(2,1)S(1)} all-gather(bf16[128,320]{0,1:T(8,128)(2,1)S(1)} %bitcast.422), channel_id=1, replica_groups=mesh['rep'=4,'shard'=8] {'shard'}, dimensions={0}, use_global_device_ids=true | all-gather | bytes 737280 | tf_op jit(solution)/shard_map/all_gather | solution.py:368
  292.8 127.0 %all-gather.26.cloned.1.call-done = bf16[1,960,5120]{2,1,0:T(8,128)(2,1)} async-done(((bf16[1,120,5120]{2,1,0:T(8,128)(2,1)}), bf16[1,960,5120]{2,1,0:T(8,128)(2,1)}) %all-gather.26.cloned.1.call-update) | async-done | bytes 9830416 | tf_op jit(solution)/shard_map/all_gather | solution.py:84
  425.3 81.6 %all-gather.28.cloned.1.call-done = bf16[1,2560,960]{2,1,0:T(8,128)(2,1)} async-done(((bf16[1,320,960]{2,1,0:T(8,128)(2,1)}), bf16[1,2560,960]{2,1,0:T(8,128)(2,1)}) %all-gather.28.cloned.1.call-update) | async-done | bytes 4915216 | tf_op jit(solution)/shard_map/all_gather | solution.py:85
  564.8 40.3 %while.83 = (s32[]{:T(128)}, f32[2,512]{1,0:T(2,128)S(1)}, f32[2,512]{1,0:T(2,128)S(1)}, f32[2,512]{1,0:T(2,128)S(1)}, bf16[2,512,960]{2,1,0:T(8,128)(2,1)}, /*i...) while((s32[]{:T(128)}, f32[2,512]{1,0:T(2,128)S(1)}, ...), condition=%wide.region_12.13_spmd.clone, body=%wide.region_8.12_spmd.clone.sunk | while | flops 6058670592 | bytes 38824056 | solution.py:399
  605.1 30.4 %all-gather.7 = f32[8,1,1024]{2,1,0:T(1,128)S(1)} all-gather(f32[1,1,1024]{2,1,0:T(1,128)S(1)} %reshape.426), channel_id=1, replica_groups=mesh['rep'=4,'shard'=8] {'shard'}, dimensions={0}, use_global_device_ids=true | all-gather | bytes 36864 | tf_op jit(solution)/shard_map/all_gather | solution.py:26
  635.6 30.4 %all-gather.8 = f32[8,1,1024]{2,1,0:T(1,128)S(1)} all-gather(f32[1,1,1024]{2,1,0:T(1,128)S(1)} %reshape.428), channel_id=1, replica_groups=mesh['rep'=4,'shard'=8] {'shard'}, dimensions={0}, use_global_device_ids=true | all-gather | bytes 36864 | tf_op jit(solution)/shard_map/all_gather | solution.py:26
  666.0 30.4 %all-gather.9 = f32[8,1,1024]{2,1,0:T(1,128)S(1)} all-gather(f32[1,1,1024]{2,1,0:T(1,128)S(1)} %reshape.430), channel_id=1, replica_groups=mesh['rep'=4,'shard'=8] {'shard'}, dimensions={0}, use_global_device_ids=true | all-gather | bytes 36864 | tf_op jit(solution)/shard_map/all_gather | solution.py:26
  697.8 37.1 %all-reduce.8 = (f32[]{:T(128)}, f32[]{:T(128)}) all-reduce(f32[]{:T(128)} %get-tuple-element.571, f32[]{:T(128)} %get-tuple-element.570), channel_id=1, replica_groups=mesh['rep'=4,'shard'=8] {'rep','shard'}, use_global_device_ids=true, to_apply=%region_16.17 | all-reduce | flops 2 | bytes 16 | tf_op jit(solution)/shard_map/psum | solution.py:415
  735.6 169.7 %while.86 = (s32[]{:T(128)}, f32[6144,960]{0,1:T(8,128)}, f32[2,512,960]{1,0,2:T(2,128)}, bf16[2,512,960]{2,1,0:T(8,128)(2,1)}, bf16[6144,960]{1,0:T(8,128)(2,1)...) while((s32[]{:T(128)}, f32[6144,960]{0,1:T(8,128)}, ...), condition=%wide.region_20.21_spmd.clone, body=%wide.region_19.20_spmd.clone.sunk | while | flops 18150064128 | bytes 102385800 | solution.py:435
  783.1 35.5 %dynamic_update_slice.70 = f32[2,512,960]{1,0,2:T(2,128)} dynamic-update-slice(f32[2,512,960]{1,0,2:T(2,128)} %get-tuple-element.1128, f32[1,512,960]{1,0,2:T(1,128)S(1)} %copy.186, s32[]{:T(128)S(6)} %copy.230, s32[]{:T(128)} %constant.208.clone.1..sunk.1, s32[]{:T(128)} %constant.208.clone.1..sunk.1) | dynamic-update-slice | bytes 3932164 | tf_op jit(solution)/shard_map/while/body/jit(dynamic_update_index_in_dim)/dynamic_update_slice | solution.py:435
  869.6 35.5 %dynamic_update_slice.70 = f32[2,512,960]{1,0,2:T(2,128)} dynamic-update-slice(f32[2,512,960]{1,0,2:T(2,128)} %get-tuple-element.1128, f32[1,512,960]{1,0,2:T(1,128)S(1)} %copy.186, s32[]{:T(128)S(6)} %copy.230, s32[]{:T(128)} %constant.208.clone.1..sunk.1, s32[]{:T(128)} %constant.208.clone.1..sunk.1) | dynamic-update-slice | bytes 3932164 | tf_op jit(solution)/shard_map/while/body/jit(dynamic_update_index_in_dim)/dynamic_update_slice | solution.py:435
  937.9 58.8 %reduce-scatter.14.cloned.1.call-done = f32[128,960]{0,1:T(8,128)} async-done(((f32[1024,960]{0,1:T(8,128)}), f32[128,960]{0,1:T(8,128)}) %reduce-scatter.14.cloned.1.call-update) | async-done | bytes 491536 | tf_op jit(solution)/shard_map/reduce_scatter | solution.py:440
  1013.6 38.9 %while.85 = (s32[]{:T(128)}, f32[5,128,3,64]{1,3,2,0:T(8,128)S(1)}, f32[5,1024,64]{1,2,0:T(8,128)}, f32[5,1024,64]{1,2,0:T(8,128)}, bf16[5,1024,64]{1,2,0:T(8,12...) while((s32[]{:T(128)}, f32[5,128,3,64]{1,3,2,0:T(8,128)S(1)}, ...), condition=%wide.region_30.31_spmd.clone, body=%wide.region_29.30_spmd.clone.sunk | while | flops 254642176 | bytes 8576645 | solution.py:153
  1053.7 63.7 %reduce-scatter.16.cloned.1.call-done = f32[128,320]{0,1:T(8,128)} async-done(((f32[1024,320]{0,1:T(8,128)}), f32[128,320]{0,1:T(8,128)}) %reduce-scatter.16.cloned.1.call-update) | async-done | bytes 163856 | tf_op jit(solution)/shard_map/reduce_scatter | solution.py:263
  1118.3 67.3 %reduce-scatter.18.cloned.1.call-done = f32[128,320]{0,1:T(8,128)} async-done(((f32[1024,320]{0,1:T(8,128)}), f32[128,320]{0,1:T(8,128)}) %reduce-scatter.18.cloned.1.call-update) | async-done | bytes 163856 | tf_op jit(solution)/shard_map/reduce_scatter | solution.py:269
  1216.9 24.3 copy.121
  1250.4 27.1 scatter_fusion
  1277.5 48.4 %reduce-scatter.20.cloned.1.call-done = f32[120,960]{1,0:T(8,128)} async-done(((f32[960,960]{1,0:T(8,128)}), f32[120,960]{1,0:T(8,128)}) %reduce-scatter.20.cloned.1.call-update) | async-done | bytes 460816 | tf_op jit(solution)/shard_map/reduce_scatter | solution.py:473
  1325.9 124.9 %reduce-scatter.28.cloned.1.call-done = f32[120,1600]{1,0:T(8,128)} async-done(((f32[960,1600]{1,0:T(8,128)}), f32[120,1600]{1,0:T(8,128)}) %reduce-scatter.28.cloned.1.call-update) | async-done | bytes 768016
  1450.8 181.3 %reduce-scatter.24.cloned.1.call-done = f32[320,960]{1,0:T(8,128)} async-done(((f32[2560,960]{1,0:T(8,128)}), f32[320,960]{1,0:T(8,128)}) %reduce-scatter.24.cloned.1.call-update) | async-done | bytes 1228816 | tf_op jit(solution)/shard_map/reduce_scatter | solution.py:475
  1632.0 328.1 %reduce-scatter.22.cloned.1.call-done = f32[120,5120]{1,0:T(8,128)} async-done(((f32[960,5120]{1,0:T(8,128)}), f32[120,5120]{1,0:T(8,128)}) %reduce-scatter.22.cloned.1.call-update) | async-done | bytes 2457616 | tf_op jit(solution)/shard_map/reduce_scatter | solution.py:474
  1960.2 24.3 copy.123
  1985.8 35.1 %all-reduce.7 = f32[3,960]{1,0:T(4,128)S(1)} all-reduce(f32[3,960]{1,0:T(4,128)S(1)} %select_add_fusion.1), channel_id=14, replica_groups=mesh['rep'=4,'shard'=8] {'shard'}, use_global_device_ids=true, to_apply=%region_52.53.clone | all-reduce | flops 2880 | bytes 23040
  2028.4 441.7 %all-reduce.12.cloned.1.call-done = (f32[6144,960]{1,0:T(8,128)}, f32[1,120,1600]{2,1,0:T(8,128)}, f32[1,120,960]{2,1,0:T(8,128)}, f32[1,120,5120]{2,1,0:T(8,128)}, f32[1,320,960]{2,1,0:T(8,128)}) async-done(((f32[6144,960]{1,0:T(8,128)}, f32[1,120,1600]{2,1,0:T(8,128)}, f32[1,120,960]{2,1,0:T(8,128)}, f32[1,120,5120]{2,1,0:T(8,128)}, f32[1,320,960]{2,1,0:T(8,128)}), (f32[6144,960]{1,0:T(8,128)}, ...) | async-done | bytes 28508176 | tf_op jit(solution)/shard_map/psum | solution.py:486
  2490.1 24.1 copy.124
  2536.8 61.7 %fusion.209 = (bf16[6144,960]{1,0:T(8,128)(2,1)}, f32[6144,960]{1,0:T(8,128)}, f32[6144,960]{1,0:T(8,128)}, f32[6144,960]{1,0:T(8,128)}) fusion(f32[6144,960]{1,0:T(8,128)} %copy.114, f32[6144,960]{1,0:T(8,128)} %get-tuple-element.666, f32[]{:T(128)S(6)} %div.181, f32[6144,960]{1,0:T(8,128)} %copy.123, f32[6144,960]{1,0:T(8,128)} %copy.124), kind=kLoop, calls=%fused_computation.314 | loop fusion | flops 94371840 | bytes 176947200 | tf_op jit(solution)/shard_map/convert_element_type | solution.py:77
  2598.5 24.0 copy.127
  2622.5 24.0 copy.128
  (433 shorter events, 558.8 us)
Async XLA Ops:
  7.2 143.4 %reduce-scatter.26.cloned.1.call-start = ((), (), s32[]{:S(2)}) async-start(), calls=%async_computation.20 | async-start | bytes 2359296
  85.5 127.7 %all-gather.22.cloned.1.call-start = ((), (), s32[]{:S(2)}) async-start(), calls=%async_computation.16 | async-start | bytes 3594240 | tf_op jit(solution)/shard_map/all_gather | solution.py:82
  86.4 203.2 %all-gather.24.cloned.1.call-start = ((), (), s32[]{:S(2)}) async-start(), calls=%async_computation.17 | async-start | bytes 2211840 | tf_op jit(solution)/shard_map/all_gather | solution.py:83
  88.2 331.6 %all-gather.26.cloned.1.call-start = ((), (), s32[]{:S(2)}) async-start(), calls=%async_computation.18 | async-start | bytes 11059200 | tf_op jit(solution)/shard_map/all_gather | solution.py:84
  89.5 417.4 %all-gather.28.cloned.1.call-start = ((), (), s32[]{:S(2)}) async-start(), calls=%async_computation.19 | async-start | bytes 5898240 | tf_op jit(solution)/shard_map/all_gather | solution.py:85
  91.8 469.0 %all-gather.18.cloned.1.call-start = ((), (), s32[]{:S(2)}) async-start(), calls=%async_computation.8 | async-start | bytes 2211840 | tf_op jit(solution)/shard_map/all_gather | solution.py:382
  108.4 108.3 %copy-start.39 = (f32[1,960]{1,0:T(1,128)}, f32[1,960]{1,0:T(1,128)S(1)}, u32[]{:S(2)}) copy-start(f32[1,960]{1,0:T(1,128)S(1)} %get-tuple-element.721) | copy-start | bytes 11524
  108.4 311.4 %copy-start.32 = (f32[1,960]{1,0:T(1,128)}, f32[1,960]{1,0:T(1,128)S(1)}, u32[]{:S(2)}) copy-start(f32[1,960]{1,0:T(1,128)S(1)} %get-tuple-element.720) | copy-start | bytes 11524
  108.4 403.0 %copy-start.41 = (f32[1,960]{1,0:T(1,128)}, f32[1,960]{1,0:T(1,128)S(1)}, u32[]{:S(2)}) copy-start(f32[1,960]{1,0:T(1,128)S(1)} %get-tuple-element.719) | copy-start | bytes 11524
  108.6 108.3 %copy-start.35 = (f32[128,32]{0,1:T(8,128)}, f32[128,32]{0,1:T(8,128)S(1)}, u32[]{:S(2)}) copy-start(f32[128,32]{0,1:T(8,128)S(1)} %get-tuple-element.722) | copy-start | bytes 49156
  108.6 108.2 %copy-start.37 = (f32[128,32]{0,1:T(8,128)}, f32[128,32]{0,1:T(8,128)S(1)}, u32[]{:S(2)}) copy-start(f32[128,32]{0,1:T(8,128)S(1)} %get-tuple-element.723) | copy-start | bytes 49156
  151.7 138.7 %copy-start.1 = (bf16[128,960]{0,1:T(8,128)(2,1)}, bf16[128,960]{0,1:T(8,128)(2,1)S(1)}, u32[]{:S(2)}) copy-start(bf16[128,960]{0,1:T(8,128)(2,1)S(1)} %copy.144) | copy-start | bytes 737284
  151.8 64.8 %copy-start.55 = (f32[128]{0:T(128)}, f32[128]{0:T(128)S(1)}, u32[]{:S(2)}) copy-start(f32[128]{0:T(128)S(1)} %fusion.173) | copy-start | bytes 1540
  289.5 130.3 %copy-start.19 = (bf16[5,1024,64]{1,2,0:T(8,128)(2,1)}, bf16[5,1024,64]{1,2,0:T(8,128)(2,1)S(1)}, u32[]{:S(2)}) copy-start(bf16[5,1024,64]{1,2,0:T(8,128)(2,1)S(1)} %get-tuple-element.1259) | copy-start | bytes 1966084
  289.6 130.3 %copy-start.34 = (bf16[5,128,3,64]{1,3,2,0:T(8,128)(2,1)}, bf16[5,128,3,64]{1,3,2,0:T(8,128)(2,1)S(1)}, u32[]{:S(2)}) copy-start(bf16[5,128,3,64]{1,3,2,0:T(8,128)(2,1)S(1)} %get-tuple-element.1275) | copy-start | bytes 737284
  425.3 87.9 %copy-start.57 = (s32[128]{0:T(128)S(1)}, s32[128]{0:T(128)}, u32[]{:S(2)}) copy-start(s32[128]{0:T(128)} %param.34) | copy-start | bytes 1540
  425.3 105.5 %copy-start.52 = (s32[128]{0:T(128)S(1)}, s32[128]{0:T(128)}, u32[]{:S(2)}) copy-start(s32[128]{0:T(128)} %param.35) | copy-start | bytes 1540
  513.1 483.6 %reduce-scatter.14.cloned.1.call-start = ((), (), s32[]{:S(2)}) async-start(), calls=%async_computation.9 | async-start | bytes 4423680 | tf_op jit(solution)/shard_map/reduce_scatter | solution.py:440
  910.3 207.1 %reduce-scatter.16.cloned.1.call-start = ((), (), s32[]{:S(2)}) async-start(), calls=%async_computation.10 | async-start | bytes 1474560 | tf_op jit(solution)/shard_map/reduce_scatter | solution.py:263
  930.7 65.9 %copy-start.10 = (f32[128,960]{0,1:T(8,128)S(1)}, f32[128,960]{0,1:T(8,128)}, u32[]{:S(2)}) copy-start(f32[128,960]{0,1:T(8,128)} %copy-done.9) | copy-start | bytes 1474564
  930.8 65.9 %copy-start.42 = (f32[1,960]{1,0:T(1,128)S(1)}, f32[1,960]{1,0:T(1,128)}, u32[]{:S(2)}) copy-start(f32[1,960]{1,0:T(1,128)} %copy-done.41) | copy-start | bytes 11524
  930.8 65.9 %copy-start.51 = (f32[128]{0:T(128)S(1)}, f32[128]{0:T(128)}, u32[]{:S(2)}) copy-start(f32[128]{0:T(128)} %copy-done.50) | copy-start | bytes 1540
  930.8 67.3 %copy-start.60 = (f32[128]{0:T(128)S(1)}, f32[128]{0:T(128)}, u32[]{:S(2)}) copy-start(f32[128]{0:T(128)} %copy-done.59) | copy-start | bytes 1540
  1052.5 134.1 %copy-start.40 = (f32[1,960]{1,0:T(1,128)S(1)}, f32[1,960]{1,0:T(1,128)}, u32[]{:S(2)}) copy-start(f32[1,960]{1,0:T(1,128)} %copy-done.39) | copy-start | bytes 11524
  1052.5 134.1 %copy-start.49 = (f32[128]{0:T(128)S(1)}, f32[128]{0:T(128)}, u32[]{:S(2)}) copy-start(f32[128]{0:T(128)} %copy-done.48) | copy-start | bytes 1540
  1052.6 133.1 %reduce-scatter.18.cloned.1.call-start = ((), (), s32[]{:S(2)}) async-start(), calls=%async_computation.11 | async-start | bytes 1474560 | tf_op jit(solution)/shard_map/reduce_scatter | solution.py:269
  1053.3 187.9 %all-gather.20.cloned.1.call-start = ((), (), s32[]{:S(2)}) async-start(), calls=%async_computation.12 | async-start | bytes 2211840 | tf_op jit(solution)/shard_map/all_gather | solution.py:481
  1190.6 135.2 %reduce-scatter.20.cloned.1.call-start = ((), (), s32[]{:S(2)}) async-start(), calls=%async_computation.13 | async-start | bytes 4423680 | tf_op jit(solution)/shard_map/reduce_scatter | solution.py:473
  1193.3 257.5 %reduce-scatter.28.cloned.1.call-start = ((), (), s32[]{:S(2)}) async-start(), calls=%async_computation.21 | async-start | bytes 7188480
  1197.1 434.9 %reduce-scatter.24.cloned.1.call-start = ((), (), s32[]{:S(2)}) async-start(), calls=%async_computation.15 | async-start | bytes 11796480 | tf_op jit(solution)/shard_map/reduce_scatter | solution.py:475
  1205.6 754.6 %reduce-scatter.22.cloned.1.call-start = ((), (), s32[]{:S(2)}) async-start(), calls=%async_computation.14 | async-start | bytes 22118400 | tf_op jit(solution)/shard_map/reduce_scatter | solution.py:474
  1216.9 1253.3 %all-reduce.12.cloned.1.call-start = ((), (), s32[]{:S(2)}) async-start(), calls=%async_computation.22 | async-start | bytes 60448768 | tf_op jit(solution)/shard_map/psum | solution.py:486
  (44 other events, 427.9 us)
Sparse Core Ops, SparseCore 0:
  85.6 64.8 reduce-scatter.25
  153.3 59.8 all-gather.21
  215.9 56.5 all-gather.23
  275.2 144.5 all-gather.25
  422.4 84.4 all-gather.27
  513.2 47.6 all-gather.17
  910.4 86.2 reduce-scatter.13
  1052.7 64.6 reduce-scatter.15
  1121.8 63.8 reduce-scatter.17
  1190.8 48.3 all-gather.19
  1243.3 82.5 reduce-scatter.19
  1329.9 120.7 reduce-scatter.27
  1454.9 177.0 reduce-scatter.23
  1636.4 323.7 reduce-scatter.21
  1963.0 507.0 all-reduce.11
where the time goes:
time: 2730 us; the launch traced here: 2710 us
  waiting for transfers between devices  1640 us (60%)
  blocking collectives  328 us (12%)
  local copies, waits for them, and re-layouts  305 us (11%)
  matrix products  236 us (9%)
  other arithmetic  177 us (6%)
    psum x1, waiting for transfers between devices, local(): lax.psum((table_grad, stacked[0], stacked[1], stacked[2], stacked[3], own...  442 us
    reduce_scatter x1, waiting for transfers between devices, local(): lax.psum_scatter(matrix_grads[2], 'shard', scatter_dimension=0, tiled=True)  328 us
    reduce_scatter x1, waiting for transfers between devices, local(): lax.psum_scatter(matrix_grads[3], 'shard', scatter_dimension=0, tiled=True)  181 us
    unnamed x141, local copies, waits for them, and re-layouts  179 us
    unnamed x17, waiting for transfers between devices  168 us
    all_gather x1, waiting for transfers between devices, gather_layer(): lax.all_gather(copies[3][layer_index], 'shard', axis=0, tiled=True)  127 us
    all_gather x3, blocking collectives, merged(): pieces = jax.tree.map(lambda part: lax.all_gather(part, axis), value)  91.2 us
    all_gather x1, waiting for transfers between devices, gather_layer(): lax.all_gather(copies[4][layer_index], 'shard', axis=0, tiled=True)  81.6 us
  transfers between devices with their start and end apart: 15, of which 13 were waited for; matrix products, arithmetic and copies ran while one was open for 6% of the time, Pallas kernels for 0%

commit v1 on v0

v1 whole, which is shorter than its diff:
```python
import jax
import jax.numpy as jnp
from jax import lax
from jax.sharding import PartitionSpec as P

D = 960
HEADS = 15
KV_HEADS = 5
HEAD_DIM = 64
FF = 2560
BLOCK = 256
STEP = 5
LINE = 4

EPS_NORM = 1e-05
ROPE_BASE = 100000.0
BETA_ONE = 0.5
BETA_TWO = 0.5
DECAY = 0.1
CLIP_AT = 0.01
ADAM_EPS = 1e-08

F32 = jnp.float32
BF16 = jnp.bfloat16
QUERY = HEADS * HEAD_DIM
KEY = KV_HEADS * HEAD_DIM


def rms_norm(values, gain):
    return values * lax.rsqrt(jnp.mean(values * values, axis=-1, keepdims=True) + EPS_NORM) * gain


def rotate(values, positions):
    half_dim = values.shape[-1] // 2
    freqs = ROPE_BASE ** (-2.0 * jnp.arange(half_dim).astype(F32) / values.shape[-1])
    angles = positions.astype(F32)[:, None] * freqs[None, :]
    cosine = jnp.cos(angles)[:, None, :]
    sine = jnp.sin(angles)[:, None, :]
    first_half = values[..., :half_dim]
    second_half = values[..., half_dim:]
    return jnp.concatenate(
        [first_half * cosine - second_half * sine, second_half * cosine + first_half * sine],
        axis=-1,
    )


def swiglu(gate, up):
    return jax.nn.silu(gate) * up


def rates(seq_len):
    out_fan = max(1, HEADS * HEAD_DIM * 16 // seq_len)
    return (
        0.8 * D ** (-0.5),
        0.5 * D ** (-0.5),
        0.5 * out_fan ** (-0.5),
        0.5 * D ** (-0.5),
        0.5 * FF ** (-0.5),
        0.2,
    )


def adam_update(master, first, second, gradient, rate):
    first_new = BETA_ONE * first + (1.0 - BETA_ONE) * gradient
    second_new = BETA_TWO * second + (1.0 - BETA_TWO) * gradient * gradient
    step_size = (
        first_new
        / (1.0 - BETA_ONE**STEP)
        / (jnp.sqrt(second_new / (1.0 - BETA_TWO**STEP)) + ADAM_EPS)
    )
    master_new = master - rate * (step_size + DECAY * master)
    return (master_new, first_new, second_new, master_new.astype(BF16))


def dot(a, b, dims=((1,), (0,))):
    return lax.dot_general(a, b, (dims, ((), ())), preferred_element_type=F32)


class Links:
    def __init__(self, n_shard, n_rep):
        self.n = n_shard
        self.wide = n_shard // LINE
        self.n_rep = n_rep
        me = lax.axis_index("shard")
        self.z = me // self.wide
        self.w = me % self.wide

    def along(self, value, step, low=0, high=LINE):
        pairs = [
            (z * self.wide + w, (z + step) * self.wide + w)
            for z in range(LINE)
            for w in range(self.wide)
            if 0 <= z + step < LINE and low <= z < high
        ]
        return lax.ppermute(value, "shard", pairs)

    def across(self, value, step):
        pairs = [
            (z * self.wide + w, z * self.wide + (w + step) % self.wide)
            for z in range(LINE)
            for w in range(self.wide)
        ]
        return lax.ppermute(value, "shard", pairs)

    def gather(self, value):
        rows = value.shape[0]
        z = self.z
        blocks = [(z, value)]
        up = [None, value]
        down = [None, value]
        up[1] = self.along(value, 1)
        down[1] = self.along(value, -1)
        for k in range(2, LINE):
            up.append(self.along(up[-1], 1, low=k - 1))
            down.append(self.along(down[-1], -1, high=LINE - k + 1))
        blocks.append((jnp.where(z == 0, 1, z - 1), jnp.where(z == 0, down[1], up[1])))
        blocks.append((jnp.where(z < 2, z + 2, z - 2), jnp.where(z < 2, down[2], up[2])))
        inner = (z == 1) | (z == 2)
        blocks.append(
            (
                jnp.where(inner, z + 1, jnp.where(z == 0, 3, 0)),
                jnp.where(inner, down[1], jnp.where(z == 0, down[3], up[3])),
            )
        )
        out = jnp.zeros((self.n * rows,) + value.shape[1:], value.dtype)
        zeros = (0,) * (value.ndim - 1)
        for source, block in blocks:
            out = lax.dynamic_update_slice(
                out, block, ((source * self.wide + self.w) * rows,) + zeros
            )
            for step in range(1, self.wide):
                other = self.across(block, step)
                place = source * self.wide + (self.w - step) % self.wide
                out = lax.dynamic_update_slice(out, other, (place * rows,) + zeros)
        return out

    def scatter(self, value):
        rows = value.shape[0] // self.n
        kind = value.dtype

        def block(z, w):
            return lax.dynamic_slice_in_dim(value, (z * self.wide + w) * rows, rows, 0)

        parts = [None] * LINE
        for k in (2, 1, 3, 0):
            target = (self.z + k) % LINE
            total = block(target, self.w).astype(F32)
            for step in range(1, self.wide):
                total = total + self.across(
                    block(target, (self.w + step) % self.wide), step
                ).astype(F32)
            parts[k] = total
        up = self.along(parts[3].astype(kind), 1, high=1).astype(F32)
        down = self.along(parts[1].astype(kind), -1, low=3).astype(F32)
        up = self.along((parts[2] + up).astype(kind), 1, high=2).astype(F32)
        down = self.along((parts[2] + down).astype(kind), -1, low=2).astype(F32)
        up = self.along((parts[1] + up).astype(kind), 1).astype(F32)
        down = self.along((parts[3] + down).astype(kind), -1).astype(F32)
        return parts[0] + up + down

    def spread(self, value):
        many = jnp.broadcast_to(value[None], (self.n,) + value.shape)
        return lax.all_to_all(many, "shard", 0, 0, tiled=True)

    def core(self, value):
        return lax.ppermute(value, "rep", [(r, r ^ 1) for r in range(self.n_rep)])

    def chip(self, value):
        return lax.ppermute(value, "rep", [(r, r ^ 2) for r in range(self.n_rep)])


def build(mesh):
    n_shard = mesh.shape["shard"]
    n_rep = mesh.shape["rep"]

    def local(
        token_ids,
        target_ids,
        loss_mask,
        table_master,
        attn_in_master,
        attn_out_master,
        mlp_in_master,
        mlp_out_master,
        gain_master,
        table_first,
        attn_in_first,
        attn_out_first,
        mlp_in_first,
        mlp_out_first,
        gain_first,
        table_second,
        attn_in_second,
        attn_out_second,
        mlp_in_second,
        mlp_out_second,
        gain_second,
    ):
        links = Links(n_shard, n_rep)
        my_rep = lax.axis_index("rep")
        my_shard = lax.axis_index("shard")
        second_core = (my_rep % 2) == 1
        tok_rows = token_ids.shape[0]
        seq_len = n_shard * tok_rows
        vocab_rows = table_master.shape[0]
        vocab_start = my_shard * vocab_rows
        positions = my_shard * tok_rows + jnp.arange(tok_rows, dtype=jnp.int32)

        def in_order(mine, other, axis=-1):
            return jnp.where(
                second_core,
                jnp.concatenate([other, mine], axis),
                jnp.concatenate([mine, other], axis),
            )

        def my_half(value, axis=-1):
            first, second = jnp.split(value, 2, axis)
            return jnp.where(second_core, second, first), jnp.where(second_core, first, second)

        packed = jnp.stack([token_ids, target_ids, loss_mask])
        reps = lax.all_gather(packed, "rep")
        everyone = links.spread(reps)
        all_ids = everyone[:, :, 0].transpose(1, 0, 2).reshape(-1)
        all_mask = everyone[:, :, 2].astype(F32)
        valid_count = jnp.sum(all_mask)
        group = lax.dynamic_index_in_dim(everyone, my_rep, 1, False)
        group_ids = group[:, 0].reshape(-1)
        group_targets = group[:, 1].reshape(-1)
        group_weights = group[:, 2].reshape(-1).astype(F32) / valid_count

        def halves(master):
            return my_half(master[0].astype(BF16))[0]

        attn_mine = links.gather(
            jnp.concatenate([halves(attn_in_master), halves(attn_out_master)], 1)
        )
        in_cols = attn_in_master.shape[2] // 2
        attn_other = links.core(attn_mine)
        attn_in = (attn_mine[:, :in_cols], attn_other[:, :in_cols])
        attn_out = (attn_mine[:, in_cols:], attn_other[:, in_cols:])
        gains = links.spread(gain_master.astype(BF16)).transpose(1, 0, 2).reshape(3, D).astype(F32)

        table_t = table_master.T.astype(BF16)
        vocab_iota = jnp.arange(vocab_rows, dtype=jnp.int32)
        pick = (group_ids[:, None] - vocab_start == vocab_iota[None, :]).astype(BF16)
        looked = dot(pick, table_t, ((1,), (1,))).astype(BF16)
        values = links.scatter(looked)

        mlp_in_mine = links.gather(halves(mlp_in_master))
        mlp_out_mine = links.gather(halves(mlp_out_master))
        mlp_in = (mlp_in_mine, links.core(mlp_in_mine))
        mlp_out = (mlp_out_mine, links.core(mlp_out_mine))

        def times(value, pair):
            return dot(value, pair[0]), dot(value, pair[1])

        def times_back(mine, other, pair):
            return dot(mine, pair[0], ((1,), (1,))) + dot(other, pair[1], ((1,), (1,)))

        normed_one, norm_one_back = jax.vjp(rms_norm, values, gains[0])
        normed_one = normed_one.astype(BF16)
        mixed = in_order(*times(normed_one, attn_in))
        heads_raw = mixed[:, : QUERY + KEY].reshape(tok_rows, HEADS + KV_HEADS, HEAD_DIM)
        rotated, rope_back = jax.vjp(lambda part: rotate(part, positions), heads_raw)
        rotated = rotated.astype(BF16)
        group_size = HEADS // KV_HEADS
        queries = rotated[:, :HEADS].reshape(tok_rows, KV_HEADS, group_size, HEAD_DIM)
        queries = queries.transpose(1, 2, 0, 3).reshape(KV_HEADS, group_size * tok_rows, HEAD_DIM)
        keys_values = jnp.concatenate(
            [rotated[:, HEADS:].reshape(tok_rows, KEY), mixed[:, QUERY + KEY :].astype(BF16)], 1
        )
        keys_values = links.gather(keys_values)
        keys_values = keys_values.reshape(seq_len, 2, KV_HEADS, HEAD_DIM).transpose(1, 2, 0, 3)
        keys, vals = keys_values[0], keys_values[1]
        scale = HEAD_DIM ** (-0.5)
        key_blocks = jnp.arange(seq_len, dtype=jnp.int32) // BLOCK
        query_blocks = jnp.tile(positions // BLOCK, group_size)
        allowed = (key_blocks[None, :] <= query_blocks[:, None])[None]

        def batched(spec, a, b):
            return jnp.einsum(spec, a, b, preferred_element_type=F32)

        scores = jnp.where(allowed, batched("htd,hsd->hts", queries, keys) * scale, -1e30)
        highest = jnp.max(scores, axis=-1, keepdims=True)
        weights = jnp.exp(scores - highest)
        totals = jnp.sum(weights, axis=-1, keepdims=True)
        chances = weights / totals
        chances_low = chances.astype(BF16)
        outputs = batched("hts,hsd->htd", chances_low, vals)

        def to_rows(heads):
            return (
                heads.reshape(KV_HEADS, group_size, tok_rows, HEAD_DIM)
                .transpose(2, 0, 1, 3)
                .reshape(tok_rows, QUERY)
            )

        attended = to_rows(outputs).astype(BF16)
        middle = values + in_order(*times(attended, attn_out))
        normed_two, norm_two_back = jax.vjp(rms_norm, middle, gains[1])
        normed_two = normed_two.astype(BF16)
        part_mine, part_other = times(normed_two, mlp_in)
        gate = jnp.where(second_core, part_other, part_mine)
        up = jnp.where(second_core, part_mine, part_other)
        hidden, glu_back = jax.vjp(swiglu, gate, up)
        hidden = hidden.astype(BF16)
        result = middle + in_order(*times(hidden, mlp_out))
        final, final_back = jax.vjp(rms_norm, result, gains[2])

        states = links.gather(final.astype(BF16))
        logits = dot(states, table_t)
        local_targets = group_targets - vocab_start
        hit = local_targets[:, None] == vocab_iota[None, :]
        high = jnp.max(logits, axis=-1)
        raised = jnp.exp(logits - high[:, None])
        stats = jnp.stack(
            [high, jnp.sum(raised, axis=-1), jnp.sum(jnp.where(hit, logits, 0.0), axis=-1)]
        )
        stats = links.spread(stats)
        top = jnp.max(stats[:, 0], axis=0)
        log_totals = top + jnp.log(jnp.sum(stats[:, 1] * jnp.exp(stats[:, 0] - top), axis=0))
        picked = jnp.sum(stats[:, 2], axis=0)
        group_loss = jnp.sum((log_totals - picked) * group[:, 2].reshape(-1).astype(F32))
        grad_logits = (
            (jnp.exp(logits - log_totals[:, None]) - jnp.where(hit, 1.0, 0.0))
            * group_weights[:, None]
        ).astype(BF16)
        grad_states = dot(grad_logits, table_t, ((1,), (1,))).astype(BF16)
        grad_final = links.scatter(grad_states)

        table_grad = dot(states, grad_logits, ((0,), (0,))).astype(BF16)
        grad_mine, grad_other = my_half(table_grad)
        chip_sum = (grad_mine.astype(F32) + links.core(grad_other).astype(F32)).astype(BF16)
        half_sum = (chip_sum.astype(F32) + links.chip(chip_sum).astype(F32)).astype(BF16)
        table_sum = in_order(half_sum, links.core(half_sum)).astype(F32)

        grad_output, grad_gain_three = final_back(grad_final)

        def weight_grad(value, mine, other):
            sent = dot(value, other, ((0,), (0,))).astype(BF16)
            return (dot(value, mine, ((0,), (0,))) + links.core(sent).astype(F32)).astype(BF16)

        def owned(part):
            part = links.scatter(part).astype(BF16)
            part = part.astype(F32) + links.chip(part).astype(F32)
            return part, links.core(part)

        branch_mine, branch_other = my_half(grad_output.astype(BF16))
        grad_mlp_out = weight_grad(hidden, branch_mine, branch_other)
        grad_hidden = times_back(branch_mine, branch_other, mlp_out)
        grad_gate, grad_up = glu_back(grad_hidden)
        grad_gate = grad_gate.astype(BF16)
        grad_up = grad_up.astype(BF16)
        glu_mine = jnp.where(second_core, grad_up, grad_gate)
        glu_other = jnp.where(second_core, grad_gate, grad_up)
        grad_mlp_in = weight_grad(normed_two, glu_mine, glu_other)
        middle_part, grad_gain_two = norm_two_back(times_back(glu_mine, glu_other, mlp_in))
        grad_middle = grad_output + middle_part
        mlp_out_sum = in_order(*owned(grad_mlp_out))
        mlp_in_sum = in_order(*owned(grad_mlp_in))

        out_mine, out_other = my_half(grad_middle.astype(BF16))
        grad_attn_out = weight_grad(attended, out_mine, out_other)
        grad_attended = times_back(out_mine, out_other, attn_out).astype(BF16)
        grad_heads = (
            grad_attended.reshape(tok_rows, KV_HEADS, group_size, HEAD_DIM)
            .transpose(1, 2, 0, 3)
            .reshape(KV_HEADS, group_size * tok_rows, HEAD_DIM)
        )
        deltas = jnp.sum(grad_heads.astype(F32) * outputs, axis=-1, keepdims=True)
        grad_chances = batched("htd,hsd->hts", grad_heads, vals)
        grad_scores = (chances * (grad_chances - deltas)).astype(BF16)
        grad_queries = batched("hts,hsd->htd", grad_scores, keys) * scale
        grad_keys = batched("hts,htd->hsd", grad_scores, queries) * scale
        grad_vals = batched("hts,htd->hsd", chances_low, grad_heads)
        grad_kv = jnp.stack([grad_keys, grad_vals]).transpose(2, 0, 1, 3).reshape(seq_len, 2 * KEY)
        grad_kv = links.scatter(grad_kv.astype(BF16))
        grad_rotated = jnp.concatenate(
            [
                to_rows(grad_queries).reshape(tok_rows, HEADS, HEAD_DIM),
                grad_kv[:, :KEY].reshape(tok_rows, KV_HEADS, HEAD_DIM),
            ],
            1,
        )
        grad_raw = rope_back(grad_rotated)[0].reshape(tok_rows, QUERY + KEY)
        grad_mixed = jnp.concatenate([grad_raw, grad_kv[:, KEY:]], 1).astype(BF16)
        mixed_mine, mixed_other = my_half(grad_mixed)
        values_part, grad_gain_one = norm_one_back(times_back(mixed_mine, mixed_other, attn_in))
        grad_values = (grad_middle + values_part).astype(BF16)
        grad_attn_in = weight_grad(normed_one, mixed_mine, mixed_other)
        grad_gains = jnp.stack([grad_gain_one, grad_gain_two, grad_gain_three], 1)
        grad_gains = grad_gains + links.core(grad_gains)
        small = jnp.concatenate([grad_attn_in, grad_attn_out, grad_gains.astype(BF16)], 1)
        small_mine, small_other = owned(small)
        attn_in_sum = in_order(small_mine[:, :in_cols], small_other[:, :in_cols])
        out_end = in_cols + D // 2
        attn_out_sum = in_order(small_mine[:, in_cols:out_end], small_other[:, in_cols:out_end])
        gain_sum = small_mine[:, out_end:].T

        embedded = lax.all_gather(grad_values, "rep").transpose(1, 0, 2).reshape(tok_rows, -1)
        embedded = links.gather(embedded).reshape(seq_len, n_rep, D).transpose(1, 0, 2)
        embedded = embedded.reshape(n_rep * seq_len, D)
        place = (all_ids[:, None] - vocab_start == vocab_iota[None, :]).astype(BF16)
        table_sum = table_sum + dot(embedded, place, ((0,), (0,)))

        sums = (
            table_sum,
            attn_in_sum[None],
            attn_out_sum[None],
            mlp_in_sum[None],
            mlp_out_sum[None],
            gain_sum,
        )
        squares = jnp.zeros((), F32)
        for gradient in sums:
            squares = squares + jnp.sum(gradient * gradient)
        loss = group_loss + links.core(group_loss)
        loss_sum = loss + links.chip(loss)
        squares = jnp.sum(links.spread(jnp.full((8, 128), squares))[:, 0, 0])
        grad_norm = jnp.sqrt(squares)
        clip_scale = CLIP_AT / jnp.maximum(grad_norm, CLIP_AT)
        results = [loss_sum, valid_count, grad_norm]
        masters = (
            table_master.T,
            attn_in_master,
            attn_out_master,
            mlp_in_master,
            mlp_out_master,
            gain_master,
        )
        firsts = (
            table_first.T,
            attn_in_first,
            attn_out_first,
            mlp_in_first,
            mlp_out_first,
            gain_first,
        )
        seconds = (
            table_second.T,
            attn_in_second,
            attn_out_second,
            mlp_in_second,
            mlp_out_second,
            gain_second,
        )
        rate_list = rates(seq_len)
        for member in range(6):
            new = adam_update(
                masters[member],
                firsts[member],
                seconds[member],
                sums[member] * clip_scale,
                rate_list[member],
            )
            if member == 0:
                new = tuple(part.T for part in new)
            results.extend(new)
        return tuple(results)

    return local


def solution(mesh):
    token = P(("rep", "shard"))
    weight = P(None, "shard", None)
    state = (P("shard", None), weight, weight, weight, weight, P(None, "shard"))
    outs = [P(), P(), P()]
    for spec in state:
        outs.extend([spec] * 4)
    return jax.shard_map(
        build(mesh),
        mesh=mesh,
        in_specs=(token, token, token) + state * 3,
        out_specs=tuple(outs),
        check_vma=False,
    )
```

time: 2730 us -> 1190 us (0.44)
  waiting for transfers between devices: 1640 us -> 313 us
  blocking collectives: 328 us -> 14.9 us
  starting transfers between devices: 0.83 us -> 234 us
  local copies, waits for them, and re-layouts: 305 us -> 146 us
  other arithmetic: 177 us -> 235 us
    reduce_scatter x6 -> x0, waiting for transfers between devices: 748 us -> none  [the longest x1 328 us: local(): lax.psum_scatter(matrix_grads[2], 'shard', scatter_dimension=0, tiled=True)]
    psum x1 -> x0, waiting for transfers between devices: 442 us -> none  [local(): lax.psum((table_grad, stacked[0], stacked[1], stacked[2], stacked[3], own...]
    ppermute x0 -> x139, waiting for transfers between devices: none -> 300 us  [the longest x48 128 us: across(): return lax.ppermute(value, 'shard', pairs)]
    all_gather x6 -> x0, waiting for transfers between devices: 283 us -> none  [the longest x1 127 us: gather_layer(): lax.all_gather(copies[3][layer_index], 'shard', axis=0, tiled=True)]
    ppermute x0 -> x139, starting transfers between devices: none -> 213 us  [the longest x72 158 us: along(): return lax.ppermute(value, 'shard', pairs)]
    all_gather x9 -> x2, blocking collectives: 227 us -> 14.9 us  [the longest x1 9.71 us: local(): lax.all_gather(grad_values, 'rep').transpose(1, 0, 2).reshape(tok_rows, -1)]
    unnamed x17 -> x0, waiting for transfers between devices: 168 us -> none
    unnamed x141 -> x206, local copies, waits for them, and re-layouts: 179 us -> 49.5 us
  transfers between devices with their start and end apart: 15 -> 143, of which waited for: 13 -> 58; matrix products, arithmetic and copies ran while one was open for 6% -> 25% of each run, Pallas kernels for 0% -> 0%
where the time goes in v1:
time: 1190 us; the launch traced here: 1180 us
  waiting for transfers between devices  313 us (26%)
  other arithmetic  235 us (20%)
  starting transfers between devices  234 us (20%)
  matrix products  224 us (19%)
  local copies, waits for them, and re-layouts  146 us (12%)
  blocking collectives  14.9 us (1%)
  between operations  12.6 us (1%)
    dot_general x29, matrix products, dot(): return lax.dot_general(a, b, (dims, ((), ())), preferred_element_type=F32)  205 us
    ppermute x72, starting transfers between devices, along(): return lax.ppermute(value, 'shard', pairs)  158 us
    ppermute x48, waiting for transfers between devices, across(): return lax.ppermute(value, 'shard', pairs)  128 us
    ppermute x5, waiting for transfers between devices, chip(): return lax.ppermute(value, 'rep', [(r, r ^ 2) for r in range(self.n_rep)])  91.2 us
    ppermute x72, waiting for transfers between devices, along(): return lax.ppermute(value, 'shard', pairs)  78.2 us
    transpose x1, other arithmetic, local(): new = tuple((part.T for part in new))  70.1 us
    ppermute x48, starting transfers between devices, across(): return lax.ppermute(value, 'shard', pairs)  50.6 us
    unnamed x206, local copies, waits for them, and re-layouts  49.5 us
  transfers between devices with their start and end apart: 143, of which 58 were waited for; matrix products, arithmetic and copies ran while one was open for 25% of the time, Pallas kernels for 0%

profile of v1, /device:TPU:0, one launch (start us, length us, event | category | flops | bytes accessed | tf_op | source)
XLA Modules:
  0.0 1179.0 jit_solution(14544623266886999382)
XLA Ops:
  39.1 6.8 all-to-all-done
  46.5 23.8 %fusion.16 = bf16[1024,960]{0,1:T(8,128)(2,1)S(1)} fusion(s32[1024]{0:T(1024)} %get-tuple-element.354, f32[6144,960]{0,1:T(8,128)} %param.24), kind=kOutput, calls=%fused_computation.55 | convolution fusion | flops 12085886976 | bytes 25563136 | tf_op jit(solution)/shard_map/dot_general | solution.py:76
  88.6 9.2 collective-permute-done.4
  143.6 9.6 collective-permute-start.6
  179.7 7.0 collective-permute-done.38
  193.0 10.9 collective-permute-done.40
  221.2 7.7 collective-permute-done.27
  352.7 23.5 %fusion.131 = (f32[1024]{0:T(1024)S(1)}, f32[1024,6144]{1,0:T(8,128)}) fusion(bf16[1024,960]{0,1:T(8,128)(2,1)} %constant_dynamic-update-slice_fusion.8, f32[6144,960]{0,1:T(8,128)} %param.24), kind=kOutput, calls=%fused_computation.414 | convolution fusion | flops 12085885952 | bytes 50728960 | tf_op jit(solution)/shard_map/dot_general | solution.py:76
  376.2 11.7 exponential_reduce_fusion
  388.6 7.9 all-to-all-start.2
  397.1 6.7 all-to-all-done.2
  405.2 17.5 %multiply_convert_fusion = bf16[1024,6144]{1,0:T(8,128)(2,1)} fusion(f32[1024,6144]{1,0:T(8,128)} %get-tuple-element.364, f32[1024]{0:T(1024)S(1)} %get-tuple-element.352, f32[1024]{0:T(1024)S(1)} %get-tuple-element.261, s32[1024]{0:T(1024)S(1)} %get-tuple-element.353), kind=kLoop, calls=%fused_computation.6 | loop fusion | flops 37748736 | bytes 37761024 | tf_op jit(solution)/shard_map/convert_element_type | solution.py:327
  422.8 21.5 %fusion.133 = bf16[1024,960]{0,1:T(8,128)(2,1)} fusion(bf16[1024,6144]{1,0:T(8,128)(2,1)} %multiply_convert_fusion, f32[6144,960]{0,1:T(8,128)} %param.24), kind=kOutput, calls=%fused_computation.416 | convolution fusion | flops 12079595520 | bytes 38141952 | tf_op jit(solution)/shard_map/dot_general | solution.py:76
  447.7 6.3 collective-permute-done.71
  485.0 20.4 %convolution_convert_fusion = bf16[960,6144]{1,0:T(8,128)(2,1)} fusion(bf16[1024,960]{0,1:T(8,128)(2,1)} %constant_dynamic-update-slice_fusion.8, bf16[1024,6144]{1,0:T(8,128)(2,1)} %multiply_convert_fusion), kind=kOutput, calls=%fused_computation.25 | convolution fusion | flops 12085493760 | bytes 26345472 | tf_op jit(solution)/shard_map/dot_general | solution.py:76
  535.5 7.6 broadcast_select_fusion
  545.8 9.0 collective-permute-start.82
  594.7 9.7 all-gather.1
  618.4 10.3 collective-permute-done.88
  642.0 19.3 %iota_compare_fusion.1.clone.4 = pred[4096,6144]{1,0:T(32,128)(4,1)} fusion(s32[4096]{0:T(1024)S(1)} %fusion.90), kind=kLoop, calls=%fused_computation.1.clone.clone.clone.clone.1 | loop fusion | flops 25165824 | bytes 25182208 | tf_op jit(solution)/shard_map/reduce_sum | solution.py:416
  675.2 6.9 collective-permute-done.129
  732.7 17.4 %collective-permute-done.117 = bf16[120,2560]{1,0:T(8,128)(2,1)S(1)} collective-permute-done((bf16[120,2560]{1,0:T(8,128)(2,1)S(1)}, bf16[120,2560]{1,0:T(8,128)(2,1)S(1)}, u32[]{:S(2)}, u32[]{:S(2)}) %collective-permute-start.117) | collective-permute-done | bytes 614432 | tf_op jit(solution)/shard_map/ppermute | solution.py:103
  757.4 6.2 collective-permute-done.116
  771.7 6.4 collective-permute-done.115
  778.7 8.5 collective-permute-start.133
  795.4 78.9 %collective-permute-done.66 = bf16[960,3072]{1,0:T(8,128)(2,1)S(1)} collective-permute-done((bf16[960,3072]{1,0:T(8,128)(2,1)S(1)}, bf16[960,3072]{1,0:T(8,128)(2,1)S(1)}, u32[]{:S(2)}, u32[]{:S(2)}) %collective-permute-start.66) | collective-permute-done | bytes 5898272 | tf_op jit(solution)/shard_map/ppermute | solution.py:169
  877.6 9.5 add_convert_fusion
  927.4 10.5 collective-permute-done.124
  942.7 7.8 copy.303
  960.8 64.2 %multiply_reduce_fusion = (f32[]{:T(128)}, f32[960,6144]{1,0:T(8,128)}) fusion(bf16[960,3072]{1,0:T(8,128)(2,1)} %collective-permute-done.67, bf16[960,3072]{1,0:T(8,128)(2,1)} %add_convert_fusion, pred[]{:T(512)S(6)} %eq.162, bf16[4096,960]{0,1:T(8,128)(2,1)} %bitcast.254, pred[4096,6144]{1,0:T(32,128)(4,1)} %iota_compare_fusion.1.clone.4), kind=kOutput, calls=%fused_computation.18 | convolution fusion | flops 48395059200 | bytes 68419592 | tf_op jit(solution)/shard_map/dot_general | solution.py:76
  1095.9 9.0 fusion.115
  1106.2 70.1 %convert_bitcast_fusion = (bf16[6144,960]{0,1:T(8,128)(2,1)}, f32[960,6144]{1,0:T(8,128)}, f32[6144,960]{0,1:T(8,128)}, f32[6144,960]{0,1:T(8,128)}) fusion(f32[6144,960]{0,1:T(8,128)} %param.36, f32[]{:T(128)S(6)} %div.178, f32[960,6144]{1,0:T(8,128)} %get-tuple-element.368, bf16[960,3072]{1,0:T(8,128)(2,1)} %collective-permute-done.67, ...), kind=kLoop, calls=%fused_computation.22 | loop fusion | flops 159252480 | bytes 188743680 | tf_op jit(solution)/shard_map/transpose | solution.py:457
  (696 shorter events, 624.6 us)
Async XLA Ops:
  5.8 66.9 %collective-permute-start.10 = (bf16[120,1280]{1,0:T(8,128)(2,1)}, bf16[120,1280]{1,0:T(8,128)(2,1)}, u32[]{:S(2)}, u32[]{:S(2)}) collective-permute-start(bf16[120,1280]{1,0:T(8,128)(2,1)} %get-tuple-element.295), channel_id=1, source_target_pairs={{0,1},{1,0},{2,3},{3,2},{4,5},{5,4},{6,7},{7,6},{8,9},{9,8},{10,11... | collective-permute-start | bytes 921608 | tf_op jit(solution)/shard_map/ppermute | solution.py:103
  8.7 72.3 %collective-permute-start.11 = (bf16[120,1280]{1,0:T(8,128)(2,1)}, bf16[120,1280]{1,0:T(8,128)(2,1)}, u32[]{:S(2)}, u32[]{:S(2)}) collective-permute-start(bf16[120,1280]{1,0:T(8,128)(2,1)} %get-tuple-element.295), channel_id=1, source_target_pairs={{2,0},{3,1},{4,2},{5,3},{6,4},{7,5},{10,8},{11,9},{12,10},{13,11},... | collective-permute-start | bytes 921608 | tf_op jit(solution)/shard_map/ppermute | solution.py:95
  10.0 72.1 %collective-permute-start.12 = (bf16[120,1280]{1,0:T(8,128)(2,1)}, bf16[120,1280]{1,0:T(8,128)(2,1)}, u32[]{:S(2)}, u32[]{:S(2)}) collective-permute-start(bf16[120,1280]{1,0:T(8,128)(2,1)} %get-tuple-element.295), channel_id=1, source_target_pairs={{0,2},{1,3},{2,4},{3,5},{4,6},{5,7},{8,10},{9,11},{10,12},{11,13},... | collective-permute-start | bytes 921608 | tf_op jit(solution)/shard_map/ppermute | solution.py:95
  23.7 75.5 %collective-permute-start.31 = (bf16[120,2560]{1,0:T(8,128)(2,1)}, bf16[120,2560]{1,0:T(8,128)(2,1)}, u32[]{:S(2)}, u32[]{:S(2)}) collective-permute-start(bf16[120,2560]{1,0:T(8,128)(2,1)} %get-tuple-element.279), channel_id=1, source_target_pairs={{0,1},{1,0},{2,3},{3,2},{4,5},{5,4},{6,7},{7,6},{8,9},{9,8},{10,11... | collective-permute-start | bytes 1843208 | tf_op jit(solution)/shard_map/ppermute | solution.py:103
  72.6 42.3 %collective-permute-start.32 = (bf16[120,2560]{1,0:T(8,128)(2,1)}, bf16[120,2560]{1,0:T(8,128)(2,1)S(1)}, u32[]{:S(2)}, u32[]{:S(2)}) collective-permute-start(bf16[120,2560]{1,0:T(8,128)(2,1)} %get-tuple-element.279), channel_id=1, source_target_pairs={{2,0},{3,1},{4,2},{5,3},{6,4},{7,5},{10,8},{11,9},{12,10},{13,11},... | collective-permute-start | bytes 1843208 | tf_op jit(solution)/shard_map/ppermute | solution.py:95
  78.6 37.1 %collective-permute-start.33 = (bf16[120,2560]{1,0:T(8,128)(2,1)}, bf16[120,2560]{1,0:T(8,128)(2,1)S(1)}, u32[]{:S(2)}, u32[]{:S(2)}) collective-permute-start(bf16[120,2560]{1,0:T(8,128)(2,1)} %get-tuple-element.279), channel_id=1, source_target_pairs={{0,2},{1,3},{2,4},{3,5},{4,6},{5,7},{8,10},{9,11},{10,12},{11,13},... | collective-permute-start | bytes 1843208 | tf_op jit(solution)/shard_map/ppermute | solution.py:95
  101.8 53.9 %collective-permute-start.43 = (bf16[320,480]{0,1:T(8,128)(2,1)S(1)}, bf16[320,480]{0,1:T(8,128)(2,1)S(1)}, u32[]{:S(2)}, u32[]{:S(2)}) collective-permute-start(bf16[320,480]{0,1:T(8,128)(2,1)S(1)} %copy-done.32), channel_id=1, source_target_pairs={{2,0},{3,1},{4,2},{5,3},{6,4},{7,5},{10,8},{11,9},{12,10},{13,11},... | collective-permute-start | bytes 921608 | tf_op jit(solution)/shard_map/ppermute | solution.py:95
  153.3 35.4 %collective-permute-start.20 = (bf16[960,1280]{1,0:T(8,128)(2,1)}, bf16[960,1280]{1,0:T(8,128)(2,1)S(1)}, u32[]{:S(2)}, u32[]{:S(2)}) collective-permute-start(bf16[960,1280]{1,0:T(8,128)(2,1)} %constant_dynamic-update-slice_fusion.32), channel_id=1, source_target_pairs={{0,8},{8,0},{16,24},{24,16},{1,9},{9,1},{17,25},{25,17},{2,10},{10... | collective-permute-start | bytes 7372808 | tf_op jit(solution)/shard_map/ppermute | solution.py:166
  173.6 36.9 %collective-permute-start.47 = (bf16[320,480]{0,1:T(8,128)(2,1)S(1)}, bf16[320,480]{0,1:T(8,128)(2,1)S(1)}, u32[]{:S(2)}, u32[]{:S(2)}) collective-permute-start(bf16[320,480]{0,1:T(8,128)(2,1)S(1)} %collective-permute-done.44), channel_id=1, source_target_pairs={{2,4},{3,5},{4,6},{5,7},{10,12},{11,13},{12,14},{13,15},{18,20},{1... | collective-permute-start | bytes 921608 | tf_op jit(solution)/shard_map/ppermute | solution.py:95
  177.6 41.5 %collective-permute-start.49 = (bf16[320,480]{0,1:T(8,128)(2,1)S(1)}, bf16[320,480]{0,1:T(8,128)(2,1)S(1)}, u32[]{:S(2)}, u32[]{:S(2)}) collective-permute-start(bf16[320,480]{0,1:T(8,128)(2,1)S(1)} %collective-permute-done.46), channel_id=1, source_target_pairs={{2,0},{3,1},{10,8},{11,9},{18,16},{19,17},{26,24},{27,25}} | collective-permute-start | bytes 921608 | tf_op jit(solution)/shard_map/ppermute | solution.py:95
  206.3 86.5 %collective-permute-start.41 = (bf16[960,2560]{1,0:T(8,128)(2,1)}, bf16[960,2560]{1,0:T(8,128)(2,1)}, u32[]{:S(2)}, u32[]{:S(2)}) collective-permute-start(bf16[960,2560]{1,0:T(8,128)(2,1)} %constant_dynamic-update-slice_fusion.16), channel_id=1, source_target_pairs={{0,8},{8,0},{16,24},{24,16},{1,9},{9,1},{17,25},{25,17},{2,10},{10... | collective-permute-start | bytes 14745608 | tf_op jit(solution)/shard_map/ppermute | solution.py:166
  228.9 32.1 %collective-permute-start.48 = (bf16[320,480]{0,1:T(8,128)(2,1)}, bf16[320,480]{0,1:T(8,128)(2,1)}, u32[]{:S(2)}, u32[]{:S(2)}) collective-permute-start(bf16[320,480]{0,1:T(8,128)(2,1)} %broadcast_select_fusion.9), channel_id=1, source_target_pairs={{0,1},{1,0},{2,3},{3,2},{4,5},{5,4},{6,7},{7,6},{8,9},{9,8},{10,11... | collective-permute-start | bytes 921608 | tf_op jit(solution)/shard_map/ppermute | solution.py:103
  231.1 39.4 %collective-permute-start.51 = (bf16[320,480]{0,1:T(8,128)(2,1)S(1)}, bf16[320,480]{0,1:T(8,128)(2,1)}, u32[]{:S(2)}, u32[]{:S(2)}) collective-permute-start(bf16[320,480]{0,1:T(8,128)(2,1)S(1)} %get-tuple-element.346), channel_id=1, source_target_pairs={{0,1},{1,0},{2,3},{3,2},{4,5},{5,4},{6,7},{7,6},{8,9},{9,8},{10,11... | collective-permute-start | bytes 921608 | tf_op jit(solution)/shard_map/ppermute | solution.py:103
  233.8 41.3 %collective-permute-start.30 = (bf16[128,640]{0,1:T(8,128)(2,1)}, bf16[128,640]{0,1:T(8,128)(2,1)S(1)}, u32[]{:S(2)}, u32[]{:S(2)}) collective-permute-start(bf16[128,640]{0,1:T(8,128)(2,1)} %get-tuple-element.283), channel_id=1, source_target_pairs={{0,1},{1,0},{2,3},{3,2},{4,5},{5,4},{6,7},{7,6},{8,9},{9,8},{10,11... | collective-permute-start | bytes 491528 | tf_op jit(solution)/shard_map/ppermute | solution.py:103
  574.6 60.4 %collective-permute-start.126 = (bf16[2560,480]{0,1:T(8,128)(2,1)S(1)}, bf16[2560,480]{0,1:T(8,128)(2,1)S(1)}, u32[]{:S(2)}, u32[]{:S(2)}) collective-permute-start(bf16[2560,480]{0,1:T(8,128)(2,1)S(1)} %convolution_convert_fusion.2), channel_id=1, source_target_pairs={{0,8},{8,0},{16,24},{24,16},{1,9},{9,1},{17,25},{25,17},{2,10},{10... | collective-permute-start | bytes 7372808 | tf_op jit(solution)/shard_map/ppermute | solution.py:166
  618.2 107.5 %collective-permute-start.65 = (bf16[960,3072]{1,0:T(8,128)(2,1)}, bf16[960,3072]{1,0:T(8,128)(2,1)}, u32[]{:S(2)}, u32[]{:S(2)}) collective-permute-start(bf16[960,3072]{1,0:T(8,128)(2,1)} %broadcast_select_fusion), channel_id=1, source_target_pairs={{0,8},{8,0},{16,24},{24,16},{1,9},{9,1},{17,25},{25,17},{2,10},{10... | collective-permute-start | bytes 17694728 | tf_op jit(solution)/shard_map/ppermute | solution.py:166
  631.5 90.2 %collective-permute-start.113 = (bf16[960,2560]{1,0:T(8,128)(2,1)S(1)}, bf16[960,2560]{1,0:T(8,128)(2,1)S(1)}, u32[]{:S(2)}, u32[]{:S(2)}) collective-permute-start(bf16[960,2560]{1,0:T(8,128)(2,1)S(1)} %bitcast.253), channel_id=1, source_target_pairs={{0,8},{8,0},{16,24},{24,16},{1,9},{9,1},{17,25},{25,17},{2,10},{10... | collective-permute-start | bytes 14745608 | tf_op jit(solution)/shard_map/ppermute | solution.py:166
  633.9 39.1 %collective-permute-start.91 = (bf16[128,3840]{0,1:T(8,128)(2,1)S(1)}, bf16[128,3840]{0,1:T(8,128)(2,1)S(1)}, u32[]{:S(2)}, u32[]{:S(2)}) collective-permute-start(bf16[128,3840]{0,1:T(8,128)(2,1)S(1)} %get-tuple-element.256), channel_id=1, source_target_pairs={{0,1},{1,0},{2,3},{3,2},{4,5},{5,4},{6,7},{7,6},{8,9},{9,8},{10,11... | collective-permute-start | bytes 2949128 | tf_op jit(solution)/shard_map/ppermute | solution.py:103
  640.9 31.1 %collective-permute-start.104 = (bf16[120,1283]{0,1:T(8,128)(2,1)S(1)}, bf16[120,1283]{0,1:T(8,128)(2,1)S(1)}, u32[]{:S(2)}, u32[]{:S(2)}) collective-permute-start(bf16[120,1283]{0,1:T(8,128)(2,1)S(1)} %get-tuple-element.313), channel_id=1, source_target_pairs={{0,1},{1,0},{2,3},{3,2},{4,5},{5,4},{6,7},{7,6},{8,9},{9,8},{10,11... | collective-permute-start | bytes 923768 | tf_op jit(solution)/shard_map/ppermute | solution.py:103
  701.6 48.6 %collective-permute-start.102 = (bf16[120,1283]{0,1:T(8,128)(2,1)}, bf16[120,1283]{0,1:T(8,128)(2,1)}, u32[]{:S(2)}, u32[]{:S(2)}) collective-permute-start(bf16[120,1283]{0,1:T(8,128)(2,1)} %get-tuple-element.315), channel_id=1, source_target_pairs={{0,1},{1,0},{2,3},{3,2},{4,5},{5,4},{6,7},{7,6},{8,9},{9,8},{10,11... | collective-permute-start | bytes 923768 | tf_op jit(solution)/shard_map/ppermute | solution.py:103
  712.0 56.6 %collective-permute-start.94 = (bf16[128,3840]{0,1:T(8,128)(2,1)}, bf16[128,3840]{0,1:T(8,128)(2,1)}, u32[]{:S(2)}, u32[]{:S(2)}) collective-permute-start(bf16[128,3840]{0,1:T(8,128)(2,1)} %get-tuple-element.254), channel_id=1, source_target_pairs={{0,1},{1,0},{2,3},{3,2},{4,5},{5,4},{6,7},{7,6},{8,9},{9,8},{10,11... | collective-permute-start | bytes 2949128 | tf_op jit(solution)/shard_map/ppermute | solution.py:103
  715.5 35.4 %collective-permute-start.106 = (bf16[120,1283]{0,1:T(8,128)(2,1)}, bf16[120,1283]{0,1:T(8,128)(2,1)}, u32[]{:S(2)}, u32[]{:S(2)}) collective-permute-start(bf16[120,1283]{0,1:T(8,128)(2,1)} %add_convert_fusion.20), channel_id=1, source_target_pairs={{0,2},{1,3},{2,4},{3,5},{8,10},{9,11},{10,12},{11,13},{16,18},{17,... | collective-permute-start | bytes 923768 | tf_op jit(solution)/shard_map/ppermute | solution.py:95
  721.7 33.0 %collective-permute-start.134 = (bf16[320,480]{0,1:T(8,128)(2,1)}, bf16[320,480]{0,1:T(8,128)(2,1)}, u32[]{:S(2)}, u32[]{:S(2)}) collective-permute-start(bf16[320,480]{0,1:T(8,128)(2,1)} %get-tuple-element.311), channel_id=1, source_target_pairs={{6,4},{7,5},{14,12},{15,13},{22,20},{23,21},{30,28},{31,29}} | collective-permute-start | bytes 921608 | tf_op jit(solution)/shard_map/ppermute | solution.py:95
  750.1 124.3 %collective-permute-start.66 = (bf16[960,3072]{1,0:T(8,128)(2,1)S(1)}, bf16[960,3072]{1,0:T(8,128)(2,1)S(1)}, u32[]{:S(2)}, u32[]{:S(2)}) collective-permute-start(bf16[960,3072]{1,0:T(8,128)(2,1)S(1)} %add_convert_fusion.1), channel_id=1, source_target_pairs={{0,16},{8,24},{16,0},{24,8},{1,17},{9,25},{17,1},{25,9},{2,18},{10... | collective-permute-start | bytes 17694728 | tf_op jit(solution)/shard_map/ppermute | solution.py:169
  754.7 33.6 %collective-permute-start.95 = (bf16[128,3840]{0,1:T(8,128)(2,1)S(1)}, bf16[128,3840]{0,1:T(8,128)(2,1)S(1)}, u32[]{:S(2)}, u32[]{:S(2)}) collective-permute-start(bf16[128,3840]{0,1:T(8,128)(2,1)S(1)} %copy-done.44), channel_id=1, source_target_pairs={{2,0},{3,1},{10,8},{11,9},{18,16},{19,17},{26,24},{27,25}} | collective-permute-start | bytes 2949128 | tf_op jit(solution)/shard_map/ppermute | solution.py:95
  778.1 110.4 %collective-permute-start.127 = (bf16[320,480]{0,1:T(8,128)(2,1)}, bf16[320,480]{0,1:T(8,128)(2,1)}, u32[]{:S(2)}, u32[]{:S(2)}) collective-permute-start(bf16[320,480]{0,1:T(8,128)(2,1)} %get-tuple-element.316), channel_id=1, source_target_pairs={{0,1},{1,0},{2,3},{3,2},{4,5},{5,4},{6,7},{7,6},{8,9},{9,8},{10,11... | collective-permute-start | bytes 921608 | tf_op jit(solution)/shard_map/ppermute | solution.py:103
  778.7 110.5 %collective-permute-start.133 = (bf16[320,480]{0,1:T(8,128)(2,1)}, bf16[320,480]{0,1:T(8,128)(2,1)}, u32[]{:S(2)}, u32[]{:S(2)}) collective-permute-start(bf16[320,480]{0,1:T(8,128)(2,1)} %get-tuple-element.310), channel_id=1, source_target_pairs={{0,2},{1,3},{2,4},{3,5},{4,6},{5,7},{8,10},{9,11},{10,12},{11,13},... | collective-permute-start | bytes 921608 | tf_op jit(solution)/shard_map/ppermute | solution.py:95
  791.5 95.6 %collective-permute-start.109 = (bf16[120,1283]{0,1:T(8,128)(2,1)}, bf16[120,1283]{0,1:T(8,128)(2,1)}, u32[]{:S(2)}, u32[]{:S(2)}) collective-permute-start(bf16[120,1283]{0,1:T(8,128)(2,1)} %add_convert_fusion.18), channel_id=1, source_target_pairs={{4,2},{5,3},{6,4},{7,5},{12,10},{13,11},{14,12},{15,13},{20,18},{2... | collective-permute-start | bytes 923768 | tf_op jit(solution)/shard_map/ppermute | solution.py:95
  793.9 98.1 %collective-permute-start.136 = (bf16[320,480]{0,1:T(8,128)(2,1)}, bf16[320,480]{0,1:T(8,128)(2,1)}, u32[]{:S(2)}, u32[]{:S(2)}) collective-permute-start(bf16[320,480]{0,1:T(8,128)(2,1)} %add_convert_fusion.12), channel_id=1, source_target_pairs={{2,0},{3,1},{4,2},{5,3},{6,4},{7,5},{10,8},{11,9},{12,10},{13,11},... | collective-permute-start | bytes 921608 | tf_op jit(solution)/shard_map/ppermute | solution.py:95
  887.1 73.7 %collective-permute-start.67 = (bf16[960,3072]{1,0:T(8,128)(2,1)}, bf16[960,3072]{1,0:T(8,128)(2,1)}, u32[]{:S(2)}, u32[]{:S(2)}) collective-permute-start(bf16[960,3072]{1,0:T(8,128)(2,1)} %add_convert_fusion), channel_id=1, source_target_pairs={{0,8},{8,0},{16,24},{24,16},{1,9},{9,1},{17,25},{25,17},{2,10},{10... | collective-permute-start | bytes 17694728 | tf_op jit(solution)/shard_map/ppermute | solution.py:166
  907.8 32.6 %collective-permute-start.97 = (bf16[128,3840]{0,1:T(8,128)(2,1)}, bf16[128,3840]{0,1:T(8,128)(2,1)}, u32[]{:S(2)}, u32[]{:S(2)}) collective-permute-start(bf16[128,3840]{0,1:T(8,128)(2,1)} %get-tuple-element.252), channel_id=1, source_target_pairs={{0,1},{1,0},{2,3},{3,2},{4,5},{5,4},{6,7},{7,6},{8,9},{9,8},{10,11... | collective-permute-start | bytes 2949128 | tf_op jit(solution)/shard_map/ppermute | solution.py:103
  917.2 33.3 %collective-permute-start.138 = (f32[320,480]{1,0:T(8,128)}, f32[320,480]{1,0:T(8,128)}, u32[]{:S(2)}, u32[]{:S(2)}) collective-permute-start(f32[320,480]{1,0:T(8,128)} %copy.266), channel_id=1, source_target_pairs={{0,8},{8,0},{16,24},{24,16},{1,9},{9,1},{17,25},{25,17},{2,10},{10... | collective-permute-start | bytes 1843208 | tf_op jit(solution)/shard_map/ppermute | solution.py:166
  (203 other events, 3499.4 us)

commit v2 on v1

--- a/solution.py
+++ b/solution.py
@@ -1,6 +1,10 @@
+import functools
+
 import jax
 import jax.numpy as jnp
 from jax import lax
+from jax.experimental import pallas as pl
+from jax.experimental.pallas import tpu as pltpu
 from jax.sharding import PartitionSpec as P
 
 D = 960
@@ -24,6 +28,7 @@
 BF16 = jnp.bfloat16
 QUERY = HEADS * HEAD_DIM
 KEY = KV_HEADS * HEAD_DIM
+VMEM = 56 * 1024 * 1024
 
 
 def rms_norm(values, gain):
@@ -74,6 +79,375 @@
 
 def dot(a, b, dims=((1,), (0,))):
     return lax.dot_general(a, b, (dims, ((), ())), preferred_element_type=F32)
+
+
+def params():
+    return pltpu.CompilerParams(vmem_limit_bytes=VMEM)
+
+
+def whole(shape):
+    return pl.BlockSpec(shape, lambda *_: (0,) * len(shape), pipeline_mode=pl.Buffered(1))
+
+
+def lookup_kernel(ids_ref, table_ref, low_ref, rows_ref, total):
+    tile = table_ref.shape[1]
+    step = pl.program_id(0)
+    low = table_ref[...].astype(BF16)
+    low_ref[...] = low
+    columns = lax.broadcasted_iota(jnp.int32, (1, tile), 1) + step * tile
+    block = min(512, rows_ref.shape[0])
+    for start in range(0, rows_ref.shape[0], block):
+        rows = pl.ds(start, block)
+        pick = jnp.where(ids_ref[rows, :] == columns, 1.0, 0.0).astype(BF16)
+        found = dot(pick, low, ((1,), (1,)))
+
+        @pl.when(step == 0)
+        def _():
+            total[rows, :] = found
+
+        @pl.when(step > 0)
+        def _():
+            total[rows, :] += found
+
+    @pl.when(step == pl.num_programs(0) - 1)
+    def _():
+        rows_ref[...] = total[...].astype(BF16)
+
+
+def lookup(table_t, local_ids, tile=512):
+    width, vocab = table_t.shape
+    count = local_ids.shape[0]
+    return pl.pallas_call(
+        lookup_kernel,
+        grid=(vocab // tile,),
+        in_specs=[
+            whole((count, 1)),
+            pl.BlockSpec((width, tile), lambda i: (0, i)),
+        ],
+        out_specs=[
+            pl.BlockSpec((width, tile), lambda i: (0, i)),
+            whole((count, width)),
+        ],
+        out_shape=[
+            jax.ShapeDtypeStruct((width, vocab), BF16),
+            jax.ShapeDtypeStruct((count, width), BF16),
+        ],
+        scratch_shapes=[pltpu.VMEM((count, width), F32)],
+        compiler_params=params(),
+        cost_estimate=pl.CostEstimate(
+            flops=2 * count * width * vocab, bytes_accessed=6 * width * vocab, transcendentals=0
+        ),
+    )(local_ids[:, None], table_t)
+
+
+def logits_kernel(states_ref, targets_ref, table_ref, raised_ref, stats_ref, logits, *, tile):
+    vocab = table_ref.shape[1]
+    rows = states_ref.shape[0]
+    states = states_ref[...]
+    high = jnp.full((rows, 1), -jnp.inf, F32)
+    for start in range(0, vocab, tile):
+        part = dot(states, table_ref[:, start : start + tile])
+        logits[:, start : start + tile] = part
+        high = jnp.maximum(high, jnp.max(part, axis=-1, keepdims=True))
+    total = jnp.zeros((rows, 128), F32)
+    picked = jnp.zeros((rows, 128), F32)
+    targets = targets_ref[...]
+    lanes = lax.broadcasted_iota(jnp.int32, (1, 128), 1)
+    for start in range(0, vocab, 128):
+        part = logits[:, start : start + 128]
+        raised = jnp.exp(part - high)
+        raised_ref[:, start : start + 128] = raised.astype(BF16)
+        total += raised
+        picked += jnp.where(targets == lanes + start, part, 0.0)
+    total = jnp.sum(total, axis=-1, keepdims=True)
+    picked = jnp.sum(picked, axis=-1, keepdims=True)
+    stats_ref[...] = jnp.where(lanes == 0, high, jnp.where(lanes == 1, total, picked))
+
+
+def head_logits(states, targets, table_low, rows=256, tile=512):
+    count, width = states.shape
+    vocab = table_low.shape[1]
+    return pl.pallas_call(
+        functools.partial(logits_kernel, tile=tile),
+        grid=(count // rows,),
+        in_specs=[
+            pl.BlockSpec((rows, width), lambda i: (i, 0)),
+            pl.BlockSpec((rows, 1), lambda i: (i, 0)),
+            whole((width, vocab)),
+        ],
+        out_specs=[
+            pl.BlockSpec((rows, vocab), lambda i: (i, 0)),
+            pl.BlockSpec((rows, 128), lambda i: (i, 0)),
+        ],
+        out_shape=[
+            jax.ShapeDtypeStruct((count, vocab), BF16),
+            jax.ShapeDtypeStruct((count, 128), F32),
+        ],
+        scratch_shapes=[pltpu.VMEM((rows, vocab), F32)],
+        compiler_params=params(),
+        cost_estimate=pl.CostEstimate(
+            flops=2 * count * width * vocab,
+            bytes_accessed=2 * vocab * (width + count),
+            transcendentals=count * vocab,
+        ),
+    )(states, targets[:, None], table_low)
+
+
+def states_kernel(raised_ref, scales_ref, targets_ref, table_ref, grads_ref, out_ref, *, tile):
+    vocab = table_ref.shape[1]
+    weight = scales_ref[:, 1:2]
+    factor = scales_ref[:, 0:1]
+    targets = targets_ref[...]
+    total = None
+    for start in range(0, vocab, tile):
+        lanes = lax.broadcasted_iota(jnp.int32, (1, tile), 1) + start
+        chances = raised_ref[:, start : start + tile].astype(F32) * factor
+        part = (jnp.where(targets == lanes, chances - weight, chances)).astype(BF16)
+        grads_ref[:, start : start + tile] = part
+        found = dot(part, table_ref[:, start : start + tile], ((1,), (1,)))
+        total = found if total is None else total + found
+    out_ref[...] = total.astype(BF16)
+
+
+def head_states(raised, factors, weights, targets, table_low, rows=256, tile=512):
+    count, vocab = raised.shape
+    width = table_low.shape[0]
+    scales = jnp.stack([factors * weights, weights], axis=1)
+    return pl.pallas_call(
+        functools.partial(states_kernel, tile=tile),
+        grid=(count // rows,),
+        in_specs=[
+            pl.BlockSpec((rows, vocab), lambda i: (i, 0)),
+            pl.BlockSpec((rows, 2), lambda i: (i, 0)),
+            pl.BlockSpec((rows, 1), lambda i: (i, 0)),
+            whole((width, vocab)),
+        ],
+        out_specs=[
+            pl.BlockSpec((rows, vocab), lambda i: (i, 0)),
+            pl.BlockSpec((rows, width), lambda i: (i, 0)),
+        ],
+        out_shape=[
+            jax.ShapeDtypeStruct((count, vocab), BF16),
+            jax.ShapeDtypeStruct((count, width), BF16),
+        ],
+        compiler_params=params(),
+        cost_estimate=pl.CostEstimate(
+            flops=2 * count * width * vocab,
+            bytes_accessed=2 * vocab * (width + 2 * count),
+            transcendentals=0,
+        ),
+    )(raised, scales, targets[:, None], table_low)
+
+
+def table_kernel(half_ref, states_ref, grads_ref, out_ref):
+    out_ref[...] = dot(states_ref[...], grads_ref[...]).astype(BF16)
+
+
+def head_table(states_t, grads, half, tile=512):
+    width, count = states_t.shape
+    vocab = grads.shape[1] // 2
+    tile = min(tile, vocab)
+    steps = vocab // tile
+    return pl.pallas_call(
+        table_kernel,
+        grid_spec=pltpu.PrefetchScalarGridSpec(
+            num_scalar_prefetch=1,
+            grid=(steps,),
+            in_specs=[
+                whole((width, count)),
+                pl.BlockSpec((count, tile), lambda i, half: (0, half[0] * steps + i)),
+            ],
+            out_specs=pl.BlockSpec((width, tile), lambda i, half: (0, i)),
+        ),
+        out_shape=jax.ShapeDtypeStruct((width, vocab), BF16),
+        compiler_params=params(),
+        cost_estimate=pl.CostEstimate(
+            flops=2 * count * width * vocab,
+            bytes_accessed=2 * (vocab * (width + count) + width * count),
+            transcendentals=0,
+        ),
+    )(jnp.reshape(half, (1,)).astype(jnp.int32), states_t, grads)
+
+
+def place_kernel(
+    starts_ref,
+    half_ref,
+    ranks_ref,
+    ids_ref,
+    rows_ref,
+    mine_ref,
+    other_ref,
+    out_ref,
+    square_ref,
+    sorted_rows,
+    *,
+    chunk,
+    block,
+):
+    step = pl.program_id(0)
+    steps = pl.num_programs(0)
+    tile = out_ref.shape[1]
+    pieces, _, lanes = rows_ref.shape
+
+    @pl.when(step == 0)
+    def _():
+        def sort(k, carry):
+            columns = pl.ds(pl.multiple_of(k * block, block), block)
+            wanted = lax.broadcasted_iota(jnp.int32, (1, block), 1) + k * block
+            total = None
+            for piece in range(0, min(pieces, 32), 2):
+                total = sort_pair(piece, wanted, total)
+            if pieces > 32:
+                total = lax.fori_loop(
+                    16, pieces // 2, lambda p, t: sort_pair(2 * p, wanted, t), total
+                )
+            sorted_rows[:, columns] = total.astype(BF16)
+            return carry
+
+        def sort_pair(piece, wanted, total):
+            start = piece * lanes
+            if not isinstance(piece, int):
+                start = pl.multiple_of(start, 2 * lanes)
+            pick = jnp.where(ranks_ref[pl.ds(start, 2 * lanes), :] == wanted, 1.0, 0.0)
+            pair = jnp.concatenate([rows_ref[piece], rows_ref[piece + 1]], axis=1)
+            found = dot(pair, pick.astype(BF16))
+            return found if total is None else total + found
+
+        lax.fori_loop(0, (starts_ref[steps] + block - 1) // block, sort, 0)
+
+    first = starts_ref[step]
+    last = starts_ref[step + 1]
+    is_mine = (step * 2 >= steps) == (half_ref[0] == 1)
+
+    @pl.when(is_mine)
+    def _():
+        out_ref[...] = mine_ref[...].astype(F32)
+
+    @pl.when(jnp.logical_not(is_mine))
+    def _():
+        out_ref[...] = other_ref[...].astype(F32)
+
+    columns = lax.broadcasted_iota(jnp.int32, (1, tile), 1) + step * tile
+
+    def add(k, carry):
+        rows = pl.ds(pl.multiple_of(k * chunk, chunk), chunk)
+        place = lax.broadcasted_iota(jnp.int32, (chunk, 1), 0) + k * chunk
+        ids = ids_ref[rows, :]
+        inside = jnp.logical_and(place >= first, place < last)
+        pick = jnp.where(jnp.logical_and(ids == columns, inside), 1.0, 0.0).astype(BF16)
+        out_ref[...] += dot(sorted_rows[:, rows], pick)
+        return carry
+
+    lax.fori_loop(first // chunk, (last + chunk - 1) // chunk, add, 0)
+    value = out_ref[...]
+    squares = jnp.sum(value * value, axis=0, keepdims=True)
+    part = jnp.zeros((1, 128), F32)
+    for start in range(0, tile, 128):
+        part += squares[:, start : start + 128]
+
+    @pl.when(step == 0)
+    def _():
+        square_ref[...] = part
+
+    @pl.when(step > 0)
+    def _():
+        square_ref[...] += part
+
+
+def place_rows(mine, other, half, rows, ranks, ids, starts, tile, chunk=128, block=512):
+    width, half_vocab = mine.shape
+    pieces, _, lanes = rows.shape
+    total = pieces * lanes
+    steps = 2 * half_vocab // tile
+    halves = steps // 2
+
+    def half_map(wanted):
+        def index(i, starts, half):
+            low = jnp.where(half[0] == wanted, 0, halves)
+            return (0, jnp.clip(i - low, 0, halves - 1))
+
+        return index
+
+    return pl.pallas_call(
+        functools.partial(place_kernel, chunk=chunk, block=block),
+        grid_spec=pltpu.PrefetchScalarGridSpec(
+            num_scalar_prefetch=2,
+            grid=(steps,),
+            in_specs=[
+                whole((total, 1)),
+                whole((total, 1)),
+                whole((pieces, width, lanes)),
+                pl.BlockSpec((width, tile), half_map(0)),
+                pl.BlockSpec((width, tile), half_map(1)),
+            ],
+            out_specs=[
+                pl.BlockSpec((width, tile), lambda i, starts, half: (0, i)),
+                whole((1, 128)),
+            ],
+            scratch_shapes=[pltpu.VMEM((width, total), BF16)],
+        ),
+        out_shape=[
+            jax.ShapeDtypeStruct((width, 2 * half_vocab), F32),
+            jax.ShapeDtypeStruct((1, 128), F32),
+        ],
+        compiler_params=params(),
+        cost_estimate=pl.CostEstimate(
+            flops=2 * 16 * chunk * tile * width,
+            bytes_accessed=12 * width * half_vocab + 2 * total * width,
+            transcendentals=0,
+        ),
+    )(
+        starts,
+        jnp.reshape(half, (1,)).astype(jnp.int32),
+        ranks[:, None],
+        ids[:, None],
+        rows,
+        mine,
+        other,
+    )
+
+
+def adam_kernel(scale_ref, w_ref, m_ref, v_ref, g_ref, wn_ref, mn_ref, vn_ref, low_ref, *, rate):
+    new = adam_update(
+        w_ref[...], m_ref[...], v_ref[...], g_ref[...] * scale_ref[0], rate
+    )
+    wn_ref[...], mn_ref[...], vn_ref[...], low_ref[...] = new
+
+
+def adam(master, first, second, gradient, scale, rate, tile):
+    rows, columns = master.shape
+    spec = pl.BlockSpec((rows, tile), lambda i: (0, i))
+    shape = jax.ShapeDtypeStruct((rows, columns), F32)
+    return pl.pallas_call(
+        functools.partial(adam_kernel, rate=rate),
+        grid=(columns // tile,),
+        in_specs=[pl.BlockSpec(memory_space=pltpu.SMEM)] + [spec] * 4,
+        out_specs=[spec] * 4,
+        out_shape=[shape] * 3 + [jax.ShapeDtypeStruct((rows, columns), BF16)],
+        compiler_params=params(),
+        cost_estimate=pl.CostEstimate(
+            flops=20 * rows * columns, bytes_accessed=30 * rows * columns, transcendentals=0
+        ),
+    )(jnp.reshape(scale, (1,)), master, first, second, gradient)
+
+
+def place_tokens(mine, other, half, rows, ranks, ids, starts, tile):
+    pieces, width, lanes = rows.shape
+    if pieces * lanes <= 4096:
+        return place_rows(mine, other, half, rows, ranks, ids, starts, tile)
+    total = jnp.where(
+        half == 1, jnp.concatenate([other, mine], 1), jnp.concatenate([mine, other], 1)
+    ).astype(F32)
+    tokens_ids = jnp.take(ids, ranks).reshape(pieces, lanes)
+    columns = jnp.arange(total.shape[1], dtype=jnp.int32)
+
+    def add(total, operands):
+        part, part_ids = operands
+        pick = (part_ids[:, None] == columns[None, :]).astype(BF16)
+        return total + dot(part, pick), None
+
+    total, _ = lax.scan(add, total, (rows, tokens_ids))
+    return total, jnp.sum(total * total)
 
 
 class Links:
@@ -122,24 +496,23 @@
                 jnp.where(inner, down[1], jnp.where(z == 0, down[3], up[3])),
             )
         )
-        out = jnp.zeros((self.n * rows,) + value.shape[1:], value.dtype)
-        zeros = (0,) * (value.ndim - 1)
+        out = jnp.zeros((self.n,) + value.shape, value.dtype)
         for source, block in blocks:
-            out = lax.dynamic_update_slice(
-                out, block, ((source * self.wide + self.w) * rows,) + zeros
-            )
+            out = lax.dynamic_update_index_in_dim(out, block, source * self.wide + self.w, 0)
             for step in range(1, self.wide):
                 other = self.across(block, step)
                 place = source * self.wide + (self.w - step) % self.wide
-                out = lax.dynamic_update_slice(out, other, (place * rows,) + zeros)
-        return out
+                out = lax.dynamic_update_index_in_dim(out, other, place, 0)
+        return out.reshape((self.n * rows,) + value.shape[1:])
 
     def scatter(self, value):
         rows = value.shape[0] // self.n
         kind = value.dtype
 
+        blocks = value.reshape((self.n, rows) + value.shape[1:])
+
         def block(z, w):
-            return lax.dynamic_slice_in_dim(value, (z * self.wide + w) * rows, rows, 0)
+            return lax.dynamic_index_in_dim(blocks, z * self.wide + w, 0, False)
 
         parts = [None] * LINE
         for k in (2, 1, 3, 0):
@@ -164,6 +537,15 @@
 
     def core(self, value):
         return lax.ppermute(value, "rep", [(r, r ^ 1) for r in range(self.n_rep)])
+
+    def rep_sum(self, value):
+        rep = lax.axis_index("rep")
+        core, chip = rep % 2, rep // 2
+        value = value.astype(BF16).reshape((2, 2, -1) + value.shape[1:])
+        mine = lax.dynamic_index_in_dim(value, core, 1, False).astype(F32)
+        mine = mine + self.core(lax.dynamic_index_in_dim(value, 1 - core, 1, False)).astype(F32)
+        sent = lax.dynamic_index_in_dim(mine, 1 - chip, 0, False).astype(BF16)
+        return lax.dynamic_index_in_dim(mine, chip, 0, False) + self.chip(sent).astype(F32)
 
     def chip(self, value):
         return lax.ppermute(value, "rep", [(r, r ^ 2) for r in range(self.n_rep)])
@@ -220,7 +602,7 @@
         packed = jnp.stack([token_ids, target_ids, loss_mask])
         reps = lax.all_gather(packed, "rep")
         everyone = links.spread(reps)
-        all_ids = everyone[:, :, 0].transpose(1, 0, 2).reshape(-1)
+        all_ids = everyone[:, :, 0].reshape(-1) - vocab_start
         all_mask = everyone[:, :, 2].astype(F32)
         valid_count = jnp.sum(all_mask)
         group = lax.dynamic_index_in_dim(everyone, my_rep, 1, False)
@@ -231,25 +613,39 @@
         def halves(master):
             return my_half(master[0].astype(BF16))[0]
 
+        unit_rows = FF // n_shard
+        unit_part = unit_rows // n_rep
+        units = n_shard * unit_part
+        mlp_in_part = mlp_in_master[0].astype(BF16)
+        mlp_in_part = mlp_in_part.reshape(-1, 2, n_shard, n_rep, unit_part)
+        mlp_in_part = lax.dynamic_index_in_dim(mlp_in_part, my_rep, 3, False).reshape(-1, 2 * units)
+        mlp_out_part = mlp_out_master[0].astype(BF16).reshape(n_rep, unit_part, D)
+        mlp_out_part = lax.dynamic_index_in_dim(mlp_out_part, my_rep, 0, False)
         attn_mine = links.gather(
             jnp.concatenate([halves(attn_in_master), halves(attn_out_master)], 1)
         )
+        mlp_in = lax.all_gather(mlp_in_part, "shard", tiled=True)
+        mlp_out = lax.all_gather(mlp_out_part, "shard", tiled=True)
         in_cols = attn_in_master.shape[2] // 2
         attn_other = links.core(attn_mine)
         attn_in = (attn_mine[:, :in_cols], attn_other[:, :in_cols])
         attn_out = (attn_mine[:, in_cols:], attn_other[:, in_cols:])
         gains = links.spread(gain_master.astype(BF16)).transpose(1, 0, 2).reshape(3, D).astype(F32)
 
-        table_t = table_master.T.astype(BF16)
-        vocab_iota = jnp.arange(vocab_rows, dtype=jnp.int32)
-        pick = (group_ids[:, None] - vocab_start == vocab_iota[None, :]).astype(BF16)
-        looked = dot(pick, table_t, ((1,), (1,))).astype(BF16)
+        vocab_tile = min(512, vocab_rows)
+        table_low, looked = lookup(table_master.T, group_ids - vocab_start, vocab_tile)
         values = links.scatter(looked)
 
-        mlp_in_mine = links.gather(halves(mlp_in_master))
-        mlp_out_mine = links.gather(halves(mlp_out_master))
-        mlp_in = (mlp_in_mine, links.core(mlp_in_mine))
-        mlp_out = (mlp_out_mine, links.core(mlp_out_mine))
+        owned_here = (all_ids >= 0) & (all_ids < vocab_rows)
+        sort_ids = jnp.where(owned_here, all_ids, vocab_rows)
+        tokens = jnp.arange(sort_ids.shape[0], dtype=jnp.int32)
+        before = (sort_ids[None, :] < sort_ids[:, None]) | (
+            (sort_ids[None, :] == sort_ids[:, None]) & (tokens[None, :] < tokens[:, None])
+        )
+        ranks = jnp.sum(before.astype(jnp.int32), axis=1)
+        sorted_ids = jnp.sort(sort_ids)
+        edges = jnp.arange(0, vocab_rows + 1, vocab_tile, dtype=jnp.int32)
+        starts = jnp.sum((sort_ids[None, :] < edges[:, None]).astype(jnp.int32), axis=1)
 
         def times(value, pair):
             return dot(value, pair[0]), dot(value, pair[1])
@@ -299,40 +695,35 @@
         middle = values + in_order(*times(attended, attn_out))
         normed_two, norm_two_back = jax.vjp(rms_norm, middle, gains[1])
         normed_two = normed_two.astype(BF16)
-        part_mine, part_other = times(normed_two, mlp_in)
-        gate = jnp.where(second_core, part_other, part_mine)
-        up = jnp.where(second_core, part_mine, part_other)
-        hidden, glu_back = jax.vjp(swiglu, gate, up)
+        normed_all = lax.all_gather(normed_two, "rep", tiled=True)
+        gate_up = dot(normed_all, mlp_in)
+        hidden, glu_back = jax.vjp(swiglu, gate_up[:, :units], gate_up[:, units:])
         hidden = hidden.astype(BF16)
-        result = middle + in_order(*times(hidden, mlp_out))
+        result = middle + links.rep_sum(dot(hidden, mlp_out))
         final, final_back = jax.vjp(rms_norm, result, gains[2])
 
         states = links.gather(final.astype(BF16))
-        logits = dot(states, table_t)
         local_targets = group_targets - vocab_start
-        hit = local_targets[:, None] == vocab_iota[None, :]
-        high = jnp.max(logits, axis=-1)
-        raised = jnp.exp(logits - high[:, None])
-        stats = jnp.stack(
-            [high, jnp.sum(raised, axis=-1), jnp.sum(jnp.where(hit, logits, 0.0), axis=-1)]
-        )
-        stats = links.spread(stats)
+        raised, stats = head_logits(states, local_targets, table_low)
+        high = stats[:, 0]
+        stats = links.spread(stats[:, :3].T)
         top = jnp.max(stats[:, 0], axis=0)
         log_totals = top + jnp.log(jnp.sum(stats[:, 1] * jnp.exp(stats[:, 0] - top), axis=0))
         picked = jnp.sum(stats[:, 2], axis=0)
         group_loss = jnp.sum((log_totals - picked) * group[:, 2].reshape(-1).astype(F32))
-        grad_logits = (
-            (jnp.exp(logits - log_totals[:, None]) - jnp.where(hit, 1.0, 0.0))
-            * group_weights[:, None]
-        ).astype(BF16)
-        grad_states = dot(grad_logits, table_t, ((1,), (1,))).astype(BF16)
+        grad_logits, grad_states = head_states(
+            raised, jnp.exp(high - log_totals), group_weights, local_targets, table_low
+        )
         grad_final = links.scatter(grad_states)
 
-        table_grad = dot(states, grad_logits, ((0,), (0,))).astype(BF16)
-        grad_mine, grad_other = my_half(table_grad)
-        chip_sum = (grad_mine.astype(F32) + links.core(grad_other).astype(F32)).astype(BF16)
+        my_core = my_rep % 2
+        states_t = states.T
+        grad_other = links.core(head_table(states_t, grad_logits, 1 - my_core))
+        grad_mine = head_table(states_t, grad_logits, my_core)
+        chip_sum = (grad_mine.astype(F32) + grad_other.astype(F32)).astype(BF16)
+        chip_sum, grad_final = lax.optimization_barrier((chip_sum, grad_final))
         half_sum = (chip_sum.astype(F32) + links.chip(chip_sum).astype(F32)).astype(BF16)
-        table_sum = in_order(half_sum, links.core(half_sum)).astype(F32)
+        other_sum = links.core(half_sum)
 
         grad_output, grad_gain_three = final_back(grad_final)
 
@@ -345,22 +736,30 @@
             part = part.astype(F32) + links.chip(part).astype(F32)
             return part, links.core(part)
 
-        branch_mine, branch_other = my_half(grad_output.astype(BF16))
-        grad_mlp_out = weight_grad(hidden, branch_mine, branch_other)
-        grad_hidden = times_back(branch_mine, branch_other, mlp_out)
-        grad_gate, grad_up = glu_back(grad_hidden)
-        grad_gate = grad_gate.astype(BF16)
-        grad_up = grad_up.astype(BF16)
-        glu_mine = jnp.where(second_core, grad_up, grad_gate)
-        glu_other = jnp.where(second_core, grad_gate, grad_up)
-        grad_mlp_in = weight_grad(normed_two, glu_mine, glu_other)
-        middle_part, grad_gain_two = norm_two_back(times_back(glu_mine, glu_other, mlp_in))
+        branch = lax.all_gather(grad_output.astype(BF16), "rep", tiled=True)
+        grad_mlp_out = dot(hidden, branch, ((0,), (0,))).astype(BF16)
+        grad_hidden = dot(branch, mlp_out, ((1,), (1,)))
+        grad_glu = jnp.concatenate(glu_back(grad_hidden), 1).astype(BF16)
+        grad_mlp_in = dot(normed_all, grad_glu, ((0,), (0,))).astype(BF16)
+        grad_normed_two = links.rep_sum(dot(grad_glu, mlp_in, ((1,), (1,))))
+        middle_part, grad_gain_two = norm_two_back(grad_normed_two)
         grad_middle = grad_output + middle_part
-        mlp_out_sum = in_order(*owned(grad_mlp_out))
-        mlp_in_sum = in_order(*owned(grad_mlp_in))
+
+        in_size = D // n_shard * 2 * units
+        both = jnp.concatenate(
+            [grad_mlp_in.reshape(n_shard, -1), grad_mlp_out.reshape(n_shard, -1)], 1
+        ).reshape(-1, 128)
+        both = lax.psum_scatter(both, "shard", tiled=True).reshape(-1)
+        mlp_in_sum = lax.all_gather(both[:in_size].reshape(-1, 2, n_shard, unit_part), "rep")
+        mlp_in_sum = mlp_in_sum.transpose(1, 2, 3, 0, 4).reshape(-1, 2 * FF).astype(F32)
+        mlp_out_sum = lax.all_gather(both[in_size:].reshape(unit_part, D), "rep", tiled=True)
+        mlp_out_sum = mlp_out_sum.astype(F32)
 
         out_mine, out_other = my_half(grad_middle.astype(BF16))
         grad_attn_out = weight_grad(attended, out_mine, out_other)
+        grad_attn_out = lax.psum_scatter(grad_attn_out, "shard", tiled=True)
+        grad_attn_out = grad_attn_out.astype(F32) + links.chip(grad_attn_out).astype(F32)
+        attn_out_sum = in_order(grad_attn_out, links.core(grad_attn_out))
         grad_attended = times_back(out_mine, out_other, attn_out).astype(BF16)
         grad_heads = (
             grad_attended.reshape(tok_rows, KV_HEADS, group_size, HEAD_DIM)
@@ -390,19 +789,15 @@
         grad_attn_in = weight_grad(normed_one, mixed_mine, mixed_other)
         grad_gains = jnp.stack([grad_gain_one, grad_gain_two, grad_gain_three], 1)
         grad_gains = grad_gains + links.core(grad_gains)
-        small = jnp.concatenate([grad_attn_in, grad_attn_out, grad_gains.astype(BF16)], 1)
+        small = jnp.concatenate([grad_attn_in, grad_gains.astype(BF16)], 1)
         small_mine, small_other = owned(small)
         attn_in_sum = in_order(small_mine[:, :in_cols], small_other[:, :in_cols])
-        out_end = in_cols + D // 2
-        attn_out_sum = in_order(small_mine[:, in_cols:out_end], small_other[:, in_cols:out_end])
-        gain_sum = small_mine[:, out_end:].T
-
-        embedded = lax.all_gather(grad_values, "rep").transpose(1, 0, 2).reshape(tok_rows, -1)
-        embedded = links.gather(embedded).reshape(seq_len, n_rep, D).transpose(1, 0, 2)
-        embedded = embedded.reshape(n_rep * seq_len, D)
-        place = (all_ids[:, None] - vocab_start == vocab_iota[None, :]).astype(BF16)
-        table_sum = table_sum + dot(embedded, place, ((0,), (0,)))
-
+        gain_sum = small_mine[:, in_cols:].T
+
+        embedded = links.gather(lax.all_gather(grad_values.T, "rep"))
+        table_sum, table_squares = place_tokens(
+            half_sum, other_sum, my_core, embedded, ranks, sorted_ids, starts, vocab_tile
+        )
         sums = (
             table_sum,
             attn_in_sum[None],
@@ -411,8 +806,8 @@
             mlp_out_sum[None],
             gain_sum,
         )
-        squares = jnp.zeros((), F32)
-        for gradient in sums:
+        squares = jnp.sum(table_squares)
+        for gradient in sums[1:]:
             squares = squares + jnp.sum(gradient * gradient)
         loss = group_loss + links.core(group_loss)
         loss_sum = loss + links.chip(loss)
@@ -445,17 +840,20 @@
             gain_second,
         )
         rate_list = rates(seq_len)
-        for member in range(6):
-            new = adam_update(
-                masters[member],
-                firsts[member],
-                seconds[member],
-                sums[member] * clip_scale,
-                rate_list[member],
+        new = adam(
+            masters[0], firsts[0], seconds[0], sums[0], clip_scale, rate_list[0], vocab_tile
+        )
+        results.extend(part.T for part in new)
+        for member in range(1, 6):
+            results.extend(
+                adam_update(
+                    masters[member],
+                    firsts[member],
+                    seconds[member],
+                    sums[member] * clip_scale,
+                    rate_list[member],
+                )
             )
-            if member == 0:
-                new = tuple(part.T for part in new)
-            results.extend(new)
         return tuple(results)
 
     return local

time: 1190 us -> 1240 us (1.042); the launches traced: 1180 us -> 1220 us
  Pallas kernels: 0 us -> 182 us
  matrix products: 224 us -> 59.7 us
  waiting for transfers between devices: 313 us -> 179 us
  local copies, waits for them, and re-layouts: 146 us -> 269 us
  blocking collectives: 14.9 us -> 127 us
  other arithmetic: 235 us -> 153 us
  starting transfers between devices: 234 us -> 219 us
  between operations: 12.6 us -> 26 us
    pallas_call x0 -> x7, Pallas kernels: none -> 182 us  [the longest x1 57.5 us: adam(): pl.pallas_call(functools.partial(adam_kernel, rate=rate), grid=(columns /...]
    dot_general x29 -> x18, matrix products: 205 us -> 37.2 us  [dot(): return lax.dot_general(a, b, (dims, ((), ())), preferred_element_type=F32)]
    all_gather x1 -> x4, blocking collectives: 9.71 us -> 121 us  [the longest x1 88.9 us: local(): embedded = links.gather(lax.all_gather(grad_values.T, 'rep'))]
    ppermute x48 -> x32, waiting for transfers between devices: 128 us -> 35.2 us  [across(): return lax.ppermute(value, 'shard', pairs)]
    ppermute x5 -> x6, waiting for transfers between devices: 91.2 us -> 14.7 us  [chip(): return lax.ppermute(value, 'rep', [(r, r ^ 2) for r in range(self.n_rep)])]
    transpose x1, other arithmetic: 70.1 us -> 0.21 us  [local(): embedded = links.gather(lax.all_gather(grad_values.T, 'rep'))]
    dynamic_update_slice x29 -> x22, local copies, waits for them, and re-layouts: 56.7 us -> 114 us  [the longest x16 65.2 us: gather(): out = lax.dynamic_update_index_in_dim(out, other, place, 0)]
    ppermute x72 -> x48, starting transfers between devices: 158 us -> 119 us  [along(): return lax.ppermute(value, 'shard', pairs)]
  transfers between devices with their start and end apart: 143 -> 106, of which waited for: 58 -> 41; matrix products, arithmetic and copies ran while one was open for 25% -> 26% of each run, Pallas kernels for 0% -> 3%
where the time goes in v2:
time: 1240 us; the launch traced here: 1220 us
  local copies, waits for them, and re-layouts  269 us (22%)
  starting transfers between devices  219 us (18%)
  Pallas kernels  182 us (15%)
  waiting for transfers between devices  179 us (14%)
  other arithmetic  153 us (12%)
  blocking collectives  127 us (10%)
  matrix products  59.7 us (5%)
  between operations  26 us (2%)
    ppermute x48, starting transfers between devices, along(): return lax.ppermute(value, 'shard', pairs)  119 us
    all_gather x1, blocking collectives, local(): embedded = links.gather(lax.all_gather(grad_values.T, 'rep'))  88.9 us
    ppermute x48, waiting for transfers between devices, along(): return lax.ppermute(value, 'shard', pairs)  80.7 us
    dynamic_update_slice x16, local copies, waits for them, and re-layouts, gather(): out = lax.dynamic_update_index_in_dim(out, other, place, 0)  65.2 us
    unnamed x242, local copies, waits for them, and re-layouts  61.4 us
    pallas_call x1, Pallas kernels, adam(): pl.pallas_call(functools.partial(adam_kernel, rate=rate), grid=(columns /...  57.5 us
    all_to_all x4, starting transfers between devices, spread(): return lax.all_to_all(many, 'shard', 0, 0, tiled=True)  53.5 us
    dynamic_update_slice x6, local copies, waits for them, and re-layouts, gather(): lax.dynamic_update_index_in_dim(out, block, source * self.wide + self.w, 0)  48.8 us
  transfers between devices with their start and end apart: 106, of which 41 were waited for; matrix products, arithmetic and copies ran while one was open for 26% of the time, Pallas kernels for 3%

profile of v2, /device:TPU:0, one launch (start us, length us, event | category | flops | bytes accessed | tf_op | source)
XLA Modules:
  0.0 1216.0 jit_solution(13064488696691343690)
XLA Ops:
  38.7 26.7 %shard_map.412 = (bf16[960,6144]{1,0:T(8,128)(2,1)}, bf16[1024,960]{1,0:T(8,128)(2,1)}) custom-call(s32[1024,1]{1,0:T(8,128)} %copy.522.ids_ref, f32[960,6144]{1,0:T(8,128)} %bitcast.389), custom_call_target="tpu_custom_call" | custom-call | flops 12079595520 | bytes 35389440 | tf_op jit(solution)/shard_map/pallas_call | solution.py:120
  129.6 12.2 %all-to-all-start.1 = ((bf16[8,3,120]{2,1,0:T(4,128)(2,1)}), bf16[8,3,120]{2,1,0:T(4,128)(2,1)S(1)}, u32[]{:S(2)}, u32[]{:S(2)}) async-start(bf16[8,3,120]{2,1,0:T(4,128)(2,1)} %broadcast_in_dim.190), calls=%async_computation.1 | async-start | bytes 16384 | tf_op jit(solution)/shard_map/all_to_all | solution.py:536
  161.6 13.5 %collective-permute-done.9 = bf16[128,960]{0,1:T(8,128)(2,1)} collective-permute-done((bf16[128,960]{0,1:T(8,128)(2,1)}, bf16[128,960]{0,1:T(8,128)(2,1)}, u32[]{:S(2)}, u32[]{:S(2)}) %collective-permute-start.9) | collective-permute-done | bytes 245792 | tf_op jit(solution)/shard_map/ppermute | solution.py:469
  244.2 11.6 all_gather.32
  269.2 8.1 collective-permute-done.32
  309.8 11.5 dynamic_update_slice.116
  323.4 11.4 dynamic_update_slice.117
  343.2 11.4 dynamic_update_slice.118
  358.9 11.4 dynamic_update_slice.119
  370.3 11.5 dynamic_update_slice.120
  381.8 11.5 dynamic_update_slice.121
  393.3 11.5 dynamic_update_slice.122
  404.7 11.5 dynamic_update_slice.123
  422.2 27.3 %shard_map.413 = (bf16[1024,6144]{1,0:T(8,128)(2,1)}, f32[1024,128]{1,0:T(8,128)}) custom-call(bf16[1024,960]{1,0:T(8,128)(2,1)} %copy.547.states_ref, s32[1024,1]{1,0:T(8,128)} %copy.548.targets_ref, bf16[960,6144]{1,0:T(8,128)(2,1)} %get-tuple-element.44.table_ref), custom_call_target="tpu_custom_call" | custom-call | flops 12079595520 | bytes 24379392 | tf_op jit(solution)/shard_map/pallas_call | solution.py:170
  472.1 21.1 %shard_map.414 = (bf16[1024,6144]{1,0:T(8,128)(2,1)}, bf16[1024,960]{1,0:T(8,128)(2,1)}) custom-call(bf16[1024,6144]{1,0:T(8,128)(2,1)} %get-tuple-element.47.raised_ref, f32[1024,2]{1,0:T(8,128)} %pad_maximum_fusion.6.scales_ref, s32[1024,1]{1,0:T(8,128)} %copy.548.targets_ref, bf16[960,6144]{1,0:T(8,128)(2,1)} %get-tuple-element.44.table_ref), custom_call_target="tpu_custom_call" | custom-call | flops 12079595520 | bytes 36962304 | tf_op jit(solution)/shard_map/pallas_call | solution.py:216
  493.3 11.1 shard_map.416
  547.5 10.9 shard_map.415
  562.4 9.7 add_convert_fusion.1
  572.6 9.1 all_gather.35
  630.0 10.3 collective-permute-start.62
  701.8 88.9 %all-gather.2 = bf16[3840,128]{1,0:T(8,128)(2,1)} all-gather(bf16[960,128]{1,0:T(8,128)(2,1)S(1)} %fusion.76), channel_id=4, replica_groups=mesh['rep'=4,'shard'=8] {'rep'}, dimensions={0}, use_global_device_ids=true | all-gather | bytes 1228800 | tf_op jit(solution)/shard_map/all_gather | solution.py:797
  800.6 12.0 pad_maximum_fusion
  841.4 9.7 add_convert_fusion.mine_ref
  851.2 19.7 %convert_reduce_fusion = s32[4096]{0:T(1024)S(1)} fusion(s32[4096]{0:T(1024)S(1)} %copy-done.75), kind=kLoop, calls=%fused_computation.1 | loop fusion | flops 117436416 | bytes 32768 | tf_op jit(solution)/shard_map/reduce_sum | solution.py:645
  891.9 8.2 collective-permute-start.86
  928.0 37.3 %all-reduce.5.cloned.1.call-done = bf16[14400,128]{1,0:T(8,128)(2,1)} async-done(((bf16[14400,128]{1,0:T(8,128)(2,1)}), bf16[14400,128]{1,0:T(8,128)(2,1)}) %all-reduce.5.cloned.1.call-update) | async-done | bytes 3686416
  969.8 10.3 collective-permute-start.88
  985.0 11.8 all_gather.39
  1013.6 15.2 %collective-permute-done.77 = bf16[4,960,128]{2,1,0:T(8,128)(2,1)S(1)} collective-permute-done((bf16[4,960,128]{2,1,0:T(8,128)(2,1)S(1)}, bf16[4,960,128]{2,1,0:T(8,128)(2,1)S(1)}, u32[]{:S(2)}, u32[]{:S(2)}) %collective-permute-start.77) | collective-permute-done | bytes 983072 | tf_op jit(solution)/shard_map/ppermute | solution.py:477
  1029.9 27.6 %shard_map.417 = (f32[960,6144]{1,0:T(8,128)}, f32[1,128]{1,0:T(1,128)}) custom-call(s32[13]{0:T(128)} %convert_reduce_fusion.1.starts_ref, s32[1]{0:T(128)} %bitcast.67.half_ref, s32[4096,1]{1,0:T(8,128)} %copy.578.ranks_ref, s32[4096,1]{1,0:T(8,128)} %copy.579.ids_ref, bf16[32,960,128]{2,1,0:T(8,128)(2,1)} %bitcast.114.rows_ref, ...), custom_call_target="tpu_custom_call" | custom-call | flops 2013265920 | bytes 43253760 | tf_op jit(solution)/shard_map/pallas_call | solution.py:371
  1063.4 27.1 %all-to-all-start.3 = ((f32[8,8,128]{2,1,0:T(8,128)}), f32[8,8,128]{2,1,0:T(8,128)S(1)}, u32[]{:S(2)}, u32[]{:S(2)}) async-start(f32[8,8,128]{2,1,0:T(8,128)} %broadcast_in_dim_broadcast_in_dim_broadcast_in_dim.3), calls=%async_computation.4 | async-start | bytes 65536 | tf_op jit(solution)/shard_map/all_to_all | solution.py:536
  1149.6 57.5 %shard_map.418 = (f32[960,6144]{1,0:T(8,128)}, f32[960,6144]{1,0:T(8,128)}, f32[960,6144]{1,0:T(8,128)}, bf16[960,6144]{1,0:T(8,128)(2,1)}) custom-call(f32[1]{0:T(128)} %bitcast.130.scale_ref, f32[960,6144]{1,0:T(8,128)} %bitcast.390, f32[960,6144]{1,0:T(8,128)} %bitcast.391, f32[960,6144]{1,0:T(8,128)} %bitcast.392, f32[960,6144]{1,0:T(8,128)} %get-tuple-element.53.g_ref), custom_call_target="tpu_custom_call" | custom-call | flops 117964800 | bytes 176947200 | tf_op jit(solution)/shard_map/pallas_call | solution.py:421
  (685 shorter events, 601.4 us)
Async XLA Ops:
  21.0 234.8 %all-gather.8.cloned.1.call-start = ((), (), s32[]{:S(2)}) async-start(), calls=%async_computation.5 | async-start | bytes 2764800 | tf_op jit(solution)/shard_map/all_gather | solution.py:627
  38.4 34.3 %collective-permute-start.13 = (bf16[120,1280]{1,0:T(8,128)(2,1)}, bf16[120,1280]{1,0:T(8,128)(2,1)}, u32[]{:S(2)}, u32[]{:S(2)}) collective-permute-start(bf16[120,1280]{1,0:T(8,128)(2,1)} %get-tuple-element.303), channel_id=1, source_target_pairs={{0,1},{1,0},{2,3},{3,2},{4,5},{5,4},{6,7},{7,6},{8,9},{9,8},{10,11... | collective-permute-start | bytes 921608 | tf_op jit(solution)/shard_map/ppermute | solution.py:477
  88.9 27.1 %collective-permute-start.2 = (bf16[128,960]{0,1:T(8,128)(2,1)}, bf16[128,960]{0,1:T(8,128)(2,1)}, u32[]{:S(2)}, u32[]{:S(2)}) collective-permute-start(bf16[128,960]{0,1:T(8,128)(2,1)} %bitcast.437), channel_id=1, source_target_pairs={{0,1},{1,0},{2,3},{3,2},{4,5},{5,4},{6,7},{7,6},{8,9},{9,8},{10,11... | collective-permute-start | bytes 737288 | tf_op jit(solution)/shard_map/ppermute | solution.py:477
  91.2 24.7 %collective-permute-start.4 = (bf16[128,960]{0,1:T(8,128)(2,1)}, bf16[128,960]{0,1:T(8,128)(2,1)}, u32[]{:S(2)}, u32[]{:S(2)}) collective-permute-start(bf16[128,960]{0,1:T(8,128)(2,1)} %fusion.60), channel_id=1, source_target_pairs={{0,2},{1,3},{8,10},{9,11},{16,18},{17,19},{24,26},{25,27}} | collective-permute-start | bytes 737288 | tf_op jit(solution)/shard_map/ppermute | solution.py:469
  119.7 57.8 %collective-permute-start.20 = (bf16[960,1280]{1,0:T(8,128)(2,1)S(1)}, bf16[960,1280]{1,0:T(8,128)(2,1)}, u32[]{:S(2)}, u32[]{:S(2)}) collective-permute-start(bf16[960,1280]{1,0:T(8,128)(2,1)S(1)} %bitcast.411), channel_id=1, source_target_pairs={{0,8},{8,0},{16,24},{24,16},{1,9},{9,1},{17,25},{25,17},{2,10},{10... | collective-permute-start | bytes 7372808 | tf_op jit(solution)/shard_map/ppermute | solution.py:539
  129.6 27.1 %all-to-all-start.1 = ((bf16[8,3,120]{2,1,0:T(4,128)(2,1)}), bf16[8,3,120]{2,1,0:T(4,128)(2,1)S(1)}, u32[]{:S(2)}, u32[]{:S(2)}) async-start(bf16[8,3,120]{2,1,0:T(4,128)(2,1)} %broadcast_in_dim.190), calls=%async_computation.1 | async-start | bytes 16384 | tf_op jit(solution)/shard_map/all_to_all | solution.py:536
  141.9 120.2 %all-gather.12.cloned.1.call-start = ((), (), s32[]{:S(2)}) async-start(), calls=%async_computation.8 | async-start | bytes 1474560 | tf_op jit(solution)/shard_map/all_gather | solution.py:628
  300.5 38.6 %collective-permute-start.39 = (bf16[128,960]{0,1:T(8,128)(2,1)}, bf16[128,960]{0,1:T(8,128)(2,1)}, u32[]{:S(2)}, u32[]{:S(2)}) collective-permute-start(bf16[128,960]{0,1:T(8,128)(2,1)} %broadcast_select_fusion.4), channel_id=1, source_target_pairs={{0,1},{1,0},{2,3},{3,2},{4,5},{5,4},{6,7},{7,6},{8,9},{9,8},{10,11... | collective-permute-start | bytes 737288 | tf_op jit(solution)/shard_map/ppermute | solution.py:477
  305.1 49.5 %collective-permute-start.36 = (bf16[128,960]{0,1:T(8,128)(2,1)}, bf16[128,960]{0,1:T(8,128)(2,1)}, u32[]{:S(2)}, u32[]{:S(2)}) collective-permute-start(bf16[128,960]{0,1:T(8,128)(2,1)} %get-tuple-element.363), channel_id=1, source_target_pairs={{0,1},{1,0},{2,3},{3,2},{4,5},{5,4},{6,7},{7,6},{8,9},{9,8},{10,11... | collective-permute-start | bytes 737288 | tf_op jit(solution)/shard_map/ppermute | solution.py:477
  306.2 50.6 %collective-permute-start.42 = (bf16[128,960]{0,1:T(8,128)(2,1)}, bf16[128,960]{0,1:T(8,128)(2,1)}, u32[]{:S(2)}, u32[]{:S(2)}) collective-permute-start(bf16[128,960]{0,1:T(8,128)(2,1)} %get-tuple-element.362), channel_id=1, source_target_pairs={{0,1},{1,0},{2,3},{3,2},{4,5},{5,4},{6,7},{7,6},{8,9},{9,8},{10,11... | collective-permute-start | bytes 737288 | tf_op jit(solution)/shard_map/ppermute | solution.py:477
  459.3 427.0 %reduce-scatter.2.cloned.1.call-start = ((), (), s32[]{:S(2)}) async-start(), calls=%async_computation.6 | async-start | bytes 1105920 | tf_op jit(solution)/shard_map/reduce_scatter | solution.py:760
  504.3 58.0 %collective-permute-start.45 = (bf16[960,3072]{1,0:T(8,128)(2,1)}, bf16[960,3072]{1,0:T(8,128)(2,1)}, u32[]{:S(2)}, u32[]{:S(2)}) collective-permute-start(bf16[960,3072]{1,0:T(8,128)(2,1)} %shard_map.416), channel_id=1, source_target_pairs={{0,8},{8,0},{16,24},{24,16},{1,9},{9,1},{17,25},{25,17},{2,10},{10... | collective-permute-start | bytes 17694728 | tf_op jit(solution)/shard_map/ppermute | solution.py:539
  651.3 36.2 %collective-permute-start.94 = (bf16[960,480]{1,0:T(8,128)(2,1)}, bf16[960,480]{1,0:T(8,128)(2,1)}, u32[]{:S(2)}, u32[]{:S(2)}) collective-permute-start(bf16[960,480]{1,0:T(8,128)(2,1)} %convolution_convert_fusion.3), channel_id=1, source_target_pairs={{0,8},{8,0},{16,24},{24,16},{1,9},{9,1},{17,25},{25,17},{2,10},{10... | collective-permute-start | bytes 2764808 | tf_op jit(solution)/shard_map/ppermute | solution.py:539
  655.7 185.7 %collective-permute-start.78 = (bf16[960,3072]{1,0:T(8,128)(2,1)}, bf16[960,3072]{1,0:T(8,128)(2,1)}, u32[]{:S(2)}, u32[]{:S(2)}) collective-permute-start(bf16[960,3072]{1,0:T(8,128)(2,1)} %add_convert_fusion.1), channel_id=1, source_target_pairs={{0,16},{8,24},{16,0},{24,8},{1,17},{9,25},{17,1},{25,9},{2,18},{10... | collective-permute-start | bytes 17694728 | tf_op jit(solution)/shard_map/ppermute | solution.py:551
  690.2 275.0 %all-reduce.5.cloned.1.call-start = ((), (), s32[]{:S(2)}) async-start(), calls=%async_computation.9 | async-start | bytes 7372800
  790.7 35.0 %collective-permute-start.68 = (bf16[4,960,128]{2,1,0:T(8,128)(2,1)}, bf16[4,960,128]{2,1,0:T(8,128)(2,1)}, u32[]{:S(2)}, u32[]{:S(2)}) collective-permute-start(bf16[4,960,128]{2,1,0:T(8,128)(2,1)} %bitcast.106), channel_id=1, source_target_pairs={{0,1},{1,0},{2,3},{3,2},{4,5},{5,4},{6,7},{7,6},{8,9},{9,8},{10,11... | collective-permute-start | bytes 2949128 | tf_op jit(solution)/shard_map/ppermute | solution.py:477
  791.2 36.7 %collective-permute-start.69 = (bf16[4,960,128]{2,1,0:T(8,128)(2,1)}, bf16[4,960,128]{2,1,0:T(8,128)(2,1)S(1)}, u32[]{:S(2)}, u32[]{:S(2)}) collective-permute-start(bf16[4,960,128]{2,1,0:T(8,128)(2,1)} %bitcast.106), channel_id=1, source_target_pairs={{2,0},{3,1},{4,2},{5,3},{6,4},{7,5},{10,8},{11,9},{12,10},{13,11},... | collective-permute-start | bytes 2949128 | tf_op jit(solution)/shard_map/ppermute | solution.py:469
  792.5 35.5 %collective-permute-start.70 = (bf16[4,960,128]{2,1,0:T(8,128)(2,1)}, bf16[4,960,128]{2,1,0:T(8,128)(2,1)}, u32[]{:S(2)}, u32[]{:S(2)}) collective-permute-start(bf16[4,960,128]{2,1,0:T(8,128)(2,1)} %bitcast.106), channel_id=1, source_target_pairs={{0,2},{1,3},{2,4},{3,5},{4,6},{5,7},{8,10},{9,11},{10,12},{11,13},... | collective-permute-start | bytes 2949128 | tf_op jit(solution)/shard_map/ppermute | solution.py:469
  800.1 30.9 %collective-permute-start.80 = (bf16[960,800]{0,1:T(8,128)(2,1)}, bf16[960,800]{0,1:T(8,128)(2,1)}, u32[]{:S(2)}, u32[]{:S(2)}) collective-permute-start(bf16[960,800]{0,1:T(8,128)(2,1)} %convolution_convert_fusion.1), channel_id=1, source_target_pairs={{0,8},{8,0},{16,24},{24,16},{1,9},{9,1},{17,25},{25,17},{2,10},{10... | collective-permute-start | bytes 4608008 | tf_op jit(solution)/shard_map/ppermute | solution.py:539
  818.2 192.8 %all-gather.10.cloned.1.call-start = ((), (), s32[]{:S(2)}) async-start(), calls=%async_computation.7 | async-start | bytes 1638400 | tf_op jit(solution)/shard_map/all_gather | solution.py:753
  829.5 81.7 %collective-permute-start.71 = (bf16[4,960,128]{2,1,0:T(8,128)(2,1)}, bf16[4,960,128]{2,1,0:T(8,128)(2,1)}, u32[]{:S(2)}, u32[]{:S(2)}) collective-permute-start(bf16[4,960,128]{2,1,0:T(8,128)(2,1)} %get-tuple-element.283), channel_id=1, source_target_pairs={{0,1},{1,0},{2,3},{3,2},{4,5},{5,4},{6,7},{7,6},{8,9},{9,8},{10,11... | collective-permute-start | bytes 2949128 | tf_op jit(solution)/shard_map/ppermute | solution.py:477
  840.9 45.4 %collective-permute-start.85 = (bf16[120,803]{0,1:T(8,128)(2,1)}, bf16[120,803]{0,1:T(8,128)(2,1)S(1)}, u32[]{:S(2)}, u32[]{:S(2)}) collective-permute-start(bf16[120,803]{0,1:T(8,128)(2,1)} %bitcast.382), channel_id=1, source_target_pairs={{0,1},{1,0},{2,3},{3,2},{4,5},{5,4},{6,7},{7,6},{8,9},{9,8},{10,11... | collective-permute-start | bytes 578168 | tf_op jit(solution)/shard_map/ppermute | solution.py:477
  851.2 178.7 %collective-permute-start.79 = (bf16[960,3072]{1,0:T(8,128)(2,1)}, bf16[960,3072]{1,0:T(8,128)(2,1)}, u32[]{:S(2)}, u32[]{:S(2)}) collective-permute-start(bf16[960,3072]{1,0:T(8,128)(2,1)} %add_convert_fusion.mine_ref), channel_id=1, source_target_pairs={{0,8},{8,0},{16,24},{24,16},{1,9},{9,1},{17,25},{25,17},{2,10},{10... | collective-permute-start | bytes 17694728 | tf_op jit(solution)/shard_map/ppermute | solution.py:539
  881.4 39.0 %collective-permute-start.72 = (bf16[4,960,128]{2,1,0:T(8,128)(2,1)S(1)}, bf16[4,960,128]{2,1,0:T(8,128)(2,1)}, u32[]{:S(2)}, u32[]{:S(2)}) collective-permute-start(bf16[4,960,128]{2,1,0:T(8,128)(2,1)S(1)} %copy-done.18), channel_id=1, source_target_pairs={{2,0},{3,1},{4,2},{5,3},{10,8},{11,9},{12,10},{13,11},{18,16},{19,... | collective-permute-start | bytes 2949128 | tf_op jit(solution)/shard_map/ppermute | solution.py:469
  891.0 29.3 %collective-permute-start.73 = (bf16[4,960,128]{2,1,0:T(8,128)(2,1)}, bf16[4,960,128]{2,1,0:T(8,128)(2,1)S(1)}, u32[]{:S(2)}, u32[]{:S(2)}) collective-permute-start(bf16[4,960,128]{2,1,0:T(8,128)(2,1)} %collective-permute-done.70), channel_id=1, source_target_pairs={{2,4},{3,5},{4,6},{5,7},{10,12},{11,13},{12,14},{13,15},{18,20},{1... | collective-permute-start | bytes 2949128 | tf_op jit(solution)/shard_map/ppermute | solution.py:469
  917.9 51.2 %collective-permute-start.82 = (bf16[120,803]{0,1:T(8,128)(2,1)}, bf16[120,803]{0,1:T(8,128)(2,1)}, u32[]{:S(2)}, u32[]{:S(2)}) collective-permute-start(bf16[120,803]{0,1:T(8,128)(2,1)} %bitcast.385), channel_id=1, source_target_pairs={{0,1},{1,0},{2,3},{3,2},{4,5},{5,4},{6,7},{7,6},{8,9},{9,8},{10,11... | collective-permute-start | bytes 578168 | tf_op jit(solution)/shard_map/ppermute | solution.py:477
  923.6 75.6 %collective-permute-start.74 = (bf16[4,960,128]{2,1,0:T(8,128)(2,1)}, bf16[4,960,128]{2,1,0:T(8,128)(2,1)}, u32[]{:S(2)}, u32[]{:S(2)}) collective-permute-start(bf16[4,960,128]{2,1,0:T(8,128)(2,1)} %get-tuple-element.281), channel_id=1, source_target_pairs={{0,1},{1,0},{2,3},{3,2},{4,5},{5,4},{6,7},{7,6},{8,9},{9,8},{10,11... | collective-permute-start | bytes 2949128 | tf_op jit(solution)/shard_map/ppermute | solution.py:477
  924.6 77.9 %collective-permute-start.75 = (bf16[4,960,128]{2,1,0:T(8,128)(2,1)}, bf16[4,960,128]{2,1,0:T(8,128)(2,1)}, u32[]{:S(2)}, u32[]{:S(2)}) collective-permute-start(bf16[4,960,128]{2,1,0:T(8,128)(2,1)} %collective-permute-done.72), channel_id=1, source_target_pairs={{2,0},{3,1},{10,8},{11,9},{18,16},{19,17},{26,24},{27,25}} | collective-permute-start | bytes 2949128 | tf_op jit(solution)/shard_map/ppermute | solution.py:469
  926.7 43.2 %collective-permute-start.90 = (bf16[120,803]{0,1:T(8,128)(2,1)}, bf16[120,803]{0,1:T(8,128)(2,1)}, u32[]{:S(2)}, u32[]{:S(2)}) collective-permute-start(bf16[120,803]{0,1:T(8,128)(2,1)} %add_convert_fusion.14), channel_id=1, source_target_pairs={{4,2},{5,3},{6,4},{7,5},{12,10},{13,11},{14,12},{15,13},{20,18},{2... | collective-permute-start | bytes 578168 | tf_op jit(solution)/shard_map/ppermute | solution.py:469
  969.1 33.4 %collective-permute-start.76 = (bf16[4,960,128]{2,1,0:T(8,128)(2,1)}, bf16[4,960,128]{2,1,0:T(8,128)(2,1)S(1)}, u32[]{:S(2)}, u32[]{:S(2)}) collective-permute-start(bf16[4,960,128]{2,1,0:T(8,128)(2,1)} %copy-done.50), channel_id=1, source_target_pairs={{4,6},{5,7},{12,14},{13,15},{20,22},{21,23},{28,30},{29,31}} | collective-permute-start | bytes 2949128 | tf_op jit(solution)/shard_map/ppermute | solution.py:469
  1005.0 23.9 %collective-permute-start.77 = (bf16[4,960,128]{2,1,0:T(8,128)(2,1)S(1)}, bf16[4,960,128]{2,1,0:T(8,128)(2,1)S(1)}, u32[]{:S(2)}, u32[]{:S(2)}) collective-permute-start(bf16[4,960,128]{2,1,0:T(8,128)(2,1)S(1)} %get-tuple-element.279), channel_id=1, source_target_pairs={{0,1},{1,0},{2,3},{3,2},{4,5},{5,4},{6,7},{7,6},{8,9},{9,8},{10,11... | collective-permute-start | bytes 2949128 | tf_op jit(solution)/shard_map/ppermute | solution.py:477
  1063.4 43.0 %all-to-all-start.3 = ((f32[8,8,128]{2,1,0:T(8,128)}), f32[8,8,128]{2,1,0:T(8,128)S(1)}, u32[]{:S(2)}, u32[]{:S(2)}) async-start(f32[8,8,128]{2,1,0:T(8,128)} %broadcast_in_dim_broadcast_in_dim_broadcast_in_dim.3), calls=%async_computation.4 | async-start | bytes 65536 | tf_op jit(solution)/shard_map/all_to_all | solution.py:536
  (176 other events, 2326.1 us)
Sparse Core Ops, SparseCore 0:
  110.6 57.5 all-gather.7
  192.4 45.1 all-gather.11
  690.4 66.3 reduce-scatter.1
  818.3 146.9 all-reduce.4
  968.1 30.3 all-gather.9

commit v3 on v2

v3 whole, which is shorter than its diff:
```python
import functools

import jax
import jax.numpy as jnp
from jax import lax
from jax.experimental import pallas as pl
from jax.experimental.pallas import tpu as pltpu
from jax.sharding import PartitionSpec as P

D = 960
HEADS = 15
KV_HEADS = 5
HEAD_DIM = 64
FF = 2560
BLOCK = 256
STEP = 5
LINE = 4

EPS_NORM = 1e-05
ROPE_BASE = 100000.0
BETA_ONE = 0.5
BETA_TWO = 0.5
DECAY = 0.1
CLIP_AT = 0.01
ADAM_EPS = 1e-08

F32 = jnp.float32
BF16 = jnp.bfloat16
QUERY = HEADS * HEAD_DIM
KEY = KV_HEADS * HEAD_DIM
VMEM = 56 * 1024 * 1024


def rms_norm(values, gain):
    return values * lax.rsqrt(jnp.mean(values * values, axis=-1, keepdims=True) + EPS_NORM) * gain


def rotate(values, positions):
    half_dim = values.shape[-1] // 2
    freqs = ROPE_BASE ** (-2.0 * jnp.arange(half_dim).astype(F32) / values.shape[-1])
    angles = positions.astype(F32)[:, None] * freqs[None, :]
    cosine = jnp.cos(angles)[:, None, :]
    sine = jnp.sin(angles)[:, None, :]
    first_half = values[..., :half_dim]
    second_half = values[..., half_dim:]
    return jnp.concatenate(
        [first_half * cosine - second_half * sine, second_half * cosine + first_half * sine],
        axis=-1,
    )


def swiglu(gate, up):
    return jax.nn.silu(gate) * up


def rates(seq_len):
    out_fan = max(1, HEADS * HEAD_DIM * 16 // seq_len)
    return (
        0.8 * D ** (-0.5),
        0.5 * D ** (-0.5),
        0.5 * out_fan ** (-0.5),
        0.5 * D ** (-0.5),
        0.5 * FF ** (-0.5),
        0.2,
    )


def adam_update(master, first, second, gradient, rate):
    first_new = BETA_ONE * first + (1.0 - BETA_ONE) * gradient
    second_new = BETA_TWO * second + (1.0 - BETA_TWO) * gradient * gradient
    step_size = (
        first_new
        / (1.0 - BETA_ONE**STEP)
        / (jnp.sqrt(second_new / (1.0 - BETA_TWO**STEP)) + ADAM_EPS)
    )
    master_new = master - rate * (step_size + DECAY * master)
    return (master_new, first_new, second_new, master_new.astype(BF16))


def dot(a, b, dims=((1,), (0,))):
    return lax.dot_general(a, b, (dims, ((), ())), preferred_element_type=F32)


def params():
    return pltpu.CompilerParams(vmem_limit_bytes=VMEM)


def whole(shape):
    return pl.BlockSpec(shape, lambda *_: (0,) * len(shape), pipeline_mode=pl.Buffered(1))


def lookup_kernel(ids_ref, table_ref, low_ref, rows_ref, total):
    tile = table_ref.shape[1]
    step = pl.program_id(0)
    low = table_ref[...].astype(BF16)
    low_ref[...] = low
    columns = lax.broadcasted_iota(jnp.int32, (1, tile), 1) + step * tile
    block = min(512, rows_ref.shape[0])
    for start in range(0, rows_ref.shape[0], block):
        rows = pl.ds(start, block)
        pick = jnp.where(ids_ref[rows, :] == columns, 1.0, 0.0).astype(BF16)
        found = dot(pick, low, ((1,), (1,)))

        @pl.when(step == 0)
        def _():
            total[rows, :] = found

        @pl.when(step > 0)
        def _():
            total[rows, :] += found

    @pl.when(step == pl.num_programs(0) - 1)
    def _():
        rows_ref[...] = total[...].astype(BF16)


def lookup(table_t, local_ids, tile=512):
    width, vocab = table_t.shape
    count = local_ids.shape[0]
    return pl.pallas_call(
        lookup_kernel,
        grid=(vocab // tile,),
        in_specs=[
            whole((count, 1)),
            pl.BlockSpec((width, tile), lambda i: (0, i)),
        ],
        out_specs=[
            pl.BlockSpec((width, tile), lambda i: (0, i)),
            whole((count, width)),
        ],
        out_shape=[
            jax.ShapeDtypeStruct((width, vocab), BF16),
            jax.ShapeDtypeStruct((count, width), BF16),
        ],
        scratch_shapes=[pltpu.VMEM((count, width), F32)],
        compiler_params=params(),
        cost_estimate=pl.CostEstimate(
            flops=2 * count * width * vocab, bytes_accessed=6 * width * vocab, transcendentals=0
        ),
    )(local_ids[:, None], table_t)


def logits_kernel(states_ref, targets_ref, table_ref, raised_ref, stats_ref, logits, *, tile):
    vocab = table_ref.shape[1]
    rows = states_ref.shape[0]
    states = states_ref[...]
    high = jnp.full((rows, 1), -jnp.inf, F32)
    for start in range(0, vocab, tile):
        part = dot(states, table_ref[:, start : start + tile])
        logits[:, start : start + tile] = part
        high = jnp.maximum(high, jnp.max(part, axis=-1, keepdims=True))
    total = jnp.zeros((rows, 128), F32)
    picked = jnp.zeros((rows, 128), F32)
    targets = targets_ref[...]
    lanes = lax.broadcasted_iota(jnp.int32, (1, 128), 1)
    for start in range(0, vocab, 128):
        part = logits[:, start : start + 128]
        raised = jnp.exp(part - high)
        raised_ref[:, start : start + 128] = raised.astype(BF16)
        total += raised
        picked += jnp.where(targets == lanes + start, part, 0.0)
    total = jnp.sum(total, axis=-1, keepdims=True)
    picked = jnp.sum(picked, axis=-1, keepdims=True)
    stats_ref[...] = jnp.where(lanes == 0, high, jnp.where(lanes == 1, total, picked))


def head_logits(states, targets, table_low, rows=256, tile=512):
    count, width = states.shape
    vocab = table_low.shape[1]
    return pl.pallas_call(
        functools.partial(logits_kernel, tile=tile),
        grid=(count // rows,),
        in_specs=[
            pl.BlockSpec((rows, width), lambda i: (i, 0)),
            pl.BlockSpec((rows, 1), lambda i: (i, 0)),
            whole((width, vocab)),
        ],
        out_specs=[
            pl.BlockSpec((rows, vocab), lambda i: (i, 0)),
            pl.BlockSpec((rows, 128), lambda i: (i, 0)),
        ],
        out_shape=[
            jax.ShapeDtypeStruct((count, vocab), BF16),
            jax.ShapeDtypeStruct((count, 128), F32),
        ],
        scratch_shapes=[pltpu.VMEM((rows, vocab), F32)],
        compiler_params=params(),
        cost_estimate=pl.CostEstimate(
            flops=2 * count * width * vocab,
            bytes_accessed=2 * vocab * (width + count),
            transcendentals=count * vocab,
        ),
    )(states, targets[:, None], table_low)


def states_kernel(raised_ref, scales_ref, targets_ref, table_ref, grads_ref, out_ref, *, tile):
    vocab = table_ref.shape[1]
    weight = scales_ref[:, 1:2]
    factor = scales_ref[:, 0:1]
    targets = targets_ref[...]
    total = None
    for start in range(0, vocab, tile):
        lanes = lax.broadcasted_iota(jnp.int32, (1, tile), 1) + start
        chances = raised_ref[:, start : start + tile].astype(F32) * factor
        part = (jnp.where(targets == lanes, chances - weight, chances)).astype(BF16)
        grads_ref[:, start : start + tile] = part
        found = dot(part, table_ref[:, start : start + tile], ((1,), (1,)))
        total = found if total is None else total + found
    out_ref[...] = total.astype(BF16)


def head_states(raised, factors, weights, targets, table_low, rows=256, tile=512):
    count, vocab = raised.shape
    width = table_low.shape[0]
    scales = jnp.stack([factors * weights, weights], axis=1)
    return pl.pallas_call(
        functools.partial(states_kernel, tile=tile),
        grid=(count // rows,),
        in_specs=[
            pl.BlockSpec((rows, vocab), lambda i: (i, 0)),
            pl.BlockSpec((rows, 2), lambda i: (i, 0)),
            pl.BlockSpec((rows, 1), lambda i: (i, 0)),
            whole((width, vocab)),
        ],
        out_specs=[
            pl.BlockSpec((rows, vocab), lambda i: (i, 0)),
            pl.BlockSpec((rows, width), lambda i: (i, 0)),
        ],
        out_shape=[
            jax.ShapeDtypeStruct((count, vocab), BF16),
            jax.ShapeDtypeStruct((count, width), BF16),
        ],
        compiler_params=params(),
        cost_estimate=pl.CostEstimate(
            flops=2 * count * width * vocab,
            bytes_accessed=2 * vocab * (width + 2 * count),
            transcendentals=0,
        ),
    )(raised, scales, targets[:, None], table_low)


def table_kernel(
    part_ref,
    near_t,
    far_t,
    near_pair_t,
    far_pair_t,
    near_grads,
    far_grads,
    near_pair,
    far_pair,
    scales,
    targets,
    table_ref,
    out_ref,
):
    tile = out_ref.shape[1]
    step = part_ref[0] * pl.num_programs(0) + pl.program_id(0)
    columns = lax.broadcasted_iota(jnp.int32, (1, tile), 1) + step * tile
    total = dot(near_t[...], near_grads[...]) + dot(far_t[...], far_grads[...])
    offset = 0
    for pair, pair_t in ((near_pair, near_pair_t), (far_pair, far_pair_t)):
        block = min(512, pair.shape[0])
        for start in range(0, pair.shape[0], block):
            rows = slice(offset + start, offset + start + block)
            weight = scales[rows, 1:2]
            logits = dot(pair[start : start + block, :], table_ref[...])
            chances = jnp.exp(logits - scales[rows, 0:1]) * weight
            grads = jnp.where(targets[rows, :] == columns, chances - weight, chances)
            total += dot(pair_t[:, start : start + block], grads.astype(BF16))
        offset += pair.shape[0]
    out_ref[...] = total.astype(BF16)


def head_table(
    near_t,
    far_t,
    near_grads,
    far_grads,
    near_pair,
    far_pair,
    scales,
    targets,
    table_low,
    part,
    tile,
):
    width, near = near_t.shape
    far = far_t.shape[1]
    both = near + far
    vocab = near_grads.shape[1] // 4
    steps = vocab // tile

    def column(i, part):
        return (0, part[0] * steps + i)

    return pl.pallas_call(
        table_kernel,
        grid_spec=pltpu.PrefetchScalarGridSpec(
            num_scalar_prefetch=1,
            grid=(steps,),
            in_specs=[
                whole((width, near)),
                whole((width, far)),
                whole((width, near)),
                whole((width, far)),
                pl.BlockSpec((near, tile), column),
                pl.BlockSpec((far, tile), column),
                whole((near, width)),
                whole((far, width)),
                whole((both, 2)),
                whole((both, 1)),
                pl.BlockSpec((width, tile), column),
            ],
            out_specs=pl.BlockSpec((width, tile), lambda i, part: (0, i)),
        ),
        out_shape=jax.ShapeDtypeStruct((width, vocab), BF16),
        compiler_params=params(),
        cost_estimate=pl.CostEstimate(
            flops=6 * both * width * vocab,
            bytes_accessed=2 * (2 * vocab + 3 * both) * width + 2 * vocab * both,
            transcendentals=both * vocab,
        ),
    )(
        jnp.reshape(part, (1,)).astype(jnp.int32),
        near_t,
        far_t,
        near_pair.T,
        far_pair.T,
        near_grads,
        far_grads,
        near_pair,
        far_pair,
        scales,
        targets[:, None],
        table_low,
    )


def place_kernel(
    starts_ref,
    ranks_ref,
    ids_ref,
    rows_ref,
    kept_ref,
    received_ref,
    out_ref,
    square_ref,
    sorted_rows,
    total,
    *,
    chunk,
    block,
):
    step = pl.program_id(0)
    tile = out_ref.shape[1]
    sources, lanes, _ = rows_ref.shape

    @pl.when(step == 0)
    def _():
        def sort(k, carry):
            columns = pl.ds(pl.multiple_of(k * block, block), block)
            wanted = lax.broadcasted_iota(jnp.int32, (1, block), 1) + k * block
            found = None
            for source in range(sources):
                pick = ranks_ref[source * lanes : (source + 1) * lanes, :] == wanted
                pick = jnp.where(pick, 1.0, 0.0).astype(BF16)
                part = dot(rows_ref[source], pick, ((0,), (0,)))
                found = part if found is None else found + part
            sorted_rows[:, columns] = found.astype(BF16)
            return carry

        lax.fori_loop(0, (starts_ref[pl.num_programs(0)] + block - 1) // block, sort, 0)

    first = starts_ref[step]
    last = starts_ref[step + 1]
    total[...] = kept_ref[...].astype(F32) + received_ref[...].astype(F32)
    columns = lax.broadcasted_iota(jnp.int32, (1, tile), 1) + step * tile

    def add(k, carry):
        rows = pl.ds(pl.multiple_of(k * chunk, chunk), chunk)
        place = lax.broadcasted_iota(jnp.int32, (chunk, 1), 0) + k * chunk
        ids = ids_ref[rows, :]
        inside = jnp.logical_and(place >= first, place < last)
        pick = jnp.where(jnp.logical_and(ids == columns, inside), 1.0, 0.0).astype(BF16)
        total[...] += dot(sorted_rows[:, rows], pick)
        return carry

    lax.fori_loop(first // chunk, (last + chunk - 1) // chunk, add, 0)
    low = total[...].astype(BF16)
    out_ref[...] = low
    value = low.astype(F32)
    squares = jnp.sum(value * value, axis=0, keepdims=True)
    part = jnp.zeros((1, 128), F32)
    for start in range(0, tile, 128):
        part += squares[:, start : start + 128]

    @pl.when(step == 0)
    def _():
        square_ref[...] = part

    @pl.when(step > 0)
    def _():
        square_ref[...] += part


def place_rows(kept, received, rows, ranks, ids, starts, tile, chunk=128, block=256):
    width, columns = kept.shape
    sources, lanes, _ = rows.shape
    total = sources * lanes
    block = min(block, total)
    spec = pl.BlockSpec((width, tile), lambda i, starts: (0, i))
    return pl.pallas_call(
        functools.partial(place_kernel, chunk=chunk, block=block),
        grid_spec=pltpu.PrefetchScalarGridSpec(
            num_scalar_prefetch=1,
            grid=(columns // tile,),
            in_specs=[whole((total, 1)), whole((total, 1)), whole((sources, lanes, width))]
            + [spec] * 2,
            out_specs=[spec, whole((1, 128))],
            scratch_shapes=[pltpu.VMEM((width, total), BF16), pltpu.VMEM((width, tile), F32)],
        ),
        out_shape=[
            jax.ShapeDtypeStruct((width, columns), BF16),
            jax.ShapeDtypeStruct((1, 128), F32),
        ],
        compiler_params=params(),
        cost_estimate=pl.CostEstimate(
            flops=2 * 4 * chunk * tile * width,
            bytes_accessed=6 * width * columns + 2 * total * width,
            transcendentals=0,
        ),
    )(starts, ranks[:, None], ids[:, None], rows, kept, received)


def adam_kernel(quarters_ref, scale_ref, w_ref, m_ref, v_ref, one_ref, two_ref, *refs, rate):
    step = pl.program_id(0)
    half = pl.num_programs(0) // 2
    outs = refs[-4:]

    def update(gradient):
        new = adam_update(w_ref[...], m_ref[...], v_ref[...], gradient * scale_ref[0], rate)
        for ref, value in zip(outs, new):
            ref[...] = value

    @pl.when(step < half)
    def _():
        update(one_ref[...].astype(F32))

    @pl.when(step >= half)
    def _():
        update(two_ref[...].astype(F32))


def adam(master, first, second, one, two, quarters, scale, rate, tile, before=None):
    rows, columns = master.shape
    steps = one.shape[1] // tile

    def column(i, quarters):
        return (0, quarters[i // steps] * steps + i % steps)

    spec = pl.BlockSpec((rows, tile), column)
    shape = jax.ShapeDtypeStruct((rows, columns), F32)
    before = list(before or [])
    return pl.pallas_call(
        functools.partial(adam_kernel, rate=rate),
        grid_spec=pltpu.PrefetchScalarGridSpec(
            num_scalar_prefetch=1,
            grid=(2 * steps,),
            in_specs=[pl.BlockSpec(memory_space=pltpu.SMEM)]
            + [spec] * 3
            + [
                pl.BlockSpec((rows, tile), lambda i, q: (0, jnp.minimum(i, steps - 1))),
                pl.BlockSpec((rows, tile), lambda i, q: (0, jnp.maximum(i - steps, 0))),
            ]
            + [pl.BlockSpec(memory_space=pl.ANY)] * len(before),
            out_specs=[spec] * 4,
        ),
        out_shape=[shape] * 3 + [jax.ShapeDtypeStruct((rows, columns), BF16)],
        input_output_aliases={7 + k: k for k in range(len(before))},
        compiler_params=params(),
        cost_estimate=pl.CostEstimate(flops=0, bytes_accessed=0, transcendentals=0),
    )(
        quarters.astype(jnp.int32),
        jnp.reshape(scale, (1,)),
        master,
        first,
        second,
        one,
        two,
        *before,
    )


def adam_many_kernel(scale_ref, *refs, rates):
    count = len(rates)
    inputs, outputs = refs[: 4 * count], refs[4 * count :]
    scale = scale_ref[0]
    for member, rate in enumerate(rates):
        olds = inputs[4 * member : 4 * member + 4]
        news = outputs[4 * member : 4 * member + 4]
        rows = olds[0].shape[0]
        block = 8 if rows % 8 == 0 else rows

        def update(k, carry, olds=olds, news=news, block=block, rate=rate):
            place = pl.ds(pl.multiple_of(k * block, block), block)
            w, m, v, g = (ref[place, :] for ref in olds)
            for ref, value in zip(news, adam_update(w, m, v, g * scale, rate)):
                ref[place, :] = value
            return carry

        lax.fori_loop(0, rows // block, update, 0)


def adam_many(olds, scale, rates):
    shapes = []
    for master, *_ in olds:
        shapes += [jax.ShapeDtypeStruct(master.shape, F32)] * 3
        shapes += [jax.ShapeDtypeStruct(master.shape, BF16)]
    inside = pl.BlockSpec(memory_space=pltpu.VMEM)
    return pl.pallas_call(
        functools.partial(adam_many_kernel, rates=rates),
        in_specs=[pl.BlockSpec(memory_space=pltpu.SMEM)] + [inside] * (4 * len(olds)),
        out_specs=[inside] * (4 * len(olds)),
        out_shape=shapes,
        compiler_params=params(),
        cost_estimate=pl.CostEstimate(flops=0, bytes_accessed=0, transcendentals=0),
    )(jnp.reshape(scale, (1,)), *[part for member in olds for part in member])


def place_slowly(kept, received, rows, ids):
    columns = jnp.arange(kept.shape[1], dtype=jnp.int32)

    def add(total, operands):
        part, part_ids = operands
        pick = (part_ids[:, None] == columns[None, :]).astype(BF16)
        return total + dot(part, pick, ((0,), (0,))), None

    total, _ = lax.scan(add, kept.astype(F32) + received.astype(F32), (rows, ids))
    total = total.astype(BF16)
    squares = jnp.sum(jnp.square(total.astype(F32)))
    return total, jnp.full((1, 128), squares / 128)


class Links:
    def __init__(self, n_shard, n_rep):
        self.n = n_shard
        self.wide = n_shard // LINE
        self.n_rep = n_rep
        me = lax.axis_index("shard")
        self.z = me // self.wide
        self.w = me % self.wide
        self.lines = [[z * self.wide + w for z in range(LINE)] for w in range(self.wide)]

    def across(self, value, step):
        pairs = [
            (z * self.wide + w, z * self.wide + (w + step) % self.wide)
            for z in range(LINE)
            for w in range(self.wide)
        ]
        return lax.ppermute(value, "shard", pairs)

    def all_across(self, value):
        return jnp.stack([self.across(value, step) for step in range(1, self.wide)])

    def sum_across(self, near, far):
        rows = near.shape[0]
        total = near.astype(F32)
        for step in range(1, self.wide):
            part = far[(step - 1) * rows : step * rows] if self.wide > 2 else far
            total = total + self.across(part, -step).astype(F32)
        return total

    def line_gather(self, value):
        return lax.all_gather(value, "shard", axis_index_groups=self.lines, tiled=True)

    def line_sum(self, value):
        parts = lax.all_to_all(
            value.astype(BF16), "shard", 0, 0, axis_index_groups=self.lines, tiled=True
        )
        return jnp.sum(parts.astype(F32), axis=0)

    def scatter(self, value):
        value = value.reshape((self.n, -1) + value.shape[1:])
        parts = lax.all_to_all(value, "shard", 0, 0, tiled=True)
        return jnp.sum(parts.astype(F32), axis=0)

    def spread(self, value):
        many = jnp.broadcast_to(value[None], (self.n,) + value.shape)
        return lax.all_to_all(many, "shard", 0, 0, tiled=True)

    def core(self, value):
        return lax.ppermute(value, "rep", [(r, r ^ 1) for r in range(self.n_rep)])

    def rep_gather(self, value):
        value = value[None]
        value = jnp.concatenate([value, self.chip(value)])
        return jnp.concatenate([value, self.core(value)])

    def rep_gather_now(self, value):
        rep = lax.axis_index("rep")
        value = lax.all_gather(value, "rep")
        return jnp.concatenate(
            [lax.dynamic_index_in_dim(value, rep ^ other, 0) for other in (0, 2, 1, 3)]
        )

    def rep_sum(self, value):
        value = value.astype(BF16)
        mine = value[:2].astype(F32) + self.core(value[2:]).astype(F32)
        return mine[0] + self.chip(mine[1].astype(BF16)).astype(F32)

    def chip(self, value):
        return lax.ppermute(value, "rep", [(r, r ^ 2) for r in range(self.n_rep)])


def build(mesh):
    n_shard = mesh.shape["shard"]
    n_rep = mesh.shape["rep"]

    def local(
        token_ids,
        target_ids,
        loss_mask,
        table_master,
        attn_in_master,
        attn_out_master,
        mlp_in_master,
        mlp_out_master,
        gain_master,
        table_first,
        attn_in_first,
        attn_out_first,
        mlp_in_first,
        mlp_out_first,
        gain_first,
        table_second,
        attn_in_second,
        attn_out_second,
        mlp_in_second,
        mlp_out_second,
        gain_second,
    ):
        links = Links(n_shard, n_rep)
        my_rep = lax.axis_index("rep")
        my_shard = lax.axis_index("shard")
        second_core = (my_rep % 2) == 1
        second_chip = (my_rep // 2) == 1
        tok_rows = token_ids.shape[0]
        seq_len = n_shard * tok_rows
        vocab_rows = table_master.shape[0]
        vocab_start = my_shard * vocab_rows
        wide = n_shard // LINE
        line_rows = LINE * tok_rows

        def in_order(mine, other, axis=-1):
            return jnp.where(
                second_core,
                jnp.concatenate([other, mine], axis),
                jnp.concatenate([mine, other], axis),
            )

        def my_half(value, axis=-1):
            first, second = jnp.split(value, 2, axis)
            return jnp.where(second_core, second, first), jnp.where(second_core, first, second)

        packed = jnp.stack([token_ids, target_ids, loss_mask])
        everyone = links.spread(lax.all_gather(packed, "rep")).transpose(1, 0, 2, 3)
        everyone = everyone.reshape(LINE, n_rep, wide, 3, tok_rows).transpose(1, 0, 2, 3, 4)
        valid_count = jnp.sum(everyone[:, :, :, 2].astype(F32))
        turn = [(links.w - step) % wide for step in range(wide)]

        def group_of(rep):
            group = lax.dynamic_index_in_dim(everyone, rep, 0, False)
            group = jnp.stack(
                [lax.dynamic_index_in_dim(group, turn[step], 1, False) for step in range(wide)]
            )
            targets = group[:, :, 1].reshape(-1) - vocab_start
            return targets, group[:, :, 2].reshape(-1).astype(F32)

        group_targets, group_mask = group_of(my_rep)
        pair_targets, pair_mask = group_of(my_rep ^ 2)
        group_weights = group_mask / valid_count
        pair_weights = pair_mask / valid_count
        place_block = my_rep * wide + links.w
        positions = place_block * tok_rows + jnp.arange(tok_rows, dtype=jnp.int32)

        def halves(master):
            return my_half(master[0].astype(BF16))[0]

        unit_rows = FF // n_shard
        unit_part = unit_rows // n_rep
        units = n_shard * unit_part
        mlp_in_part = mlp_in_master[0].astype(BF16)
        mlp_in_part = mlp_in_part.reshape(-1, 2, n_shard, n_rep, unit_part)
        mlp_in_part = lax.dynamic_index_in_dim(mlp_in_part, my_rep, 3, False).reshape(-1, 2 * units)
        mlp_out_part = mlp_out_master[0].astype(BF16).reshape(n_rep, unit_part, D)
        mlp_out_part = lax.dynamic_index_in_dim(mlp_out_part, my_rep, 0, False)
        in_rows = D // n_shard
        in_cols = attn_in_master.shape[2] // 2
        attn_part = jnp.concatenate([halves(attn_in_master), halves(attn_out_master)], 1)
        mlp_part = jnp.concatenate([mlp_in_part, mlp_out_part.reshape(in_rows, -1)], 1)
        attn_mine = lax.all_gather(attn_part, "shard", tiled=True)

        room = min(64, tok_rows)
        vocab_tile = min(512, vocab_rows // 4)
        all_ids = everyone[:, :, :, 0].reshape(n_rep, n_shard, tok_rows)
        earlier = jnp.tril(jnp.ones((tok_rows, tok_rows), BF16), -1)

        def places(inside):
            found = jnp.einsum(
                "...j,ij->...i", inside.astype(BF16), earlier, preferred_element_type=F32
            )
            return jnp.where(inside, found.astype(jnp.int32), -1)

        owners = jnp.arange(n_shard, dtype=jnp.int32)
        owned = (all_ids // vocab_rows)[:, :, None, :] == owners[:, None]
        enough = jnp.max(jnp.sum(owned.astype(jnp.int32), -1)) <= room
        local_ids = all_ids - vocab_start
        inside = (local_ids >= 0) & (local_ids < vocab_rows)
        room_iota = jnp.arange(room, dtype=jnp.int32)
        slots = places(inside)
        slot_ids = jnp.max(
            jnp.where(slots[:, :, None, :] == room_iota[:, None], local_ids[:, :, None, :], -1), -1
        )
        slot_ids = jnp.where(slot_ids < 0, vocab_rows, slot_ids)
        own_ids = lax.dynamic_index_in_dim(
            lax.dynamic_index_in_dim(all_ids, my_rep, 0, False), my_shard, 0, False
        )
        own_slots = places((own_ids // vocab_rows)[None, :] == owners[:, None])
        packing = (own_slots[:, None, :] == room_iota[:, None]).astype(BF16).reshape(-1, tok_rows)

        my_slots = lax.dynamic_index_in_dim(slot_ids, my_rep, 0, False).reshape(-1)
        table_low, looked = lookup(table_master.T, my_slots, min(512, vocab_rows))

        looked, mlp_part = lax.optimization_barrier((looked, mlp_part))
        mlp_all = lax.all_gather(mlp_part, "shard", tiled=True)
        packed = lax.all_to_all(looked.reshape(n_shard, room, D), "shard", 0, 0, tiled=True)
        packed = dot(packing, packed.reshape(-1, D), ((0,), (0,)))

        def read_whole(packed, table_low):
            ids = lax.dynamic_index_in_dim(local_ids, my_rep, 0, False).reshape(-1)
            columns = jnp.arange(vocab_rows, dtype=jnp.int32)
            pick = (ids[:, None] == columns[None, :]).astype(BF16)
            rows = dot(pick, table_low, ((1,), (1,))).astype(BF16)
            rows = lax.all_to_all(rows.reshape(n_shard, tok_rows, D), "shard", 0, 0, tiled=True)
            return jnp.sum(rows.astype(F32), axis=0)

        values = lax.cond(enough, lambda packed, _: packed, read_whole, packed, table_low)
        values, gain_low = lax.optimization_barrier((values, gain_master.astype(BF16)))
        gains = links.spread(gain_low).transpose(1, 0, 2).reshape(3, D).astype(F32)

        rank_ids = jnp.concatenate(
            [lax.dynamic_index_in_dim(slot_ids, my_rep ^ r, 0, False) for r in (0, 2, 1, 3)]
        ).reshape(-1)
        quarter_rows = vocab_rows // n_rep
        quarter_start = my_rep * quarter_rows
        rank_ids = rank_ids - quarter_start
        rank_ids = jnp.where((rank_ids >= 0) & (rank_ids < quarter_rows), rank_ids, quarter_rows)
        slot_iota = jnp.arange(rank_ids.shape[0], dtype=jnp.int32)
        before = (rank_ids[None, :] < rank_ids[:, None]) | (
            (rank_ids[None, :] == rank_ids[:, None]) & (slot_iota[None, :] < slot_iota[:, None])
        )
        ranks = jnp.sum(before.astype(jnp.int32), axis=1)
        sorted_ids = jnp.sort(rank_ids)
        edges = jnp.arange(0, quarter_rows + 1, vocab_tile, dtype=jnp.int32)
        starts = jnp.sum((rank_ids[None, :] < edges[:, None]).astype(jnp.int32), axis=1)
        attn_mine, ranks, sorted_ids, starts, gains = lax.optimization_barrier(
            (attn_mine, ranks, sorted_ids, starts, gains)
        )
        attn_other = links.core(attn_mine)
        attn_in = (attn_mine[:, :in_cols], attn_other[:, :in_cols])
        attn_out = (attn_mine[:, in_cols:], attn_other[:, in_cols:])
        mlp_in = mlp_all[:, : 2 * units]
        mlp_out = mlp_all[:, 2 * units :].reshape(n_shard * unit_part, D)

        def times(value, pair):
            return dot(value, pair[0]), dot(value, pair[1])

        def times_back(mine, other, pair):
            return dot(mine, pair[0], ((1,), (1,))) + dot(other, pair[1], ((1,), (1,)))

        normed_one, norm_one_back = jax.vjp(rms_norm, values, gains[0])
        normed_one = normed_one.astype(BF16)
        mixed = in_order(*times(normed_one, attn_in))
        heads_raw = mixed[:, : QUERY + KEY].reshape(tok_rows, HEADS + KV_HEADS, HEAD_DIM)
        rotated, rope_back = jax.vjp(lambda part: rotate(part, positions), heads_raw)
        rotated = rotated.astype(BF16)
        group_size = HEADS // KV_HEADS
        queries = rotated[:, :HEADS].reshape(tok_rows, KV_HEADS, group_size, HEAD_DIM)
        queries = queries.transpose(1, 2, 0, 3).reshape(KV_HEADS, group_size * tok_rows, HEAD_DIM)
        queries = jnp.pad(queries, ((0, 0), (0, 0), (0, HEAD_DIM)))
        vals = mixed[:, QUERY + KEY :].astype(BF16).reshape(tok_rows, KV_HEADS, HEAD_DIM)
        kv = jnp.concatenate([rotated[:, HEADS:], vals], 2).transpose(1, 0, 2)
        kv = links.rep_gather(jnp.concatenate([kv[None], links.all_across(kv)]))
        kv = kv.transpose(2, 0, 1, 3, 4).reshape(KV_HEADS, seq_len, 2 * HEAD_DIM)
        scale = HEAD_DIM ** (-0.5)
        key_places = (
            (jnp.stack([my_rep ^ other for other in (0, 2, 1, 3)]) * wide)[:, None, None]
            + ((links.w - jnp.arange(wide, dtype=jnp.int32)) % wide)[None, :, None]
        ) * tok_rows + jnp.arange(tok_rows, dtype=jnp.int32)
        key_blocks = key_places.reshape(-1) // BLOCK
        query_blocks = jnp.tile(positions // BLOCK, group_size)
        allowed = (key_blocks[None, :] <= query_blocks[:, None])[None]

        def batched(spec, a, b):
            return jnp.einsum(spec, a, b, preferred_element_type=F32)

        scores = jnp.where(allowed, batched("htd,hsd->hts", queries, kv) * scale, -1e30)
        highest = jnp.max(scores, axis=-1, keepdims=True)
        weights = jnp.exp(scores - highest)
        totals = jnp.sum(weights, axis=-1, keepdims=True)
        chances = weights / totals
        chances_low = chances.astype(BF16)
        outputs = batched("hts,hsd->htd", chances_low, kv)[:, :, HEAD_DIM:]

        def to_rows(heads):
            return (
                heads.reshape(KV_HEADS, group_size, tok_rows, HEAD_DIM)
                .transpose(2, 0, 1, 3)
                .reshape(tok_rows, QUERY)
            )

        attended = to_rows(outputs).astype(BF16)
        middle = values + in_order(*times(attended, attn_out))
        normed_two, norm_two_back = jax.vjp(rms_norm, middle, gains[1])
        normed_two = normed_two.astype(BF16)
        normed_all = links.rep_gather_now(normed_two).reshape(-1, D)
        gate_up = dot(normed_all, mlp_in)
        hidden, glu_back = jax.vjp(swiglu, gate_up[:, :units], gate_up[:, units:])
        hidden = hidden.astype(BF16)
        result = middle + links.rep_sum(dot(hidden, mlp_out).reshape(n_rep, tok_rows, D))
        final, final_back = jax.vjp(rms_norm, result, gains[2])

        near = links.line_gather(final.astype(BF16))
        far = links.all_across(near).reshape(-1, D)
        near_targets, far_targets = group_targets[:line_rows], group_targets[line_rows:]
        pair_near = links.chip(near)
        pair_far = links.chip(far)
        near_raised, near_stats = head_logits(near, near_targets, table_low)
        far, near_stats = lax.optimization_barrier((far, near_stats))
        far_raised, far_stats = head_logits(far, far_targets, table_low)
        stats = jnp.concatenate([near_stats, far_stats])[:, :3].T
        high = stats[0]
        stats = stats.reshape(3, wide, LINE, tok_rows)
        ordered = jnp.stack(
            [lax.dynamic_index_in_dim(stats, turn[step], 1, False) for step in range(wide)], 1
        )
        stats = links.spread(ordered)
        top = jnp.max(stats[:, 0], axis=0)
        log_totals = top + jnp.log(jnp.sum(stats[:, 1] * jnp.exp(stats[:, 0] - top), axis=0))
        picked = jnp.sum(stats[:, 2], axis=0)
        losses = log_totals - picked

        def turned(part):
            return jnp.stack(
                [lax.dynamic_index_in_dim(part, turn[step], 0, False) for step in range(wide)]
            ).reshape(-1)

        log_totals = turned(log_totals)
        group_loss = jnp.sum(turned(losses) * group_mask)
        pair_logs = links.chip(log_totals)
        factors = jnp.exp(high - log_totals)
        far_grads, far_part = head_states(
            far_raised, factors[line_rows:], group_weights[line_rows:], far_targets, table_low
        )
        far_sent = far_part
        near_raised, far_part = lax.optimization_barrier((near_raised, far_part))
        near_grads, near_part = head_states(
            near_raised, factors[:line_rows], group_weights[:line_rows], near_targets, table_low
        )

        table_operands = (
            near.T,
            far.T,
            near_grads,
            far_grads,
            pair_near,
            pair_far,
            jnp.stack([pair_logs, pair_weights], axis=1),
            pair_targets,
            table_low,
        )
        sent = head_table(*table_operands, my_rep ^ 1, vocab_tile)
        received = links.core(sent)
        sent, near_part = lax.optimization_barrier((sent, near_part))
        grad_states = links.sum_across(near_part, far_sent)
        grad_final = links.line_sum(grad_states.reshape(LINE, tok_rows, D))
        kept = head_table(*table_operands, my_rep, vocab_tile)
        kept, grad_final = lax.optimization_barrier((kept, grad_final))

        grad_output, grad_gain_three = final_back(grad_final)

        def weight_grad(value, mine, other):
            sent = dot(value, other, ((0,), (0,))).astype(BF16)
            half = dot(value, mine, ((0,), (0,))) + links.core(sent).astype(F32)
            first, second = jnp.split(half, 2, 1)
            sent = links.chip(jnp.where(second_chip, first, second).astype(BF16))
            return (jnp.where(second_chip, second, first) + sent.astype(F32)).astype(BF16)

        pad_rows = -in_rows % 16

        def pad_blocks(value):
            value = value.reshape(-1, n_shard, in_rows)
            value = jnp.pad(value, ((0, 0), (0, 0), (0, pad_rows)))
            return value.reshape(-1, n_shard * (in_rows + pad_rows))

        branch = links.rep_gather_now(grad_output.astype(BF16)).reshape(-1, D)
        grad_mlp_out = dot(hidden, branch, ((0,), (0,))).astype(BF16)
        grad_hidden = dot(branch, mlp_out, ((1,), (1,)))
        grad_glu = jnp.concatenate(glu_back(grad_hidden), 1).astype(BF16)
        grad_mlp_in = dot(pad_blocks(normed_all), grad_glu, ((0,), (0,))).astype(BF16)
        grad_normed_two = dot(grad_glu, mlp_in, ((1,), (1,))).reshape(n_rep, tok_rows, D)
        grad_normed_two = links.rep_sum(grad_normed_two)
        middle_part, grad_gain_two = norm_two_back(grad_normed_two)
        grad_middle = grad_output + middle_part

        grad_mlp = [
            links.scatter(grad_mlp_in)[:in_rows].astype(BF16),
            grad_mlp_out,
        ]

        out_mine, out_other = my_half(grad_middle.astype(BF16))
        grad_attn_out = weight_grad(pad_blocks(attended), out_mine, out_other)
        grad_attended = times_back(out_mine, out_other, attn_out).astype(BF16)
        grad_heads = (
            grad_attended.reshape(tok_rows, KV_HEADS, group_size, HEAD_DIM)
            .transpose(1, 2, 0, 3)
            .reshape(KV_HEADS, group_size * tok_rows, HEAD_DIM)
        )
        deltas = jnp.sum(grad_heads.astype(F32) * outputs, axis=-1, keepdims=True)
        grad_heads = jnp.pad(grad_heads, ((0, 0), (0, 0), (HEAD_DIM, 0)))
        grad_chances = batched("htd,hsd->hts", grad_heads, kv)
        grad_scores = (chances * (grad_chances - deltas)).astype(BF16)
        grad_kv = batched("hts,htd->hsd", grad_scores, queries) * scale
        grad_kv = grad_kv + batched("hts,htd->hsd", chances_low, grad_heads)
        grad_kv = grad_kv.astype(BF16).reshape(KV_HEADS, n_rep, wide, tok_rows, 2 * HEAD_DIM)
        grad_kv = links.rep_sum(grad_kv.transpose(1, 2, 0, 3, 4))
        far_kv = grad_kv[1:].astype(BF16).reshape(-1, tok_rows, 2 * HEAD_DIM)
        grad_kv = links.sum_across(grad_kv[0], far_kv).transpose(1, 0, 2)
        grad_queries = batched("hts,hsd->htd", grad_scores, kv)[:, :, :HEAD_DIM] * scale
        grad_rotated = jnp.concatenate(
            [
                to_rows(grad_queries).reshape(tok_rows, HEADS, HEAD_DIM),
                grad_kv[:, :, :HEAD_DIM],
            ],
            1,
        )
        grad_raw = rope_back(grad_rotated)[0].reshape(tok_rows, QUERY + KEY)
        grad_mixed = jnp.concatenate([grad_raw, grad_kv[:, :, HEAD_DIM:].reshape(tok_rows, KEY)], 1).astype(BF16)
        mixed_mine, mixed_other = my_half(grad_mixed)
        values_part, grad_gain_one = norm_one_back(times_back(mixed_mine, mixed_other, attn_in))
        grad_values = (grad_middle + values_part).astype(BF16)
        grad_gains = jnp.stack([grad_gain_one, grad_gain_two, grad_gain_three], 1)
        grad_gains = grad_gains + links.core(grad_gains)
        grad_gains = pad_blocks((grad_gains + links.chip(grad_gains)).T).T
        grad_values, grad_mlp[0] = lax.optimization_barrier((grad_values, grad_mlp[0]))
        packed = dot(packing, grad_values).astype(BF16).reshape(n_shard, room, D)
        packed = lax.all_to_all(packed, "shard", 0, 0, tiled=True)
        packed, grad_mlp[1] = lax.optimization_barrier((packed, grad_mlp[1]))
        grad_mlp[1] = links.scatter(grad_mlp[1]).astype(BF16).reshape(in_rows, -1)
        rows = packed.reshape(1, n_shard * room, D)
        rows = jnp.concatenate([rows, links.chip(rows)])
        rows, grad_mlp[1], normed_one, grad_attn_out = lax.optimization_barrier(
            (rows, grad_mlp[1], normed_one, grad_attn_out)
        )
        grad_attn_in = weight_grad(pad_blocks(normed_one), mixed_mine, mixed_other)
        grad_small = jnp.concatenate([grad_attn_in, grad_gains.astype(BF16)], 1)
        grad_attn_out = links.scatter(grad_attn_out)[:in_rows].astype(BF16)
        rows = jnp.concatenate([rows, links.core(rows)])
        grad_small = links.scatter(grad_small)[:in_rows].astype(BF16)
        placed = place_rows(kept, received, rows, ranks, sorted_ids, starts, vocab_tile)

        def place_whole(placed, grad_values, kept, received):
            rows = lax.all_gather(lax.all_gather(grad_values, "rep"), "shard")
            ids = local_ids.transpose(1, 0, 2).reshape(-1, tok_rows) - quarter_start
            return place_slowly(kept, received, rows.reshape(-1, tok_rows, D), ids)

        table_sum, table_squares = lax.cond(
            enough, lambda placed, *_: tuple(placed), place_whole, placed, grad_values, kept, received
        )

        parts = [*grad_mlp, grad_attn_out, grad_small[:, :-3]]
        gain_sum = grad_small[:, -3:].astype(F32).T
        squares = jnp.sum(table_squares) + jnp.sum(gain_sum * gain_sum) / n_rep
        for part in parts:
            squares = squares + jnp.sum(jnp.square(part.astype(F32)))
        squares = jnp.sum(lax.all_gather(squares, "rep"))
        squares = jnp.sum(links.spread(jnp.full((8, 128), squares))[:, 0, 0])
        grad_norm = jnp.sqrt(squares)
        clip_scale = CLIP_AT / jnp.maximum(grad_norm, CLIP_AT)

        table_core = links.core(table_sum)
        table_chip = links.chip(table_sum)
        mlp = lax.all_gather(jnp.concatenate(grad_mlp, 1), "rep")
        mlp_in_sum = mlp[:, :, : 2 * units].reshape(n_rep, in_rows, 2, n_shard, unit_part)
        mlp_in_sum = mlp_in_sum.transpose(1, 2, 3, 0, 4).reshape(in_rows, 2 * FF).astype(F32)
        mlp_out_sum = mlp[:, :, 2 * units :].reshape(n_rep * unit_part, D).astype(F32)
        attn = lax.all_gather(jnp.concatenate(parts[2:], 1), "rep")[jnp.array([0, 2, 1, 3])]
        attn = attn.transpose(1, 0, 2).astype(F32)
        out_cols = D // n_rep
        attn_out_sum = attn[:, :, :out_cols].reshape(in_rows, D)
        attn_in_sum = attn[:, :, out_cols:].reshape(in_rows, 2 * in_cols)
        weight_sum = (attn_in_sum, attn_out_sum, mlp_in_sum, mlp_out_sum, gain_sum)
        loss = group_loss + links.core(group_loss)
        loss_sum = loss + links.chip(loss)
        results = [loss_sum, valid_count, grad_norm]
        masters = (
            table_master.T,
            attn_in_master,
            attn_out_master,
            mlp_in_master,
            mlp_out_master,
            gain_master,
        )
        firsts = (
            table_first.T,
            attn_in_first,
            attn_out_first,
            mlp_in_first,
            mlp_out_first,
            gain_first,
        )
        seconds = (
            table_second.T,
            attn_in_second,
            attn_out_second,
            mlp_in_second,
            mlp_out_second,
            gain_second,
        )
        rate_list = rates(seq_len)
        table = (masters[0], firsts[0], seconds[0])
        half = jnp.stack([my_rep, my_rep ^ 1])
        settings = (clip_scale, rate_list[0], vocab_tile)
        new = list(adam(*table, table_sum, table_core, half, *settings))
        olds = [
            tuple(part.reshape(-1, part.shape[-1]) for part in member)
            for member in zip(masters[1:], firsts[1:], seconds[1:], weight_sum)
        ]
        new[0], table_chip = lax.optimization_barrier((new[0], table_chip))
        table_both = links.core(table_chip)
        news = adam_many(olds, clip_scale, rate_list[1:])
        new = adam(*table, table_chip, table_both, half ^ 2, *settings, new)
        results.extend(part.T for part in new)
        for index, new in enumerate(news):
            results.append(new.reshape(masters[1 + index // 4].shape))
        return tuple(results)

    return local


def solution(mesh):
    token = P(("rep", "shard"))
    weight = P(None, "shard", None)
    state = (P("shard", None), weight, weight, weight, weight, P(None, "shard"))
    outs = [P(), P(), P()]
    for spec in state:
        outs.extend([spec] * 4)
    return jax.shard_map(
        build(mesh),
        mesh=mesh,
        in_specs=(token, token, token) + state * 3,
        out_specs=tuple(outs),
        check_vma=False,
    )
```

time: 1240 us -> 839 us (0.68); the launches traced: 1220 us -> 829 us
  local copies, waits for them, and re-layouts: 269 us -> 114 us
  starting transfers between devices: 219 us -> 71.8 us
  other arithmetic: 153 us -> 94.7 us
  blocking collectives: 127 us -> 78.2 us
  Pallas kernels: 182 us -> 200 us
    ppermute x48 -> x0, starting transfers between devices: 119 us -> none  [along(): return lax.ppermute(value, 'shard', pairs)]
    dynamic_update_slice x22 -> x0, local copies, waits for them, and re-layouts: 114 us -> none  [the longest x16 65.2 us: gather(): out = lax.dynamic_update_index_in_dim(out, other, place, 0)]
    ppermute x48 -> x0, waiting for transfers between devices: 80.7 us -> none  [along(): return lax.ppermute(value, 'shard', pairs)]
    all_to_all x0 -> x7, waiting for transfers between devices: none -> 74 us  [the longest x4 25.8 us: scatter(): parts = lax.all_to_all(value, 'shard', 0, 0, tiled=True)]
    all_gather x5, blocking collectives: 127 us -> 53.8 us  [the longest x1 20.6 us: line_gather(): lax.all_gather(value, 'shard', axis_index_groups=self.lines, tiled=True)]
    convert_element_type x33 -> x12, other arithmetic: 66.1 us -> 14.1 us  [the longest x2 5.16 us: weight_grad(): (jnp.where(second_chip, second, first) + sent.astype(F32)).astype(BF16)]
    unnamed x242 -> x197, local copies, waits for them, and re-layouts: 61.4 us -> 16 us
    ppermute x6 -> x13, waiting for transfers between devices: 14.7 us -> 52.9 us  [chip(): return lax.ppermute(value, 'rep', [(r, r ^ 2) for r in range(self.n_rep)])]
  transfers between devices with their start and end apart: 106 -> 44, of which waited for: 41 -> 22; matrix products, arithmetic and copies ran while one was open for 26% -> 24% of each run, Pallas kernels for 3% -> 21%
where the time goes in v3:
time: 839 us; the launch traced here: 829 us
  Pallas kernels  200 us (24%)
  waiting for transfers between devices  175 us (21%)
  local copies, waits for them, and re-layouts  114 us (14%)
  other arithmetic  94.7 us (11%)
  blocking collectives  78.2 us (9%)
  starting transfers between devices  71.8 us (9%)
  matrix products  63.1 us (8%)
  between operations  25.6 us (3%)
    pallas_call x2, Pallas kernels, adam(): pl.pallas_call(functools.partial(adam_kernel, rate=rate), grid_spec=pltpu...  58 us
    ppermute x13, waiting for transfers between devices, chip(): return lax.ppermute(value, 'rep', [(r, r ^ 2) for r in range(self.n_rep)])  52.9 us
    dot_general x20, matrix products, dot(): return lax.dot_general(a, b, (dims, ((), ())), preferred_element_type=F32)  40.9 us
    pallas_call x2, Pallas kernels, head_logits(): pl.pallas_call(functools.partial(logits_kernel, tile=tile), grid=(count /...  33.2 us
    pallas_call x2, Pallas kernels, head_table(): pl.pallas_call(table_kernel, grid_spec=pltpu.PrefetchScalarGridSpec(num_s...  30.5 us
    pallas_call x2, Pallas kernels, head_states(): pl.pallas_call(functools.partial(states_kernel, tile=tile), grid=(count /...  27.4 us
    all_to_all x4, waiting for transfers between devices, scatter(): parts = lax.all_to_all(value, 'shard', 0, 0, tiled=True)  25.8 us
    unnamed x1, blocking collectives  24.4 us
  transfers between devices with their start and end apart: 44, of which 22 were waited for; matrix products, arithmetic and copies ran while one was open for 24% of the time, Pallas kernels for 21%

profile of v3, /device:TPU:0, one launch (start us, length us, event | category | flops | bytes accessed | tf_op | source)
XLA Modules:
  0.0 829.4 jit_solution(5319839970373697320)
XLA Ops:
  10.7 6.1 all-gather.7
  17.4 6.3 all-to-all-start.1
  33.8 20.2 %shard_map.421 = (bf16[960,6144]{1,0:T(8,128)(2,1)}, bf16[512,960]{1,0:T(8,128)(2,1)}) custom-call(s32[512,1]{1,0:T(8,128)} %broadcast_in_dim_reshape.4.ids_ref, f32[960,6144]{1,0:T(8,128)} %bitcast.355), custom_call_target="tpu_custom_call" | custom-call | flops 6039797760 | bytes 35389440 | tf_op jit(solution)/shard_map/pallas_call | solution.py:120
  66.7 22.4 %all-to-all-done.2 = bf16[8,64,960]{2,1,0:T(8,128)(2,1)S(1)} async-done(((bf16[8,64,960]{2,1,0:T(8,128)(2,1)}), bf16[8,64,960]{2,1,0:T(8,128)(2,1)S(1)}, u32[]{:S(2)}, u32[]{:S(2)}) %all-to-all-start.2) | async-done | bytes 983072 | tf_op jit(solution)/shard_map/all_to_all | solution.py:737
  89.7 6.6 conditional.2
  116.2 8.8 %collective-permute-done.1 = bf16[5,128,128]{1,2,0:T(8,128)(2,1)S(1)} collective-permute-done((bf16[5,128,128]{1,2,0:T(8,128)(2,1)S(1)}, bf16[5,128,128]{1,2,0:T(8,128)(2,1)S(1)}, u32[]{:S(2)}, u32[]{:S(2)}) %collective-permute-start.1) | collective-permute-done | bytes 163872 | tf_op jit(solution)/shard_map/ppermute | solution.py:561
  126.9 7.3 collective-permute-done.2
  136.1 14.5 %all-gather.17.cloned.1.call-done = bf16[960,1920]{1,0:T(8,128)(2,1)} async-done(((bf16[120,1920]{1,0:T(8,128)(2,1)}), bf16[960,1920]{1,0:T(8,128)(2,1)}) %all-gather.17.cloned.1.call-update) | async-done | bytes 3686416 | tf_op jit(solution)/shard_map/all_gather | solution.py:736
  159.2 5.9 fusion.163
  177.1 9.7 %all-gather.3 = bf16[512,960]{0,1:T(8,128)(2,1)S(1)} all-gather(bf16[128,960]{0,1:T(8,128)(2,1)S(1)} %multiply_convert_fusion.4), channel_id=5, replica_groups=mesh['rep'=4,'shard'=8] {'rep'}, dimensions={0}, use_global_device_ids=true | all-gather | bytes 1228800 | tf_op jit(solution)/shard_map/all_gather | solution.py:602
  207.0 20.6 %all_gather.63 = bf16[512,960]{0,1:T(8,128)(2,1)S(1)} all-gather(bf16[128,960]{0,1:T(8,128)(2,1)S(1)} %multiply_convert_fusion.3), channel_id=1, replica_groups={{0,2,4,6},{1,3,5,7},{8,10,12,14},{9,11,13,15},{16,18,20,22},{17,19,21,2..., dimensions={0}, use_global_device_ids=true | all-gather | bytes 1228800 | tf_op jit(solution)/shard_map/all_gather | solution.py:575
  232.0 16.6 %shard_map.422 = (bf16[512,6144]{1,0:T(8,128)(2,1)}, f32[512,128]{1,0:T(8,128)}) custom-call(bf16[512,960]{1,0:T(8,128)(2,1)} %copy.529.states_ref, s32[512,1]{1,0:T(8,128)} %copy.530.targets_ref, bf16[960,6144]{1,0:T(8,128)(2,1)} %get-tuple-element.160.table_ref), custom_call_target="tpu_custom_call" | custom-call | flops 6039797760 | bytes 18087936 | tf_op jit(solution)/shard_map/pallas_call | solution.py:170
  251.5 16.6 %shard_map.423 = (bf16[512,6144]{1,0:T(8,128)(2,1)}, f32[512,128]{1,0:T(8,128)}) custom-call(bf16[512,960]{1,0:T(8,128)(2,1)} %copy.531.states_ref, s32[512,1]{1,0:T(8,128)} %copy.532.targets_ref, bf16[960,6144]{1,0:T(8,128)(2,1)} %get-tuple-element.160.table_ref), custom_call_target="tpu_custom_call" | custom-call | flops 6039797760 | bytes 18087936 | tf_op jit(solution)/shard_map/pallas_call | solution.py:170
  287.1 13.7 %shard_map.424 = (bf16[512,6144]{1,0:T(8,128)(2,1)}, bf16[512,960]{1,0:T(8,128)(2,1)}) custom-call(bf16[512,6144]{1,0:T(8,128)(2,1)} %get-tuple-element.174.raised_ref, f32[512,2]{1,0:T(8,128)} %copy.539.scales_ref, s32[512,1]{1,0:T(8,128)} %copy.532.targets_ref, bf16[960,6144]{1,0:T(8,128)(2,1)} %get-tuple-element.160.table_ref), custom_call_target="tpu_custom_call" | custom-call | flops 6039797760 | bytes 24379392 | tf_op jit(solution)/shard_map/pallas_call | solution.py:216
  305.1 13.7 %shard_map.425 = (bf16[512,6144]{1,0:T(8,128)(2,1)}, bf16[512,960]{1,0:T(8,128)(2,1)}) custom-call(bf16[512,6144]{1,0:T(8,128)(2,1)} %get-tuple-element.176.raised_ref, f32[512,2]{1,0:T(8,128)} %copy.541.scales_ref, s32[512,1]{1,0:T(8,128)} %copy.530.targets_ref, bf16[960,6144]{1,0:T(8,128)(2,1)} %get-tuple-element.160.table_ref), custom_call_target="tpu_custom_call" | custom-call | flops 6039797760 | bytes 24379392 | tf_op jit(solution)/shard_map/pallas_call | solution.py:216
  322.1 15.6 %shard_map.427 = bf16[960,1536]{1,0:T(8,128)(2,1)} custom-call(s32[1]{0:T(128)} %bitcast.22.part_ref, bf16[960,512]{1,0:T(8,128)(2,1)} %bitcast.365, bf16[960,512]{1,0:T(8,128)(2,1)} %bitcast.376, bf16[960,512]{1,0:T(8,128)(2,1)} %bitcast.378, bf16[960,512]{1,0:T(8,128)(2,1)} %bitcast.70.far_pair_t, bf16[512,6144]{1,0:T(8,128)(2,1)} %get-tuple-element.177.near_grads, ...), custom_call_target="tpu_custom_call" | custom-call | flops 9059696640 | bytes 14942208 | tf_op jit(solution)/shard_map/pallas_call | solution.py:297
  345.9 14.9 %shard_map.426.kept_ref = bf16[960,1536]{1,0:T(8,128)(2,1)S(1)} custom-call(s32[1]{0:T(128)} %bitcast.20.part_ref, bf16[960,512]{1,0:T(8,128)(2,1)} %bitcast.366, bf16[960,512]{1,0:T(8,128)(2,1)} %bitcast.377, bf16[960,512]{1,0:T(8,128)(2,1)} %bitcast.379, bf16[960,512]{1,0:T(8,128)(2,1)} %bitcast.70.far_pair_t, ...), custom_call_target="tpu_custom_call" | custom-call | flops 9059696640 | bytes 14942208 | tf_op jit(solution)/shard_map/pallas_call | solution.py:297
  360.8 6.4 all-to-all-done.5
  369.8 9.2 %all-gather.4 = bf16[512,960]{0,1:T(8,128)(2,1)} all-gather(bf16[128,960]{0,1:T(8,128)(2,1)S(1)} %fusion.94), channel_id=6, replica_groups=mesh['rep'=4,'shard'=8] {'rep'}, dimensions={0}, use_global_device_ids=true | all-gather | bytes 1228800 | tf_op jit(solution)/shard_map/all_gather | solution.py:602
  443.3 8.4 %collective-permute-done.17 = bf16[2,5,128,128]{2,3,1,0:T(8,128)(2,1)} collective-permute-done((bf16[2,5,128,128]{2,3,1,0:T(8,128)(2,1)S(1)}, bf16[2,5,128,128]{2,3,1,0:T(8,128)(2,1)}, u32[]{:S(2)}, u32[]{:S(2)}) %collective-permute-start.17) | collective-permute-done | bytes 327712 | tf_op jit(solution)/shard_map/ppermute | solution.py:613
  480.2 6.1 all-to-all-start.7
  492.9 19.4 %all-to-all-done.7 = bf16[8,64,960]{2,1,0:T(8,128)(2,1)} async-done(((bf16[8,64,960]{2,1,0:T(8,128)(2,1)}), bf16[8,64,960]{2,1,0:T(8,128)(2,1)}, u32[]{:S(2)}, u32[]{:S(2)}) %all-to-all-start.7) | async-done | bytes 983072 | tf_op jit(solution)/shard_map/all_to_all | solution.py:958
  528.1 31.2 %collective-permute-done.21 = bf16[1024,240]{0,1:T(8,128)(2,1)S(1)} collective-permute-done((bf16[1024,240]{0,1:T(8,128)(2,1)S(1)}, bf16[1024,240]{0,1:T(8,128)(2,1)S(1)}, u32[]{:S(2)}, u32[]{:S(2)}) %collective-permute-start.21) | collective-permute-done | bytes 491552 | tf_op jit(solution)/shard_map/ppermute | solution.py:613
  599.7 12.5 %shard_map.428 = (bf16[960,1536]{1,0:T(8,128)(2,1)}, f32[1,128]{1,0:T(1,128)S(1)}) custom-call(s32[4]{0:T(128)} %convert_reduce_fusion.4.starts_ref, s32[2048,1]{1,0:T(8,128)} %copy.574.ranks_ref, s32[2048,1]{1,0:T(8,128)} %copy.575.ids_ref, bf16[4,512,960]{2,1,0:T(8,128)(2,1)} %pad_maximum_fusion.rows_ref, bf16[960,1536]{1,0:T(8,128)(2,1)S(1)} %shard_map.426.kept_ref, ...), custom_call_target="tpu_custom_call" | custom-call | flops 503316480 | bytes 12779520 | tf_op jit(solution)/shard_map/pallas_call | solution.py:413
  626.3 9.4 %all-to-all-done.10 = bf16[8,128,240]{1,2,0:T(8,128)(2,1)} async-done(((bf16[8,128,240]{1,2,0:T(8,128)(2,1)}), bf16[8,128,240]{1,2,0:T(8,128)(2,1)}, u32[]{:S(2)}, u32[]{:S(2)}) %all-to-all-start.10) | async-done | bytes 491552 | tf_op jit(solution)/shard_map/all_to_all | solution.py:585
  644.6 16.4 %all-to-all-done.9 = bf16[8,128,403]{1,2,0:T(8,128)(2,1)} async-done(((bf16[8,128,403]{1,2,0:T(8,128)(2,1)}), bf16[8,128,403]{1,2,0:T(8,128)(2,1)}, u32[]{:S(2)}, u32[]{:S(2)}) %all-to-all-start.9) | async-done | bytes 825376 | tf_op jit(solution)/shard_map/all_to_all | solution.py:585
  668.2 24.4 %all-reduce.8 = f32[4]{0:T(128)S(1)} all-reduce(f32[4]{0:T(128)S(1)} %dynamic-update-slice), channel_id=1, replica_groups=mesh['rep'=4,'shard'=8] {'rep'}, use_global_device_ids=true, to_apply=%add.8 | all-reduce | flops 4 | bytes 32
  699.1 6.1 all-to-all-done.11
  706.5 28.6 %shard_map.429 = (f32[960,6144]{1,0:T(8,128)}, f32[960,6144]{1,0:T(8,128)}, f32[960,6144]{1,0:T(8,128)}, bf16[960,6144]{1,0:T(8,128)(2,1)}) custom-call(s32[2]{0:T(128)} %get-tuple-element.315.quarters_ref, f32[1]{0:T(128)} %bitcast.121.scale_ref, f32[960,6144]{1,0:T(8,128)} %bitcast.356, f32[960,6144]{1,0:T(8,128)} %bitcast.358, f32[960,6144]{1,0:T(8,128)} %bitcast.360, ...), custom_call_target="tpu_custom_call" | custom-call | tf_op jit(solution)/shard_map/pallas_call | solution.py:465
  759.9 8.2 all-gather.5
  772.6 18.3 %shard_map.431 = (f32[120,1600]{1,0:T(8,128)}, f32[120,1600]{1,0:T(8,128)}, f32[120,1600]{1,0:T(8,128)}, bf16[120,1600]{1,0:T(8,128)(2,1)}, f32[120,960]{1,0:T(8...) custom-call(f32[1]{0:T(128)} %bitcast.121.scale_ref, ...), custom_call_target="tpu_custom_call" | custom-call | tf_op jit(solution)/shard_map/pallas_call | solution.py:521
  790.9 29.4 %shard_map.430 = (f32[960,6144]{1,0:T(8,128)}, f32[960,6144]{1,0:T(8,128)}, f32[960,6144]{1,0:T(8,128)}, bf16[960,6144]{1,0:T(8,128)(2,1)}) custom-call(s32[2]{0:T(128)} %get-tuple-element.314.quarters_ref, f32[1]{0:T(128)} %bitcast.121.scale_ref, f32[960,6144]{1,0:T(8,128)} %bitcast.357, ...), custom_call_target="tpu_custom_call", output_to_operand_aliasing={{0}: (7, {}), {1}: (8, {}), {2}: (9, {}), {3}: (10, {})} | custom-call | tf_op jit(solution)/shard_map/pallas_call | solution.py:465
  (530 shorter events, 352.6 us)
Async XLA Ops:
  7.2 99.7 %all-gather.15.cloned.1.call-start = ((), (), s32[]{:S(2)}) async-start(), calls=%async_computation.13 | async-start | bytes 2764800 | tf_op jit(solution)/shard_map/all_gather | solution.py:702
  17.4 13.8 %all-to-all-start.1 = ((s32[8,4,3,128]{3,1,2,0:T(4,128)}), s32[8,4,3,128]{3,1,2,0:T(4,128)S(1)}, u32[]{:S(2)}, u32[]{:S(2)}) async-start(s32[8,4,3,128]{3,1,2,0:T(4,128)} %broadcast_in_dim.69), calls=%async_computation.1 | async-start | bytes 98304 | tf_op jit(solution)/shard_map/all_to_all | solution.py:590
  54.0 35.1 %all-to-all-start.2 = ((bf16[8,64,960]{2,1,0:T(8,128)(2,1)}), bf16[8,64,960]{2,1,0:T(8,128)(2,1)S(1)}, u32[]{:S(2)}, u32[]{:S(2)}) async-start(bf16[8,64,960]{2,1,0:T(8,128)(2,1)} %bitcast.420), calls=%async_computation.2 | async-start | bytes 2097152 | tf_op jit(solution)/shard_map/all_to_all | solution.py:737
  57.5 93.1 %all-gather.17.cloned.1.call-start = ((), (), s32[]{:S(2)}) async-start(), calls=%async_computation.14 | async-start | bytes 4147200 | tf_op jit(solution)/shard_map/all_gather | solution.py:736
  114.7 10.3 %collective-permute-start.1 = (bf16[5,128,128]{1,2,0:T(8,128)(2,1)S(1)}, bf16[5,128,128]{1,2,0:T(8,128)(2,1)S(1)}, u32[]{:S(2)}, u32[]{:S(2)}) collective-permute-start(bf16[5,128,128]{1,2,0:T(8,128)(2,1)S(1)} %get-tuple-element.345), channel_id=1, source_target_pairs={{0,1},{1,0},{2,3},{3,2},{4,5},{5,4},{6,7},{7,6},{8,9},{9,8},{10,11... | collective-permute-start | bytes 491528 | tf_op jit(solution)/shard_map/ppermute | solution.py:561
  135.1 19.8 %collective-permute-start.3 = (bf16[2,2,5,128,128]{3,4,2,1,0:T(8,128)(2,1)}, bf16[2,2,5,128,128]{3,4,2,1,0:T(8,128)(2,1)}, u32[]{:S(2)}, u32[]{:S(2)}) collective-permute-start(bf16[2,2,5,128,128]{3,4,2,1,0:T(8,128)(2,1)} %pad_maximum_fusion.8), channel_id=1, source_target_pairs={{0,8},{8,0},{16,24},{24,16},{1,9},{9,1},{17,25},{25,17},{2,10},{10... | collective-permute-start | bytes 1966088 | tf_op jit(solution)/shard_map/ppermute | solution.py:593
  227.7 22.4 %collective-permute-start.6 = (bf16[512,960]{0,1:T(8,128)(2,1)S(1)}, bf16[512,960]{0,1:T(8,128)(2,1)S(1)}, u32[]{:S(2)}, u32[]{:S(2)}) collective-permute-start(bf16[512,960]{0,1:T(8,128)(2,1)S(1)} %all_gather.63), channel_id=1, source_target_pairs={{0,1},{1,0},{2,3},{3,2},{4,5},{5,4},{6,7},{7,6},{8,9},{9,8},{10,11... | collective-permute-start | bytes 2949128 | tf_op jit(solution)/shard_map/ppermute | solution.py:561
  231.4 50.1 %collective-permute-start.9 = (bf16[512,960]{0,1:T(8,128)(2,1)S(1)}, bf16[512,960]{0,1:T(8,128)(2,1)S(1)}, u32[]{:S(2)}, u32[]{:S(2)}) collective-permute-start(bf16[512,960]{0,1:T(8,128)(2,1)S(1)} %all_gather.63), channel_id=1, source_target_pairs={{0,16},{8,24},{16,0},{24,8},{1,17},{9,25},{17,1},{25,9},{2,18},{10... | collective-permute-start | bytes 2949128 | tf_op jit(solution)/shard_map/ppermute | solution.py:613
  273.5 10.8 %all-to-all-start.4 = ((f32[8,3,2,4,128]{4,3,2,1,0:T(4,128)}), f32[8,3,2,4,128]{4,3,2,1,0:T(4,128)S(1)}, u32[]{:S(2)}, u32[]{:S(2)}) async-start(f32[8,3,2,4,128]{4,3,2,1,0:T(4,128)} %broadcast_in_dim.83), calls=%async_computation.4 | async-start | bytes 196608 | tf_op jit(solution)/shard_map/all_to_all | solution.py:590
  280.9 39.0 %collective-permute-start.10 = (bf16[512,960]{0,1:T(8,128)(2,1)S(1)}, bf16[512,960]{0,1:T(8,128)(2,1)}, u32[]{:S(2)}, u32[]{:S(2)}) collective-permute-start(bf16[512,960]{0,1:T(8,128)(2,1)S(1)} %collective-permute-done.6), channel_id=1, source_target_pairs={{0,16},{8,24},{16,0},{24,8},{1,17},{9,25},{17,1},{25,9},{2,18},{10... | collective-permute-start | bytes 2949128 | tf_op jit(solution)/shard_map/ppermute | solution.py:613
  285.0 33.8 %collective-permute-start.11 = (f32[1024]{0:T(1024)S(1)}, f32[1024]{0:T(1024)S(1)}, u32[]{:S(2)}, u32[]{:S(2)}) collective-permute-start(f32[1024]{0:T(1024)S(1)} %bitcast.481), channel_id=1, source_target_pairs={{0,16},{8,24},{16,0},{24,8},{1,17},{9,25},{17,1},{25,9},{2,18},{10... | collective-permute-start | bytes 12296 | tf_op jit(solution)/shard_map/ppermute | solution.py:613
  303.1 34.5 %collective-permute-start.12 = (bf16[512,960]{0,1:T(8,128)(2,1)S(1)}, bf16[512,960]{0,1:T(8,128)(2,1)S(1)}, u32[]{:S(2)}, u32[]{:S(2)}) collective-permute-start(bf16[512,960]{0,1:T(8,128)(2,1)S(1)} %copy.555), channel_id=1, source_target_pairs={{0,1},{1,0},{2,3},{3,2},{4,5},{5,4},{6,7},{7,6},{8,9},{9,8},{10,11... | collective-permute-start | bytes 2949128 | tf_op jit(solution)/shard_map/ppermute | solution.py:561
  341.1 26.1 %all-to-all-start.5 = ((bf16[4,128,960]{1,2,0:T(8,128)(2,1)}), bf16[4,128,960]{1,2,0:T(8,128)(2,1)}, u32[]{:S(2)}, u32[]{:S(2)}) async-start(bf16[4,128,960]{1,2,0:T(8,128)(2,1)} %copy.557), calls=%async_computation.5 | async-start | bytes 1966080 | tf_op jit(solution)/shard_map/all_to_all | solution.py:578
  406.0 65.0 %all-to-all-start.6 = ((bf16[8,128,1280]{2,1,0:T(8,128)(2,1)}), bf16[8,128,1280]{2,1,0:T(8,128)(2,1)}, u32[]{:S(2)}, u32[]{:S(2)}) async-start(bf16[8,128,1280]{2,1,0:T(8,128)(2,1)} %bitcast.397), calls=%async_computation.6 | async-start | bytes 5242880 | tf_op jit(solution)/shard_map/all_to_all | solution.py:585
  454.5 11.2 %collective-permute-start.18 = (bf16[5,128,128]{1,2,0:T(8,128)(2,1)}, bf16[5,128,128]{1,2,0:T(8,128)(2,1)}, u32[]{:S(2)}, u32[]{:S(2)}) collective-permute-start(bf16[5,128,128]{1,2,0:T(8,128)(2,1)} %fusion.92), channel_id=1, source_target_pairs={{0,1},{1,0},{2,3},{3,2},{4,5},{5,4},{6,7},{7,6},{8,9},{9,8},{10,11... | collective-permute-start | bytes 491528 | tf_op jit(solution)/shard_map/ppermute | solution.py:561
  480.2 32.1 %all-to-all-start.7 = ((bf16[8,64,960]{2,1,0:T(8,128)(2,1)}), bf16[8,64,960]{2,1,0:T(8,128)(2,1)}, u32[]{:S(2)}, u32[]{:S(2)}) async-start(bf16[8,64,960]{2,1,0:T(8,128)(2,1)} %bitcast.387), calls=%async_computation.7 | async-start | bytes 2097152 | tf_op jit(solution)/shard_map/all_to_all | solution.py:958
  489.6 29.6 %collective-permute-start.20 = (bf16[1024,480]{0,1:T(8,128)(2,1)}, bf16[1024,480]{0,1:T(8,128)(2,1)}, u32[]{:S(2)}, u32[]{:S(2)}) collective-permute-start(bf16[1024,480]{0,1:T(8,128)(2,1)} %convolution_convert_fusion.3), channel_id=1, source_target_pairs={{0,8},{8,0},{16,24},{24,16},{1,9},{9,1},{17,25},{25,17},{2,10},{10... | collective-permute-start | bytes 2949128 | tf_op jit(solution)/shard_map/ppermute | solution.py:593
  514.7 52.4 %all-to-all-start.8 = ((bf16[8,80,960]{2,1,0:T(8,128)(2,1)}), bf16[8,80,960]{2,1,0:T(8,128)(2,1)}, u32[]{:S(2)}, u32[]{:S(2)}) async-start(bf16[8,80,960]{2,1,0:T(8,128)(2,1)} %bitcast.382), calls=%async_computation.8 | async-start | bytes 2621440 | tf_op jit(solution)/shard_map/all_to_all | solution.py:585
  519.1 66.0 %collective-permute-start.13 = (bf16[960,1536]{1,0:T(8,128)(2,1)}, bf16[960,1536]{1,0:T(8,128)(2,1)}, u32[]{:S(2)}, u32[]{:S(2)}) collective-permute-start(bf16[960,1536]{1,0:T(8,128)(2,1)} %shard_map.427), channel_id=1, source_target_pairs={{0,8},{8,0},{16,24},{24,16},{1,9},{9,1},{17,25},{25,17},{2,10},{10... | collective-permute-start | bytes 8847368 | tf_op jit(solution)/shard_map/ppermute | solution.py:593
  524.4 37.4 %collective-permute-start.19 = (bf16[1,512,960]{1,2,0:T(8,128)(2,1)}, bf16[1,512,960]{1,2,0:T(8,128)(2,1)}, u32[]{:S(2)}, u32[]{:S(2)}) collective-permute-start(bf16[1,512,960]{1,2,0:T(8,128)(2,1)} %copy.568), channel_id=1, source_target_pairs={{0,16},{8,24},{16,0},{24,8},{1,17},{9,25},{17,1},{25,9},{2,18},{10... | collective-permute-start | bytes 2949128 | tf_op jit(solution)/shard_map/ppermute | solution.py:613
  526.6 32.7 %collective-permute-start.21 = (bf16[1024,240]{0,1:T(8,128)(2,1)S(1)}, bf16[1024,240]{0,1:T(8,128)(2,1)S(1)}, u32[]{:S(2)}, u32[]{:S(2)}) collective-permute-start(bf16[1024,240]{0,1:T(8,128)(2,1)S(1)} %select_convert_fusion.1), channel_id=1, source_target_pairs={{0,16},{8,24},{16,0},{24,8},{1,17},{9,25},{17,1},{25,9},{2,18},{10... | collective-permute-start | bytes 1474568 | tf_op jit(solution)/shard_map/ppermute | solution.py:613
  573.3 11.7 %collective-permute-start.23 = (bf16[1024,800]{0,1:T(8,128)(2,1)}, bf16[1024,800]{0,1:T(8,128)(2,1)}, u32[]{:S(2)}, u32[]{:S(2)}) collective-permute-start(bf16[1024,800]{0,1:T(8,128)(2,1)} %convolution_convert_fusion.1), channel_id=1, source_target_pairs={{0,8},{8,0},{16,24},{24,16},{1,9},{9,1},{17,25},{25,17},{2,10},{10... | collective-permute-start | bytes 4915208 | tf_op jit(solution)/shard_map/ppermute | solution.py:593
  577.2 14.1 %collective-permute-start.22 = (bf16[2,512,960]{1,2,0:T(8,128)(2,1)}, bf16[2,512,960]{1,2,0:T(8,128)(2,1)}, u32[]{:S(2)}, u32[]{:S(2)}) collective-permute-start(bf16[2,512,960]{1,2,0:T(8,128)(2,1)} %copy.572), channel_id=1, source_target_pairs={{0,8},{8,0},{16,24},{24,16},{1,9},{9,1},{17,25},{25,17},{2,10},{10... | collective-permute-start | bytes 5898248 | tf_op jit(solution)/shard_map/ppermute | solution.py:593
  584.5 36.9 %collective-permute-start.26 = (f32[960,3]{0,1:T(4,128)}, f32[960,3]{0,1:T(4,128)}, u32[]{:S(2)}, u32[]{:S(2)}) collective-permute-start(f32[960,3]{0,1:T(4,128)} %fusion.151), channel_id=1, source_target_pairs={{0,16},{8,24},{16,0},{24,8},{1,17},{9,25},{17,1},{25,9},{2,18},{10... | collective-permute-start | bytes 34568 | tf_op jit(solution)/shard_map/ppermute | solution.py:613
  589.8 32.5 %collective-permute-start.24 = (bf16[1024,400]{0,1:T(8,128)(2,1)}, bf16[1024,400]{0,1:T(8,128)(2,1)}, u32[]{:S(2)}, u32[]{:S(2)}) collective-permute-start(bf16[1024,400]{0,1:T(8,128)(2,1)} %select_convert_fusion), channel_id=1, source_target_pairs={{0,16},{8,24},{16,0},{24,8},{1,17},{9,25},{17,1},{25,9},{2,18},{10... | collective-permute-start | bytes 2457608 | tf_op jit(solution)/shard_map/ppermute | solution.py:613
  614.9 91.6 %collective-permute-start.27 = (bf16[960,1536]{1,0:T(8,128)(2,1)S(1)}, bf16[960,1536]{1,0:T(8,128)(2,1)}, u32[]{:S(2)}, u32[]{:S(2)}) collective-permute-start(bf16[960,1536]{1,0:T(8,128)(2,1)S(1)} %get-tuple-element.197.one_ref), channel_id=1, source_target_pairs={{0,8},{8,0},{16,24},{24,16},{1,9},{9,1},{17,25},{25,17},{2,10},{10... | collective-permute-start | bytes 8847368 | tf_op jit(solution)/shard_map/ppermute | solution.py:593
  614.9 120.2 %collective-permute-start.28 = (bf16[960,1536]{1,0:T(8,128)(2,1)S(1)}, bf16[960,1536]{1,0:T(8,128)(2,1)}, u32[]{:S(2)}, u32[]{:S(2)}) collective-permute-start(bf16[960,1536]{1,0:T(8,128)(2,1)S(1)} %get-tuple-element.197.one_ref), channel_id=1, source_target_pairs={{0,16},{8,24},{16,0},{24,8},{1,17},{9,25},{17,1},{25,9},{2,18},{10... | collective-permute-start | bytes 8847368 | tf_op jit(solution)/shard_map/ppermute | solution.py:613
  616.8 18.9 %all-to-all-start.10 = ((bf16[8,128,240]{1,2,0:T(8,128)(2,1)}), bf16[8,128,240]{1,2,0:T(8,128)(2,1)}, u32[]{:S(2)}, u32[]{:S(2)}) async-start(bf16[8,128,240]{1,2,0:T(8,128)(2,1)} %copy_bitcast_fusion.2), calls=%async_computation.10 | async-start | bytes 983040 | tf_op jit(solution)/shard_map/all_to_all | solution.py:585
  635.7 25.3 %all-to-all-start.9 = ((bf16[8,128,403]{1,2,0:T(8,128)(2,1)}), bf16[8,128,403]{1,2,0:T(8,128)(2,1)}, u32[]{:S(2)}, u32[]{:S(2)}) async-start(bf16[8,128,403]{1,2,0:T(8,128)(2,1)} %copy.577), calls=%async_computation.9 | async-start | bytes 1671168 | tf_op jit(solution)/shard_map/all_to_all | solution.py:585
  639.9 106.6 %all-gather.19.cloned.1.call-start = ((), (), s32[]{:S(2)}) async-start(), calls=%async_computation.15 | async-start | bytes 2304000 | tf_op jit(solution)/shard_map/all_gather | solution.py:994
  694.4 10.7 %all-to-all-start.11 = ((f32[8,8,128]{2,1,0:T(8,128)}), f32[8,8,128]{2,1,0:T(8,128)S(1)}, u32[]{:S(2)}, u32[]{:S(2)}) async-start(f32[8,8,128]{2,1,0:T(8,128)} %broadcast_in_dim_broadcast_in_dim_broadcast_in_dim.3), calls=%async_computation.11 | async-start | bytes 65536 | tf_op jit(solution)/shard_map/all_to_all | solution.py:590
  735.1 55.8 %collective-permute-start.29 = (bf16[960,1536]{1,0:T(8,128)(2,1)}, bf16[960,1536]{1,0:T(8,128)(2,1)}, u32[]{:S(2)}, u32[]{:S(2)}) collective-permute-start(bf16[960,1536]{1,0:T(8,128)(2,1)} %collective-permute-done.28.one_ref), channel_id=1, source_target_pairs={{0,8},{8,0},{16,24},{24,16},{1,9},{9,1},{17,25},{25,17},{2,10},{10... | collective-permute-start | bytes 8847368 | tf_op jit(solution)/shard_map/ppermute | solution.py:593
  (107 other events, 1216.3 us)
Sparse Core Ops, SparseCore 0:
  10.8 62.8 all-gather.14
  76.5 74.1 all-gather.16
  642.9 32.7 all-gather.18

commit v4 on v3

--- a/solution.py
+++ b/solution.py
@@ -341,20 +341,15 @@
     starts_ref,
     ranks_ref,
     ids_ref,
-    rows_ref,
-    kept_ref,
-    received_ref,
-    out_ref,
-    square_ref,
-    sorted_rows,
-    total,
-    *,
+    *refs,
     chunk,
     block,
 ):
+    rows_refs = refs[:-6]
+    kept_ref, received_ref, out_ref, square_ref, sorted_rows, total = refs[-6:]
     step = pl.program_id(0)
     tile = out_ref.shape[1]
-    sources, lanes, _ = rows_ref.shape
+    lanes = rows_refs[0].shape[0]
 
     @pl.when(step == 0)
     def _():
@@ -362,10 +357,10 @@
             columns = pl.ds(pl.multiple_of(k * block, block), block)
             wanted = lax.broadcasted_iota(jnp.int32, (1, block), 1) + k * block
             found = None
-            for source in range(sources):
+            for source, rows_ref in enumerate(rows_refs):
                 pick = ranks_ref[source * lanes : (source + 1) * lanes, :] == wanted
                 pick = jnp.where(pick, 1.0, 0.0).astype(BF16)
-                part = dot(rows_ref[source], pick, ((0,), (0,)))
+                part = dot(rows_ref[...], pick, ((0,), (0,)))
                 found = part if found is None else found + part
             sorted_rows[:, columns] = found.astype(BF16)
             return carry
@@ -406,8 +401,8 @@
 
 def place_rows(kept, received, rows, ranks, ids, starts, tile, chunk=128, block=256):
     width, columns = kept.shape
-    sources, lanes, _ = rows.shape
-    total = sources * lanes
+    lanes = rows[0].shape[0]
+    total = len(rows) * lanes
     block = min(block, total)
     spec = pl.BlockSpec((width, tile), lambda i, starts: (0, i))
     return pl.pallas_call(
@@ -415,7 +410,8 @@
         grid_spec=pltpu.PrefetchScalarGridSpec(
             num_scalar_prefetch=1,
             grid=(columns // tile,),
-            in_specs=[whole((total, 1)), whole((total, 1)), whole((sources, lanes, width))]
+            in_specs=[whole((total, 1)), whole((total, 1))]
+            + [whole((lanes, width))] * len(rows)
             + [spec] * 2,
             out_specs=[spec, whole((1, 128))],
             scratch_shapes=[pltpu.VMEM((width, total), BF16), pltpu.VMEM((width, tile), F32)],
@@ -430,64 +426,57 @@
             bytes_accessed=6 * width * columns + 2 * total * width,
             transcendentals=0,
         ),
-    )(starts, ranks[:, None], ids[:, None], rows, kept, received)
-
-
-def adam_kernel(quarters_ref, scale_ref, w_ref, m_ref, v_ref, one_ref, two_ref, *refs, rate):
-    step = pl.program_id(0)
-    half = pl.num_programs(0) // 2
-    outs = refs[-4:]
-
-    def update(gradient):
-        new = adam_update(w_ref[...], m_ref[...], v_ref[...], gradient * scale_ref[0], rate)
-        for ref, value in zip(outs, new):
-            ref[...] = value
-
-    @pl.when(step < half)
-    def _():
-        update(one_ref[...].astype(F32))
-
-    @pl.when(step >= half)
-    def _():
-        update(two_ref[...].astype(F32))
-
-
-def adam(master, first, second, one, two, quarters, scale, rate, tile, before=None):
+    )(starts, ranks[:, None], ids[:, None], *rows, kept, received)
+
+
+def adam_kernel(quarters_ref, scale_ref, w_ref, m_ref, v_ref, *refs, rate, count):
+    grads, outs = refs[:count], refs[-4:]
+    part = pl.program_id(0) // (pl.num_programs(0) // count)
+    for index, ref in enumerate(grads):
+
+        @pl.when(part == index)
+        def _(ref=ref):
+            gradient = ref[...].astype(F32) * scale_ref[0]
+            new = adam_update(w_ref[...], m_ref[...], v_ref[...], gradient, rate)
+            for out, value in zip(outs, new):
+                out[...] = value
+
+
+def adam(master, first, second, grads, quarters, scale, rate, tile, before=()):
     rows, columns = master.shape
-    steps = one.shape[1] // tile
+    count = len(grads)
+    steps = grads[0].shape[1] // tile
 
     def column(i, quarters):
         return (0, quarters[i // steps] * steps + i % steps)
 
+    def own(index):
+        return lambda i, quarters: (0, jnp.clip(i - index * steps, 0, steps - 1))
+
     spec = pl.BlockSpec((rows, tile), column)
     shape = jax.ShapeDtypeStruct((rows, columns), F32)
-    before = list(before or [])
     return pl.pallas_call(
-        functools.partial(adam_kernel, rate=rate),
+        functools.partial(adam_kernel, rate=rate, count=count),
         grid_spec=pltpu.PrefetchScalarGridSpec(
             num_scalar_prefetch=1,
-            grid=(2 * steps,),
+            grid=(count * steps,),
             in_specs=[pl.BlockSpec(memory_space=pltpu.SMEM)]
             + [spec] * 3
-            + [
-                pl.BlockSpec((rows, tile), lambda i, q: (0, jnp.minimum(i, steps - 1))),
-                pl.BlockSpec((rows, tile), lambda i, q: (0, jnp.maximum(i - steps, 0))),
-            ]
+            + [pl.BlockSpec((rows, tile), own(index)) for index in range(count)]
             + [pl.BlockSpec(memory_space=pl.ANY)] * len(before),
             out_specs=[spec] * 4,
         ),
         out_shape=[shape] * 3 + [jax.ShapeDtypeStruct((rows, columns), BF16)],
-        input_output_aliases={7 + k: k for k in range(len(before))},
+        input_output_aliases={5 + count + k: k for k in range(len(before))},
         compiler_params=params(),
         cost_estimate=pl.CostEstimate(flops=0, bytes_accessed=0, transcendentals=0),
     )(
-        quarters.astype(jnp.int32),
+        jnp.stack(quarters).astype(jnp.int32),
         jnp.reshape(scale, (1,)),
         master,
         first,
         second,
-        one,
-        two,
+        *grads,
         *before,
     )
 
@@ -505,23 +494,30 @@
         def update(k, carry, olds=olds, news=news, block=block, rate=rate):
             place = pl.ds(pl.multiple_of(k * block, block), block)
             w, m, v, g = (ref[place, :] for ref in olds)
-            for ref, value in zip(news, adam_update(w, m, v, g * scale, rate)):
+            for ref, value in zip(news, adam_update(w, m, v, g.astype(F32) * scale, rate)):
                 ref[place, :] = value
             return carry
 
         lax.fori_loop(0, rows // block, update, 0)
 
 
-def adam_many(olds, scale, rates):
-    shapes = []
-    for master, *_ in olds:
+def adam_many(olds, scale, rates, steps=5):
+    if any(master.shape[0] % (8 * steps) for master, *_ in olds[:-1]):
+        steps = 1
+    shapes, specs = [], []
+    for index, (master, *_) in enumerate(olds):
+        rows, columns = master.shape
         shapes += [jax.ShapeDtypeStruct(master.shape, F32)] * 3
         shapes += [jax.ShapeDtypeStruct(master.shape, BF16)]
-    inside = pl.BlockSpec(memory_space=pltpu.VMEM)
+        if index < len(olds) - 1:
+            specs += [pl.BlockSpec((rows // steps, columns), lambda i: (i, 0))] * 4
+        else:
+            specs += [pl.BlockSpec((rows, columns), lambda i: (0, 0))] * 4
     return pl.pallas_call(
         functools.partial(adam_many_kernel, rates=rates),
-        in_specs=[pl.BlockSpec(memory_space=pltpu.SMEM)] + [inside] * (4 * len(olds)),
-        out_specs=[inside] * (4 * len(olds)),
+        grid=(steps,),
+        in_specs=[pl.BlockSpec(memory_space=pltpu.SMEM)] + specs,
+        out_specs=specs,
         out_shape=shapes,
         compiler_params=params(),
         cost_estimate=pl.CostEstimate(flops=0, bytes_accessed=0, transcendentals=0),
@@ -597,12 +593,16 @@
         value = jnp.concatenate([value, self.chip(value)])
         return jnp.concatenate([value, self.core(value)])
 
-    def rep_gather_now(self, value):
+    def in_turn(self, value, back=False):
         rep = lax.axis_index("rep")
-        value = lax.all_gather(value, "rep")
-        return jnp.concatenate(
-            [lax.dynamic_index_in_dim(value, rep ^ other, 0) for other in (0, 2, 1, 3)]
-        )
+        places = [rep ^ k for k in (0, 2, 1, 3)]
+        if back:
+            places = [(rep ^ k) % 2 * 2 + (rep ^ k) // 2 for k in range(4)]
+        return [lax.dynamic_index_in_dim(value, place, 0, False) for place in places]
+
+    def rep_scatter(self, value):
+        parts = lax.all_to_all(value.astype(BF16), "rep", 0, 0, tiled=True)
+        return jnp.sum(parts.astype(F32), axis=0)
 
     def rep_sum(self, value):
         value = value.astype(BF16)
@@ -663,7 +663,15 @@
             first, second = jnp.split(value, 2, axis)
             return jnp.where(second_core, second, first), jnp.where(second_core, first, second)
 
+        def halves(master):
+            return my_half(master[0].astype(BF16))[0]
+
+        in_rows = D // n_shard
+        in_cols = attn_in_master.shape[2] // 2
+        attn_part = jnp.concatenate([halves(attn_in_master), halves(attn_out_master)], 1)
+
         packed = jnp.stack([token_ids, target_ids, loss_mask])
+        packed, attn_part = lax.optimization_barrier((packed, attn_part))
         everyone = links.spread(lax.all_gather(packed, "rep")).transpose(1, 0, 2, 3)
         everyone = everyone.reshape(LINE, n_rep, wide, 3, tok_rows).transpose(1, 0, 2, 3, 4)
         valid_count = jnp.sum(everyone[:, :, :, 2].astype(F32))
@@ -683,9 +691,6 @@
         pair_weights = pair_mask / valid_count
         place_block = my_rep * wide + links.w
         positions = place_block * tok_rows + jnp.arange(tok_rows, dtype=jnp.int32)
-
-        def halves(master):
-            return my_half(master[0].astype(BF16))[0]
 
         unit_rows = FF // n_shard
         unit_part = unit_rows // n_rep
@@ -695,9 +700,6 @@
         mlp_in_part = lax.dynamic_index_in_dim(mlp_in_part, my_rep, 3, False).reshape(-1, 2 * units)
         mlp_out_part = mlp_out_master[0].astype(BF16).reshape(n_rep, unit_part, D)
         mlp_out_part = lax.dynamic_index_in_dim(mlp_out_part, my_rep, 0, False)
-        in_rows = D // n_shard
-        in_cols = attn_in_master.shape[2] // 2
-        attn_part = jnp.concatenate([halves(attn_in_master), halves(attn_out_master)], 1)
         mlp_part = jnp.concatenate([mlp_in_part, mlp_out_part.reshape(in_rows, -1)], 1)
         attn_mine = lax.all_gather(attn_part, "shard", tiled=True)
 
@@ -772,7 +774,6 @@
         attn_out = (attn_mine[:, in_cols:], attn_other[:, in_cols:])
         mlp_in = mlp_all[:, : 2 * units]
         mlp_out = mlp_all[:, 2 * units :].reshape(n_shard * unit_part, D)
-
         def times(value, pair):
             return dot(value, pair[0]), dot(value, pair[1])
 
@@ -824,11 +825,11 @@
         middle = values + in_order(*times(attended, attn_out))
         normed_two, norm_two_back = jax.vjp(rms_norm, middle, gains[1])
         normed_two = normed_two.astype(BF16)
-        normed_all = links.rep_gather_now(normed_two).reshape(-1, D)
+        normed_all = lax.all_gather(normed_two, "rep", tiled=True)
         gate_up = dot(normed_all, mlp_in)
         hidden, glu_back = jax.vjp(swiglu, gate_up[:, :units], gate_up[:, units:])
         hidden = hidden.astype(BF16)
-        result = middle + links.rep_sum(dot(hidden, mlp_out).reshape(n_rep, tok_rows, D))
+        result = middle + links.rep_scatter(dot(hidden, mlp_out).reshape(n_rep, tok_rows, D))
         final, final_back = jax.vjp(rms_norm, result, gains[2])
 
         near = links.line_gather(final.astype(BF16))
@@ -904,20 +905,21 @@
             value = jnp.pad(value, ((0, 0), (0, 0), (0, pad_rows)))
             return value.reshape(-1, n_shard * (in_rows + pad_rows))
 
-        branch = links.rep_gather_now(grad_output.astype(BF16)).reshape(-1, D)
+        branch = lax.all_gather(grad_output.astype(BF16), "rep", tiled=True)
         grad_mlp_out = dot(hidden, branch, ((0,), (0,))).astype(BF16)
         grad_hidden = dot(branch, mlp_out, ((1,), (1,)))
         grad_glu = jnp.concatenate(glu_back(grad_hidden), 1).astype(BF16)
         grad_mlp_in = dot(pad_blocks(normed_all), grad_glu, ((0,), (0,))).astype(BF16)
         grad_normed_two = dot(grad_glu, mlp_in, ((1,), (1,))).reshape(n_rep, tok_rows, D)
-        grad_normed_two = links.rep_sum(grad_normed_two)
+        turns = links.in_turn(grad_normed_two)
+        sent = links.core(jnp.stack(turns[2:]).astype(BF16)).astype(F32)
+        passed = links.chip((turns[1] + sent[1]).astype(BF16))
+        grad_normed_two = turns[0] + sent[0] + passed.astype(F32)
         middle_part, grad_gain_two = norm_two_back(grad_normed_two)
         grad_middle = grad_output + middle_part
 
-        grad_mlp = [
-            links.scatter(grad_mlp_in)[:in_rows].astype(BF16),
-            grad_mlp_out,
-        ]
+        grad_mlp = [grad_mlp_in, grad_mlp_out.reshape(grad_mlp_in.shape[0], -1)]
+        grad_mlp = lax.psum_scatter(jnp.concatenate(grad_mlp, 1), "shard", tiled=True)
 
         out_mine, out_other = my_half(grad_middle.astype(BF16))
         grad_attn_out = weight_grad(pad_blocks(attended), out_mine, out_other)
@@ -953,21 +955,20 @@
         grad_gains = jnp.stack([grad_gain_one, grad_gain_two, grad_gain_three], 1)
         grad_gains = grad_gains + links.core(grad_gains)
         grad_gains = pad_blocks((grad_gains + links.chip(grad_gains)).T).T
-        grad_values, grad_mlp[0] = lax.optimization_barrier((grad_values, grad_mlp[0]))
         packed = dot(packing, grad_values).astype(BF16).reshape(n_shard, room, D)
         packed = lax.all_to_all(packed, "shard", 0, 0, tiled=True)
-        packed, grad_mlp[1] = lax.optimization_barrier((packed, grad_mlp[1]))
-        grad_mlp[1] = links.scatter(grad_mlp[1]).astype(BF16).reshape(in_rows, -1)
-        rows = packed.reshape(1, n_shard * room, D)
-        rows = jnp.concatenate([rows, links.chip(rows)])
-        rows, grad_mlp[1], normed_one, grad_attn_out = lax.optimization_barrier(
-            (rows, grad_mlp[1], normed_one, grad_attn_out)
-        )
         grad_attn_in = weight_grad(pad_blocks(normed_one), mixed_mine, mixed_other)
-        grad_small = jnp.concatenate([grad_attn_in, grad_gains.astype(BF16)], 1)
-        grad_attn_out = links.scatter(grad_attn_out)[:in_rows].astype(BF16)
-        rows = jnp.concatenate([rows, links.core(rows)])
-        grad_small = links.scatter(grad_small)[:in_rows].astype(BF16)
+        grad_attn = jnp.concatenate([grad_attn_out, grad_attn_in, grad_gains.astype(BF16)], 1)
+        packed, grad_attn = lax.optimization_barrier((packed, grad_attn))
+        packed = packed.reshape(n_shard * room, D)
+        across = links.chip(packed)
+        grad_attn = links.scatter(grad_attn)[:in_rows].astype(BF16)
+        across, grad_mlp = lax.optimization_barrier((across, grad_mlp))
+        grad_mlp_in = grad_mlp[:in_rows, : 2 * units]
+        grad_mlp_out = grad_mlp[:, 2 * units :].reshape(unit_part, D)
+        mlp_in_sum = lax.all_gather(grad_mlp_in, "rep")
+        rows = (packed, across, links.core(packed), links.core(across))
+        rows, mlp_in_sum = lax.optimization_barrier((rows, mlp_in_sum))
         placed = place_rows(kept, received, rows, ranks, sorted_ids, starts, vocab_tile)
 
         def place_whole(placed, grad_values, kept, received):
@@ -979,30 +980,39 @@
             enough, lambda placed, *_: tuple(placed), place_whole, placed, grad_values, kept, received
         )
 
-        parts = [*grad_mlp, grad_attn_out, grad_small[:, :-3]]
-        gain_sum = grad_small[:, -3:].astype(F32).T
+        table_squares, grad_attn = lax.optimization_barrier((table_squares, grad_attn))
+        gain_sum = grad_attn[:, -3:].astype(F32).T
+        grad_attn = grad_attn[:, :-3]
+        table_core = links.core(table_sum)
         squares = jnp.sum(table_squares) + jnp.sum(gain_sum * gain_sum) / n_rep
-        for part in parts:
+        for part in (grad_mlp_in, grad_mlp_out, grad_attn):
             squares = squares + jnp.sum(jnp.square(part.astype(F32)))
-        squares = jnp.sum(lax.all_gather(squares, "rep"))
-        squares = jnp.sum(links.spread(jnp.full((8, 128), squares))[:, 0, 0])
-        grad_norm = jnp.sqrt(squares)
-        clip_scale = CLIP_AT / jnp.maximum(grad_norm, CLIP_AT)
-
-        table_core = links.core(table_sum)
+        totals = jnp.stack([squares, group_loss])
+        totals = totals + links.core(totals)
+        shared = jnp.concatenate([grad_attn, grad_mlp_out.reshape(in_rows, -1)], 1)[None]
+        totals, shared = lax.optimization_barrier((totals, shared))
+        totals = totals + links.chip(totals)
+        shared = jnp.concatenate([shared, links.chip(shared)])
+        totals, table_sum, shared = lax.optimization_barrier((totals, table_sum, shared))
         table_chip = links.chip(table_sum)
-        mlp = lax.all_gather(jnp.concatenate(grad_mlp, 1), "rep")
-        mlp_in_sum = mlp[:, :, : 2 * units].reshape(n_rep, in_rows, 2, n_shard, unit_part)
-        mlp_in_sum = mlp_in_sum.transpose(1, 2, 3, 0, 4).reshape(in_rows, 2 * FF).astype(F32)
-        mlp_out_sum = mlp[:, :, 2 * units :].reshape(n_rep * unit_part, D).astype(F32)
-        attn = lax.all_gather(jnp.concatenate(parts[2:], 1), "rep")[jnp.array([0, 2, 1, 3])]
-        attn = attn.transpose(1, 0, 2).astype(F32)
+        shared = jnp.concatenate([shared, links.core(shared)])
+        shared = jnp.stack(links.in_turn(shared, True))
+        loss_sum = totals[1]
+        squares = links.spread(jnp.broadcast_to(totals[0], (8, 128)))
         out_cols = D // n_rep
+        mlp_in_sum = mlp_in_sum.reshape(n_rep, in_rows, 2, n_shard, unit_part)
+        mlp_in_sum = mlp_in_sum.transpose(1, 2, 3, 0, 4).reshape(in_rows, 2 * FF)
+        attn_cols = out_cols + 2 * in_cols // n_rep
+        attn = jnp.stack([shared[r, :, :attn_cols] for r in (0, 2, 1, 3)], 1)
+        mlp_out_sum = shared[:, :, attn_cols:].reshape(n_rep * unit_part, D)
         attn_out_sum = attn[:, :, :out_cols].reshape(in_rows, D)
         attn_in_sum = attn[:, :, out_cols:].reshape(in_rows, 2 * in_cols)
+        squares, attn_in_sum, attn_out_sum, mlp_in_sum, mlp_out_sum = lax.optimization_barrier(
+            (squares, attn_in_sum, attn_out_sum, mlp_in_sum, mlp_out_sum)
+        )
+        grad_norm = jnp.sqrt(jnp.sum(squares[:, 0, 0]))
+        clip_scale = CLIP_AT / jnp.maximum(grad_norm, CLIP_AT)
         weight_sum = (attn_in_sum, attn_out_sum, mlp_in_sum, mlp_out_sum, gain_sum)
-        loss = group_loss + links.core(group_loss)
-        loss_sum = loss + links.chip(loss)
         results = [loss_sum, valid_count, grad_norm]
         masters = (
             table_master.T,
@@ -1030,17 +1040,18 @@
         )
         rate_list = rates(seq_len)
         table = (masters[0], firsts[0], seconds[0])
-        half = jnp.stack([my_rep, my_rep ^ 1])
         settings = (clip_scale, rate_list[0], vocab_tile)
-        new = list(adam(*table, table_sum, table_core, half, *settings))
+        new = list(adam(*table, (table_sum, table_core), (my_rep, my_rep ^ 1), *settings))
         olds = [
             tuple(part.reshape(-1, part.shape[-1]) for part in member)
             for member in zip(masters[1:], firsts[1:], seconds[1:], weight_sum)
         ]
-        new[0], table_chip = lax.optimization_barrier((new[0], table_chip))
+        olds[0] = (*olds[0][:3], lax.optimization_barrier((olds[0][3], new[0]))[0])
+        news = list(adam_many(olds, clip_scale, rate_list[1:]))
+        news[0], table_chip = lax.optimization_barrier((news[0], table_chip))
         table_both = links.core(table_chip)
-        news = adam_many(olds, clip_scale, rate_list[1:])
-        new = adam(*table, table_chip, table_both, half ^ 2, *settings, new)
+        new = list(adam(*table, (table_chip,), (my_rep ^ 2,), *settings, new))
+        new = adam(*table, (table_both,), (my_rep ^ 3,), *settings, new)
         results.extend(part.T for part in new)
         for index, new in enumerate(news):
             results.append(new.reshape(masters[1 + index // 4].shape))

time: 839 us -> 747 us (0.89)
  blocking collectives: 78.2 us -> 45.8 us
  waiting for transfers between devices: 175 us -> 148 us
  other arithmetic: 94.7 us -> 77.3 us
  starting transfers between devices: 71.8 us -> 61 us
    unnamed x1 -> x0, blocking collectives: 24.4 us -> none
    all_to_all x1, waiting for transfers between devices: 19.4 us -> 0.01 us  [local(): packed = lax.all_to_all(packed, 'shard', 0, 0, tiled=True)]
    all_to_all x4 -> x1, waiting for transfers between devices: 25.8 us -> 11.2 us  [scatter(): parts = lax.all_to_all(value, 'shard', 0, 0, tiled=True)]
    all_to_all x4 -> x1, starting transfers between devices: 18 us -> 5.82 us  [scatter(): parts = lax.all_to_all(value, 'shard', 0, 0, tiled=True)]
    all_to_all x0 -> x1, waiting for transfers between devices: none -> 11.2 us  [rep_scatter(): parts = lax.all_to_all(value.astype(BF16), 'rep', 0, 0, tiled=True)]
    optimization_barrier x2 -> x8, local copies, waits for them, and re-layouts: 6.32 us -> 15.7 us  [the longest x4 9.21 us: local(): rows, mlp_in_sum = lax.optimization_barrier((rows, mlp_in_sum))]
    all_gather x3 -> x2, blocking collectives: 27.1 us -> 19.1 us  [the longest x1 9.66 us: local(): normed_all = lax.all_gather(normed_two, 'rep', tiled=True)]
    unnamed x197 -> x206, local copies, waits for them, and re-layouts: 16 us -> 18.4 us
  transfers between devices with their start and end apart: 44 -> 44, of which waited for: 22 -> 19; matrix products, arithmetic and copies ran while one was open for 24% -> 22% of each run, Pallas kernels for 21% -> 23%
where the time goes in v4:
time: 747 us; the launch traced here: 739 us
  Pallas kernels  199 us (27%)
  waiting for transfers between devices  148 us (20%)
  local copies, waits for them, and re-layouts  118 us (16%)
  other arithmetic  77.3 us (10%)
  matrix products  62.4 us (8%)
  starting transfers between devices  61 us (8%)
  blocking collectives  45.8 us (6%)
  between operations  21.7 us (3%)
    pallas_call x3, Pallas kernels, adam(): pl.pallas_call(functools.partial(adam_kernel, rate=rate, count=count), gr...  62.3 us
    ppermute x13, waiting for transfers between devices, chip(): return lax.ppermute(value, 'rep', [(r, r ^ 2) for r in range(self.n_rep)])  56 us
    dot_general x20, matrix products, dot(): return lax.dot_general(a, b, (dims, ((), ())), preferred_element_type=F32)  40.3 us
    pallas_call x2, Pallas kernels, head_logits(): pl.pallas_call(functools.partial(logits_kernel, tile=tile), grid=(count /...  33.2 us
    pallas_call x2, Pallas kernels, head_table(): pl.pallas_call(table_kernel, grid_spec=pltpu.PrefetchScalarGridSpec(num_s...  30.5 us
    pallas_call x2, Pallas kernels, head_states(): pl.pallas_call(functools.partial(states_kernel, tile=tile), grid=(count /...  27.4 us
    all_to_all x1, waiting for transfers between devices, local(): lax.all_to_all(looked.reshape(n_shard, room, D), 'shard', 0, 0, tiled=True)  22.9 us
    all_gather x1, blocking collectives, line_gather(): lax.all_gather(value, 'shard', axis_index_groups=self.lines, tiled=True)  20.6 us
  transfers between devices with their start and end apart: 44, of which 19 were waited for; matrix products, arithmetic and copies ran while one was open for 22% of the time, Pallas kernels for 23%

profile of v4, /device:TPU:0, one launch (start us, length us, event | category | flops | bytes accessed | tf_op | source)
XLA Modules:
  0.0 739.5 jit_solution(16717795107504810210)
XLA Ops:
  10.7 6.1 all-gather.4
  17.4 6.3 all-to-all-start.1
  33.1 20.0 %shard_map.412 = (bf16[960,6144]{1,0:T(8,128)(2,1)}, bf16[512,960]{1,0:T(8,128)(2,1)}) custom-call(s32[512,1]{1,0:T(8,128)} %broadcast_in_dim_reshape.4.ids_ref, f32[960,6144]{1,0:T(8,128)} %bitcast.321), custom_call_target="tpu_custom_call" | custom-call | flops 6039797760 | bytes 35389440 | tf_op jit(solution)/shard_map/pallas_call | solution.py:120
  60.1 5.8 convert_reduce_fusion.1
  65.9 22.9 %all-to-all-done.2 = bf16[8,64,960]{2,1,0:T(8,128)(2,1)S(1)} async-done(((bf16[8,64,960]{2,1,0:T(8,128)(2,1)}), bf16[8,64,960]{2,1,0:T(8,128)(2,1)S(1)}, u32[]{:S(2)}, u32[]{:S(2)}) %all-to-all-start.2) | async-done | bytes 983072 | tf_op jit(solution)/shard_map/all_to_all | solution.py:739
  89.3 6.7 conditional.2
  116.0 9.0 %collective-permute-done.1 = bf16[5,128,128]{1,2,0:T(8,128)(2,1)S(1)} collective-permute-done((bf16[5,128,128]{1,2,0:T(8,128)(2,1)S(1)}, bf16[5,128,128]{1,2,0:T(8,128)(2,1)S(1)}, u32[]{:S(2)}, u32[]{:S(2)}) %collective-permute-start.1) | collective-permute-done | bytes 163872 | tf_op jit(solution)/shard_map/ppermute | solution.py:557
  126.9 7.3 collective-permute-done.2
  136.2 15.0 %all-gather.14.cloned.1.call-done = bf16[960,1920]{1,0:T(8,128)(2,1)} async-done(((bf16[120,1920]{1,0:T(8,128)(2,1)}), bf16[960,1920]{1,0:T(8,128)(2,1)}) %all-gather.14.cloned.1.call-update) | async-done | bytes 3686416 | tf_op jit(solution)/shard_map/all_gather | solution.py:738
  158.2 7.5 %fusion.157 = (f32[5,384]{1,0:T(8,128)S(1)}, f32[5,384,1024]{2,1,0:T(8,128)}) fusion(pred[384,1024]{1,0:T(8,128)(4,1)} %broadcast_compare_fusion, bf16[5,1024,128]{2,1,0:T(8,128)(2,1)S(1)} %bitcast.337, bf16[5,384,64]{2,1,0:T(8,128)(2,1)} %bitcast.375), kind=kOutput, calls=%fused_computation.366 | convolution fusion | flops 511181824 | bytes 9821696 | tf_op jit(solution)/shard_map/sub | solution.py:811
  178.0 9.7 %all_gather.42 = bf16[512,960]{0,1:T(8,128)(2,1)S(1)} all-gather(bf16[128,960]{0,1:T(8,128)(2,1)S(1)} %multiply_convert_fusion.4), channel_id=1, replica_groups=mesh['rep'=4,'shard'=8] {'rep'}, dimensions={0}, use_global_device_ids=true | all-gather | bytes 1228800 | tf_op jit(solution)/shard_map/all_gather | solution.py:828
  200.0 11.2 %all-to-all-done.4 = bf16[4,128,960]{1,2,0:T(8,128)(2,1)S(1)} async-done(((bf16[4,128,960]{1,2,0:T(8,128)(2,1)}), bf16[4,128,960]{1,2,0:T(8,128)(2,1)S(1)}, u32[]{:S(2)}, u32[]{:S(2)}) %all-to-all-start.4) | async-done | bytes 983072 | tf_op jit(solution)/shard_map/all_to_all | solution.py:604
  211.7 20.6 %all_gather.44 = bf16[512,960]{0,1:T(8,128)(2,1)S(1)} all-gather(bf16[128,960]{0,1:T(8,128)(2,1)S(1)} %multiply_convert_fusion.3), channel_id=1, replica_groups={{0,2,4,6},{1,3,5,7},{8,10,12,14},{9,11,13,15},{16,18,20,22},{17,19,21,2..., dimensions={0}, use_global_device_ids=true | all-gather | bytes 1228800 | tf_op jit(solution)/shard_map/all_gather | solution.py:571
  236.8 16.6 %shard_map.413 = (bf16[512,6144]{1,0:T(8,128)(2,1)}, f32[512,128]{1,0:T(8,128)}) custom-call(bf16[512,960]{1,0:T(8,128)(2,1)} %copy.534.states_ref, s32[512,1]{1,0:T(8,128)} %copy.535.targets_ref, bf16[960,6144]{1,0:T(8,128)(2,1)} %get-tuple-element.174.table_ref), custom_call_target="tpu_custom_call" | custom-call | flops 6039797760 | bytes 18087936 | tf_op jit(solution)/shard_map/pallas_call | solution.py:170
  256.2 16.6 %shard_map.414 = (bf16[512,6144]{1,0:T(8,128)(2,1)}, f32[512,128]{1,0:T(8,128)}) custom-call(bf16[512,960]{1,0:T(8,128)(2,1)} %copy.536.states_ref, s32[512,1]{1,0:T(8,128)} %copy.537.targets_ref, bf16[960,6144]{1,0:T(8,128)(2,1)} %get-tuple-element.174.table_ref), custom_call_target="tpu_custom_call" | custom-call | flops 6039797760 | bytes 18087936 | tf_op jit(solution)/shard_map/pallas_call | solution.py:170
  292.7 13.7 %shard_map.415 = (bf16[512,6144]{1,0:T(8,128)(2,1)}, bf16[512,960]{1,0:T(8,128)(2,1)}) custom-call(bf16[512,6144]{1,0:T(8,128)(2,1)} %get-tuple-element.187.raised_ref, f32[512,2]{1,0:T(8,128)} %copy.543.scales_ref, s32[512,1]{1,0:T(8,128)} %copy.537.targets_ref, bf16[960,6144]{1,0:T(8,128)(2,1)} %get-tuple-element.174.table_ref), custom_call_target="tpu_custom_call" | custom-call | flops 6039797760 | bytes 24379392 | tf_op jit(solution)/shard_map/pallas_call | solution.py:216
  309.9 13.7 %shard_map.416 = (bf16[512,6144]{1,0:T(8,128)(2,1)}, bf16[512,960]{1,0:T(8,128)(2,1)}) custom-call(bf16[512,6144]{1,0:T(8,128)(2,1)} %get-tuple-element.191.raised_ref, f32[512,2]{1,0:T(8,128)} %copy.545.scales_ref, s32[512,1]{1,0:T(8,128)} %copy.535.targets_ref, bf16[960,6144]{1,0:T(8,128)(2,1)} %get-tuple-element.174.table_ref), custom_call_target="tpu_custom_call" | custom-call | flops 6039797760 | bytes 24379392 | tf_op jit(solution)/shard_map/pallas_call | solution.py:216
  326.9 15.6 %shard_map.418 = bf16[960,1536]{1,0:T(8,128)(2,1)} custom-call(s32[1]{0:T(128)} %bitcast.24.part_ref, bf16[960,512]{1,0:T(8,128)(2,1)} %bitcast.335, bf16[960,512]{1,0:T(8,128)(2,1)} %bitcast.343, bf16[960,512]{1,0:T(8,128)(2,1)} %bitcast.345, bf16[960,512]{1,0:T(8,128)(2,1)} %bitcast.60.far_pair_t, bf16[512,6144]{1,0:T(8,128)(2,1)} %get-tuple-element.192.near_grads, ...), custom_call_target="tpu_custom_call" | custom-call | flops 9059696640 | bytes 14942208 | tf_op jit(solution)/shard_map/pallas_call | solution.py:297
  350.8 14.9 %shard_map.417.refs_4_ = bf16[960,1536]{1,0:T(8,128)(2,1)S(1)} custom-call(s32[1]{0:T(128)} %bitcast.13.part_ref, bf16[960,512]{1,0:T(8,128)(2,1)} %bitcast.336, bf16[960,512]{1,0:T(8,128)(2,1)} %bitcast.344, bf16[960,512]{1,0:T(8,128)(2,1)} %bitcast.346, bf16[960,512]{1,0:T(8,128)(2,1)} %bitcast.60.far_pair_t, ...), custom_call_target="tpu_custom_call" | custom-call | flops 9059696640 | bytes 14942208 | tf_op jit(solution)/shard_map/pallas_call | solution.py:297
  365.7 6.2 all-to-all-done.6
  375.9 9.5 %all_gather.45 = bf16[512,960]{0,1:T(8,128)(2,1)S(1)} all-gather(bf16[128,960]{0,1:T(8,128)(2,1)S(1)} %fusion.85), channel_id=1, replica_groups=mesh['rep'=4,'shard'=8] {'rep'}, dimensions={0}, use_global_device_ids=true | all-gather | bytes 1228800 | tf_op jit(solution)/shard_map/all_gather | solution.py:908
  471.5 6.9 collective-permute-done.14
  502.9 18.2 %collective-permute-done.20 = f32[960,3]{0,1:T(4,128)S(1)} collective-permute-done((f32[960,3]{0,1:T(4,128)S(1)}, f32[960,3]{0,1:T(4,128)S(1)}, u32[]{:S(2)}, u32[]{:S(2)}) %collective-permute-start.20) | collective-permute-done | bytes 11552 | tf_op jit(solution)/shard_map/ppermute | solution.py:613
  542.2 14.4 %collective-permute-done.21 = bf16[512,960]{0,1:T(8,128)(2,1)} collective-permute-done((bf16[512,960]{0,1:T(8,128)(2,1)}, bf16[512,960]{0,1:T(8,128)(2,1)}, u32[]{:S(2)}, u32[]{:S(2)}) %collective-permute-start.21) | collective-permute-done | bytes 983072 | tf_op jit(solution)/shard_map/ppermute | solution.py:613
  562.3 11.2 %all-to-all-done.8 = bf16[8,128,643]{1,2,0:T(8,128)(2,1)} async-done(((bf16[8,128,643]{1,2,0:T(8,128)(2,1)}), bf16[8,128,643]{1,2,0:T(8,128)(2,1)}, u32[]{:S(2)}, u32[]{:S(2)}) %all-to-all-start.8) | async-done | bytes 1316896 | tf_op jit(solution)/shard_map/all_to_all | solution.py:581
  587.3 9.8 %shard_map.419 = (bf16[960,1536]{1,0:T(8,128)(2,1)}, f32[1,128]{1,0:T(1,128)S(1)}) custom-call(s32[4]{0:T(128)} %convert_reduce_fusion.5.starts_ref, s32[2048,1]{1,0:T(8,128)} %copy.578.ranks_ref, s32[2048,1]{1,0:T(8,128)} %copy.579.ids_ref, bf16[512,960]{1,0:T(8,128)(2,1)} %bitcast.111.refs_0_, bf16[512,960]{1,0:T(8,128)(2,1)} %copy.580.refs_1_, ...), custom_call_target="tpu_custom_call" | custom-call | flops 503316480 | bytes 12779520 | tf_op jit(solution)/shard_map/pallas_call | solution.py:408
  608.7 7.9 %collective-permute-done.25 = f32[2]{0:T(128)S(1)} collective-permute-done((f32[2]{0:T(128)S(1)}, f32[2]{0:T(128)S(1)}, u32[]{:S(2)}, u32[]{:S(2)}) %collective-permute-start.25) | collective-permute-done | bytes 40 | tf_op jit(solution)/shard_map/ppermute | solution.py:613
  628.7 6.0 all-to-all-start.9
  650.4 28.5 %shard_map.420 = (f32[960,6144]{1,0:T(8,128)}, f32[960,6144]{1,0:T(8,128)}, f32[960,6144]{1,0:T(8,128)}, bf16[960,6144]{1,0:T(8,128)(2,1)}) custom-call(s32[2]{0:T(128)} %pad_add_fusion.3.quarters_ref, f32[1]{0:T(128)} %bitcast.131.scale_ref, f32[960,6144]{1,0:T(8,128)} %bitcast.322, f32[960,6144]{1,0:T(8,128)} %bitcast.325, f32[960,6144]{1,0:T(8,128)} %bitcast.328, ...), custom_call_target="tpu_custom_call" | custom-call | tf_op jit(solution)/shard_map/pallas_call | solution.py:458
  680.0 16.0 %shard_map.421 = (f32[120,1600]{1,0:T(8,128)}, f32[120,1600]{1,0:T(8,128)}, f32[120,1600]{1,0:T(8,128)}, bf16[120,1600]{1,0:T(8,128)(2,1)}, f32[120,960]{1,0:T(8...) custom-call(f32[1]{0:T(128)} %bitcast.131.scale_ref, ...), custom_call_target="tpu_custom_call" | custom-call | tf_op jit(solution)/shard_map/pallas_call | solution.py:516
  696.3 16.9 %shard_map.422 = (f32[960,6144]{1,0:T(8,128)}, f32[960,6144]{1,0:T(8,128)}, f32[960,6144]{1,0:T(8,128)}, bf16[960,6144]{1,0:T(8,128)(2,1)}) custom-call(s32[1]{0:T(128)} %bitcast.23.quarters_ref, f32[1]{0:T(128)} %bitcast.131.scale_ref, f32[960,6144]{1,0:T(8,128)} %bitcast.323, ...), custom_call_target="tpu_custom_call", output_to_operand_aliasing={{0}: (6, {}), {1}: (7, {}), {2}: (8, {}), {3}: (9, {})} | custom-call | tf_op jit(solution)/shard_map/pallas_call | solution.py:458
  714.7 16.9 %shard_map.423 = (f32[960,6144]{1,0:T(8,128)}, f32[960,6144]{1,0:T(8,128)}, f32[960,6144]{1,0:T(8,128)}, bf16[960,6144]{1,0:T(8,128)(2,1)}) custom-call(s32[1]{0:T(128)} %bitcast.25.quarters_ref, f32[1]{0:T(128)} %bitcast.131.scale_ref, f32[960,6144]{1,0:T(8,128)} %bitcast.324, ...), custom_call_target="tpu_custom_call", output_to_operand_aliasing={{0}: (6, {}), {1}: (7, {}), {2}: (8, {}), {3}: (9, {})} | custom-call | tf_op jit(solution)/shard_map/pallas_call | solution.py:458
  (537 shorter events, 312.1 us)
Async XLA Ops:
  7.2 99.5 %all-gather.12.cloned.1.call-start = ((), (), s32[]{:S(2)}) async-start(), calls=%async_computation.12 | async-start | bytes 2764800 | tf_op jit(solution)/shard_map/all_gather | solution.py:704
  17.4 13.8 %all-to-all-start.1 = ((s32[8,4,3,128]{3,1,2,0:T(4,128)}), s32[8,4,3,128]{3,1,2,0:T(4,128)S(1)}, u32[]{:S(2)}, u32[]{:S(2)}) async-start(s32[8,4,3,128]{3,1,2,0:T(4,128)} %broadcast_in_dim.71), calls=%async_computation.1 | async-start | bytes 98304 | tf_op jit(solution)/shard_map/all_to_all | solution.py:586
  53.2 35.6 %all-to-all-start.2 = ((bf16[8,64,960]{2,1,0:T(8,128)(2,1)}), bf16[8,64,960]{2,1,0:T(8,128)(2,1)S(1)}, u32[]{:S(2)}, u32[]{:S(2)}) async-start(bf16[8,64,960]{2,1,0:T(8,128)(2,1)} %bitcast.393), calls=%async_computation.2 | async-start | bytes 2097152 | tf_op jit(solution)/shard_map/all_to_all | solution.py:739
  56.7 94.4 %all-gather.14.cloned.1.call-start = ((), (), s32[]{:S(2)}) async-start(), calls=%async_computation.13 | async-start | bytes 4147200 | tf_op jit(solution)/shard_map/all_gather | solution.py:738
  135.1 21.0 %collective-permute-start.3 = (bf16[2,2,5,128,128]{3,4,2,1,0:T(8,128)(2,1)}, bf16[2,2,5,128,128]{3,4,2,1,0:T(8,128)(2,1)}, u32[]{:S(2)}, u32[]{:S(2)}) collective-permute-start(bf16[2,2,5,128,128]{3,4,2,1,0:T(8,128)(2,1)} %pad_maximum_fusion.8), channel_id=1, source_target_pairs={{0,8},{8,0},{16,24},{24,16},{1,9},{9,1},{17,25},{25,17},{2,10},{10... | collective-permute-start | bytes 1966088 | tf_op jit(solution)/shard_map/ppermute | solution.py:589
  194.0 17.2 %all-to-all-start.4 = ((bf16[4,128,960]{1,2,0:T(8,128)(2,1)}), bf16[4,128,960]{1,2,0:T(8,128)(2,1)S(1)}, u32[]{:S(2)}, u32[]{:S(2)}) async-start(bf16[4,128,960]{1,2,0:T(8,128)(2,1)} %convolution_convert_fusion.5), calls=%async_computation.4 | async-start | bytes 1966080 | tf_op jit(solution)/shard_map/all_to_all | solution.py:604
  232.3 22.5 %collective-permute-start.4 = (bf16[512,960]{0,1:T(8,128)(2,1)S(1)}, bf16[512,960]{0,1:T(8,128)(2,1)S(1)}, u32[]{:S(2)}, u32[]{:S(2)}) collective-permute-start(bf16[512,960]{0,1:T(8,128)(2,1)S(1)} %all_gather.44), channel_id=1, source_target_pairs={{0,1},{1,0},{2,3},{3,2},{4,5},{5,4},{6,7},{7,6},{8,9},{9,8},{10,11... | collective-permute-start | bytes 2949128 | tf_op jit(solution)/shard_map/ppermute | solution.py:557
  234.8 51.7 %collective-permute-start.5 = (bf16[512,960]{0,1:T(8,128)(2,1)S(1)}, bf16[512,960]{0,1:T(8,128)(2,1)S(1)}, u32[]{:S(2)}, u32[]{:S(2)}) collective-permute-start(bf16[512,960]{0,1:T(8,128)(2,1)S(1)} %all_gather.44), channel_id=1, source_target_pairs={{0,16},{8,24},{16,0},{24,8},{1,17},{9,25},{17,1},{25,9},{2,18},{10... | collective-permute-start | bytes 2949128 | tf_op jit(solution)/shard_map/ppermute | solution.py:613
  285.6 39.0 %collective-permute-start.6 = (bf16[512,960]{0,1:T(8,128)(2,1)S(1)}, bf16[512,960]{0,1:T(8,128)(2,1)}, u32[]{:S(2)}, u32[]{:S(2)}) collective-permute-start(bf16[512,960]{0,1:T(8,128)(2,1)S(1)} %collective-permute-done.4), channel_id=1, source_target_pairs={{0,16},{8,24},{16,0},{24,8},{1,17},{9,25},{17,1},{25,9},{2,18},{10... | collective-permute-start | bytes 2949128 | tf_op jit(solution)/shard_map/ppermute | solution.py:613
  289.8 33.8 %collective-permute-start.7 = (f32[1024]{0:T(1024)S(1)}, f32[1024]{0:T(1024)S(1)}, u32[]{:S(2)}, u32[]{:S(2)}) collective-permute-start(f32[1024]{0:T(1024)S(1)} %bitcast.452), channel_id=1, source_target_pairs={{0,16},{8,24},{16,0},{24,8},{1,17},{9,25},{17,1},{25,9},{2,18},{10... | collective-permute-start | bytes 12296 | tf_op jit(solution)/shard_map/ppermute | solution.py:613
  307.9 34.6 %collective-permute-start.8 = (bf16[512,960]{0,1:T(8,128)(2,1)S(1)}, bf16[512,960]{0,1:T(8,128)(2,1)S(1)}, u32[]{:S(2)}, u32[]{:S(2)}) collective-permute-start(bf16[512,960]{0,1:T(8,128)(2,1)S(1)} %copy.559), channel_id=1, source_target_pairs={{0,1},{1,0},{2,3},{3,2},{4,5},{5,4},{6,7},{7,6},{8,9},{9,8},{10,11... | collective-permute-start | bytes 2949128 | tf_op jit(solution)/shard_map/ppermute | solution.py:557
  346.0 25.9 %all-to-all-start.6 = ((bf16[4,128,960]{1,2,0:T(8,128)(2,1)}), bf16[4,128,960]{1,2,0:T(8,128)(2,1)}, u32[]{:S(2)}, u32[]{:S(2)}) async-start(bf16[4,128,960]{1,2,0:T(8,128)(2,1)} %copy.561), calls=%async_computation.6 | async-start | bytes 1966080 | tf_op jit(solution)/shard_map/all_to_all | solution.py:574
  350.6 206.1 %reduce-scatter.2.cloned.1.call-start = ((), (), s32[]{:S(2)}) async-start(), calls=%async_computation.14 | async-start | bytes 4423680 | tf_op jit(solution)/shard_map/reduce_scatter | solution.py:922
  434.2 20.5 %collective-permute-start.12 = (bf16[2,2,5,128,128]{3,4,2,1,0:T(8,128)(2,1)}, bf16[2,2,5,128,128]{3,4,2,1,0:T(8,128)(2,1)}, u32[]{:S(2)}, u32[]{:S(2)}) collective-permute-start(bf16[2,2,5,128,128]{3,4,2,1,0:T(8,128)(2,1)} %slice.289), channel_id=1, source_target_pairs={{0,8},{8,0},{16,24},{24,16},{1,9},{9,1},{17,25},{25,17},{2,10},{10... | collective-permute-start | bytes 1966088 | tf_op jit(solution)/shard_map/ppermute | solution.py:589
  454.2 15.7 %collective-permute-start.15 = (bf16[1024,480]{0,1:T(8,128)(2,1)}, bf16[1024,480]{0,1:T(8,128)(2,1)}, u32[]{:S(2)}, u32[]{:S(2)}) collective-permute-start(bf16[1024,480]{0,1:T(8,128)(2,1)} %convolution_convert_fusion.3), channel_id=1, source_target_pairs={{0,8},{8,0},{16,24},{24,16},{1,9},{9,1},{17,25},{25,17},{2,10},{10... | collective-permute-start | bytes 2949128 | tf_op jit(solution)/shard_map/ppermute | solution.py:589
  480.5 14.7 %collective-permute-start.17 = (bf16[1024,800]{0,1:T(8,128)(2,1)}, bf16[1024,800]{0,1:T(8,128)(2,1)}, u32[]{:S(2)}, u32[]{:S(2)}) collective-permute-start(bf16[1024,800]{0,1:T(8,128)(2,1)} %convolution_convert_fusion.1), channel_id=1, source_target_pairs={{0,8},{8,0},{16,24},{24,16},{1,9},{9,1},{17,25},{25,17},{2,10},{10... | collective-permute-start | bytes 4915208 | tf_op jit(solution)/shard_map/ppermute | solution.py:589
  481.4 40.6 %collective-permute-start.16 = (bf16[1024,240]{0,1:T(8,128)(2,1)}, bf16[1024,240]{0,1:T(8,128)(2,1)}, u32[]{:S(2)}, u32[]{:S(2)}) collective-permute-start(bf16[1024,240]{0,1:T(8,128)(2,1)} %select_convert_fusion.1), channel_id=1, source_target_pairs={{0,16},{8,24},{16,0},{24,8},{1,17},{9,25},{17,1},{25,9},{2,18},{10... | collective-permute-start | bytes 1474568 | tf_op jit(solution)/shard_map/ppermute | solution.py:613
  486.1 14.7 %collective-permute-start.19 = (f32[960,3]{0,1:T(4,128)}, f32[960,3]{0,1:T(4,128)}, u32[]{:S(2)}, u32[]{:S(2)}) collective-permute-start(f32[960,3]{0,1:T(4,128)} %pad_maximum_fusion.19), channel_id=1, source_target_pairs={{0,8},{8,0},{16,24},{24,16},{1,9},{9,1},{17,25},{25,17},{2,10},{10... | collective-permute-start | bytes 34568 | tf_op jit(solution)/shard_map/ppermute | solution.py:589
  491.0 37.0 %all-to-all-start.7 = ((bf16[8,64,960]{2,1,0:T(8,128)(2,1)}), bf16[8,64,960]{2,1,0:T(8,128)(2,1)}, u32[]{:S(2)}, u32[]{:S(2)}) async-start(bf16[8,64,960]{2,1,0:T(8,128)(2,1)} %bitcast.357), calls=%async_computation.7 | async-start | bytes 2097152 | tf_op jit(solution)/shard_map/all_to_all | solution.py:959
  500.0 24.1 %collective-permute-start.18 = (bf16[1024,400]{0,1:T(8,128)(2,1)}, bf16[1024,400]{0,1:T(8,128)(2,1)}, u32[]{:S(2)}, u32[]{:S(2)}) collective-permute-start(bf16[1024,400]{0,1:T(8,128)(2,1)} %select_convert_fusion), channel_id=1, source_target_pairs={{0,16},{8,24},{16,0},{24,8},{1,17},{9,25},{17,1},{25,9},{2,18},{10... | collective-permute-start | bytes 2457608 | tf_op jit(solution)/shard_map/ppermute | solution.py:613
  501.6 19.5 %collective-permute-start.20 = (f32[960,3]{0,1:T(4,128)S(1)}, f32[960,3]{0,1:T(4,128)S(1)}, u32[]{:S(2)}, u32[]{:S(2)}) collective-permute-start(f32[960,3]{0,1:T(4,128)S(1)} %fusion.144), channel_id=1, source_target_pairs={{0,16},{8,24},{16,0},{24,8},{1,17},{9,25},{17,1},{25,9},{2,18},{10... | collective-permute-start | bytes 34568 | tf_op jit(solution)/shard_map/ppermute | solution.py:613
  502.9 59.4 %collective-permute-start.9 = (bf16[960,1536]{1,0:T(8,128)(2,1)}, bf16[960,1536]{1,0:T(8,128)(2,1)}, u32[]{:S(2)}, u32[]{:S(2)}) collective-permute-start(bf16[960,1536]{1,0:T(8,128)(2,1)} %shard_map.418), channel_id=1, source_target_pairs={{0,8},{8,0},{16,24},{24,16},{1,9},{9,1},{17,25},{25,17},{2,10},{10... | collective-permute-start | bytes 8847368 | tf_op jit(solution)/shard_map/ppermute | solution.py:589
  532.9 23.7 %collective-permute-start.21 = (bf16[512,960]{0,1:T(8,128)(2,1)}, bf16[512,960]{0,1:T(8,128)(2,1)}, u32[]{:S(2)}, u32[]{:S(2)}) collective-permute-start(bf16[512,960]{0,1:T(8,128)(2,1)} %copy.575), channel_id=1, source_target_pairs={{0,16},{8,24},{16,0},{24,8},{1,17},{9,25},{17,1},{25,9},{2,18},{10... | collective-permute-start | bytes 2949128 | tf_op jit(solution)/shard_map/ppermute | solution.py:613
  536.4 37.1 %all-to-all-start.8 = ((bf16[8,128,643]{1,2,0:T(8,128)(2,1)}), bf16[8,128,643]{1,2,0:T(8,128)(2,1)}, u32[]{:S(2)}, u32[]{:S(2)}) async-start(bf16[8,128,643]{1,2,0:T(8,128)(2,1)} %copy.584), calls=%async_computation.9 | async-start | bytes 2654208 | tf_op jit(solution)/shard_map/all_to_all | solution.py:581
  542.2 38.3 %all-gather.16.cloned.1.call-start = ((), (), s32[]{:S(2)}) async-start(), calls=%async_computation.15 | async-start | bytes 1536000 | tf_op jit(solution)/shard_map/all_gather | solution.py:969
  558.4 22.1 %collective-permute-start.22 = (bf16[512,960]{0,1:T(8,128)(2,1)}, bf16[512,960]{0,1:T(8,128)(2,1)}, u32[]{:S(2)}, u32[]{:S(2)}) collective-permute-start(bf16[512,960]{0,1:T(8,128)(2,1)} %copy.575), channel_id=1, source_target_pairs={{0,8},{8,0},{16,24},{24,16},{1,9},{9,1},{17,25},{25,17},{2,10},{10... | collective-permute-start | bytes 2949128 | tf_op jit(solution)/shard_map/ppermute | solution.py:589
  558.5 22.0 %collective-permute-start.23 = (bf16[512,960]{0,1:T(8,128)(2,1)}, bf16[512,960]{0,1:T(8,128)(2,1)}, u32[]{:S(2)}, u32[]{:S(2)}) collective-permute-start(bf16[512,960]{0,1:T(8,128)(2,1)} %collective-permute-done.21), channel_id=1, source_target_pairs={{0,8},{8,0},{16,24},{24,16},{1,9},{9,1},{17,25},{25,17},{2,10},{10... | collective-permute-start | bytes 2949128 | tf_op jit(solution)/shard_map/ppermute | solution.py:589
  607.7 42.7 %collective-permute-start.28 = (bf16[960,1536]{1,0:T(8,128)(2,1)S(1)}, bf16[960,1536]{1,0:T(8,128)(2,1)}, u32[]{:S(2)}, u32[]{:S(2)}) collective-permute-start(bf16[960,1536]{1,0:T(8,128)(2,1)S(1)} %get-tuple-element.220.refs_0_), channel_id=1, source_target_pairs={{0,8},{8,0},{16,24},{24,16},{1,9},{9,1},{17,25},{25,17},{2,10},{10... | collective-permute-start | bytes 8847368 | tf_op jit(solution)/shard_map/ppermute | solution.py:589
  617.6 78.4 %collective-permute-start.29 = (bf16[960,1536]{1,0:T(8,128)(2,1)S(1)}, bf16[960,1536]{1,0:T(8,128)(2,1)}, u32[]{:S(2)}, u32[]{:S(2)}) collective-permute-start(bf16[960,1536]{1,0:T(8,128)(2,1)S(1)} %get-tuple-element.220.refs_0_), channel_id=1, source_target_pairs={{0,16},{8,24},{16,0},{24,8},{1,17},{9,25},{17,1},{25,9},{2,18},{10... | collective-permute-start | bytes 8847368 | tf_op jit(solution)/shard_map/ppermute | solution.py:613
  620.7 13.9 %collective-permute-start.27 = (bf16[2,120,1280]{2,1,0:T(8,128)(2,1)}, bf16[2,120,1280]{2,1,0:T(8,128)(2,1)}, u32[]{:S(2)}, u32[]{:S(2)}) collective-permute-start(bf16[2,120,1280]{2,1,0:T(8,128)(2,1)} %copy.587), channel_id=1, source_target_pairs={{0,8},{8,0},{16,24},{24,16},{1,9},{9,1},{17,25},{25,17},{2,10},{10... | collective-permute-start | bytes 1843208 | tf_op jit(solution)/shard_map/ppermute | solution.py:589
  628.7 17.1 %all-to-all-start.9 = ((f32[8,8,128]{2,1,0:T(8,128)}), f32[8,8,128]{2,1,0:T(8,128)S(1)}, u32[]{:S(2)}, u32[]{:S(2)}) async-start(f32[8,8,128]{2,1,0:T(8,128)} %broadcast_in_dim_broadcast_in_dim_broadcast_in_dim.3), calls=%async_computation.10 | async-start | bytes 65536 | tf_op jit(solution)/shard_map/all_to_all | solution.py:586
  696.0 17.2 %collective-permute-start.30 = (bf16[960,1536]{1,0:T(8,128)(2,1)}, bf16[960,1536]{1,0:T(8,128)(2,1)S(1)}, u32[]{:S(2)}, u32[]{:S(2)}) collective-permute-start(bf16[960,1536]{1,0:T(8,128)(2,1)} %collective-permute-done.29.refs_0_), channel_id=1, source_target_pairs={{0,8},{8,0},{16,24},{24,16},{1,9},{9,1},{17,25},{25,17},{2,10},{10... | collective-permute-start | bytes 8847368 | tf_op jit(solution)/shard_map/ppermute | solution.py:589
  (115 other events, 1347.8 us)
Sparse Core Ops, SparseCore 0:
  10.8 63.3 all-gather.11
  77.0 74.1 all-gather.13
  448.9 92.9 reduce-scatter.1
  558.5 17.7 all-gather.15

commit v5 on v4

--- a/solution.py
+++ b/solution.py
@@ -140,50 +140,81 @@
     )(local_ids[:, None], table_t)
 
 
-def logits_kernel(states_ref, targets_ref, table_ref, raised_ref, stats_ref, logits, *, tile):
-    vocab = table_ref.shape[1]
-    rows = states_ref.shape[0]
-    states = states_ref[...]
-    high = jnp.full((rows, 1), -jnp.inf, F32)
-    for start in range(0, vocab, tile):
-        part = dot(states, table_ref[:, start : start + tile])
-        logits[:, start : start + tile] = part
-        high = jnp.maximum(high, jnp.max(part, axis=-1, keepdims=True))
-    total = jnp.zeros((rows, 128), F32)
-    picked = jnp.zeros((rows, 128), F32)
-    targets = targets_ref[...]
+def logits_kernel(
+    states_ref,
+    targets_ref,
+    table_ref,
+    raised_ref,
+    highs_ref,
+    stats_ref,
+    high,
+    total,
+    picked,
+    *,
+    block,
+):
+    tile = table_ref.shape[1]
+    step = pl.program_id(0)
     lanes = lax.broadcasted_iota(jnp.int32, (1, 128), 1)
-    for start in range(0, vocab, 128):
-        part = logits[:, start : start + 128]
-        raised = jnp.exp(part - high)
-        raised_ref[:, start : start + 128] = raised.astype(BF16)
-        total += raised
-        picked += jnp.where(targets == lanes + start, part, 0.0)
-    total = jnp.sum(total, axis=-1, keepdims=True)
-    picked = jnp.sum(picked, axis=-1, keepdims=True)
-    stats_ref[...] = jnp.where(lanes == 0, high, jnp.where(lanes == 1, total, picked))
-
-
-def head_logits(states, targets, table_low, rows=256, tile=512):
+
+    @pl.when(step == 0)
+    def _():
+        high[...] = jnp.full(high.shape, -jnp.inf, F32)
+        total[...] = jnp.zeros(total.shape, F32)
+        picked[...] = jnp.zeros(picked.shape, F32)
+        highs_ref[...] = jnp.zeros(highs_ref.shape, F32)
+
+    for start in range(0, states_ref.shape[0], block):
+        rows = pl.ds(start, block)
+        part = dot(states_ref[rows, :], table_ref[...])
+        most = part[:, :128]
+        for k in range(128, tile, 128):
+            most = jnp.maximum(most, part[:, k : k + 128])
+        old = high[rows, :]
+        new = jnp.maximum(old, jnp.max(most, axis=-1, keepdims=True))
+        high[rows, :] = new
+        highs_ref[rows, :] = jnp.where(lanes == step, new, highs_ref[rows, :])
+        targets = targets_ref[rows, :] - step * tile
+        sums = total[rows, :] * jnp.exp(old - new)
+        found = picked[rows, :]
+        for k in range(0, tile, 128):
+            logits = part[:, k : k + 128]
+            raised = jnp.exp(logits - new)
+            raised_ref[rows, k : k + 128] = raised.astype(BF16)
+            sums += raised
+            found += jnp.where(targets == lanes + k, logits, 0.0)
+        total[rows, :] = sums
+        picked[rows, :] = found
+
+    @pl.when(step == pl.num_programs(0) - 1)
+    def _():
+        sums = jnp.sum(total[...], axis=-1, keepdims=True)
+        found = jnp.sum(picked[...], axis=-1, keepdims=True)
+        stats_ref[...] = jnp.where(lanes == 0, high[...], jnp.where(lanes == 1, sums, found))
+
+
+def head_logits(states, targets, table_low, tile, block=256):
     count, width = states.shape
     vocab = table_low.shape[1]
     return pl.pallas_call(
-        functools.partial(logits_kernel, tile=tile),
-        grid=(count // rows,),
+        functools.partial(logits_kernel, block=block),
+        grid=(vocab // tile,),
         in_specs=[
-            pl.BlockSpec((rows, width), lambda i: (i, 0)),
-            pl.BlockSpec((rows, 1), lambda i: (i, 0)),
-            whole((width, vocab)),
+            whole((count, width)),
+            whole((count, 1)),
+            pl.BlockSpec((width, tile), lambda i: (0, i)),
         ],
         out_specs=[
-            pl.BlockSpec((rows, vocab), lambda i: (i, 0)),
-            pl.BlockSpec((rows, 128), lambda i: (i, 0)),
+            pl.BlockSpec((count, tile), lambda i: (0, i)),
+            whole((count, 128)),
+            whole((count, 128)),
         ],
         out_shape=[
             jax.ShapeDtypeStruct((count, vocab), BF16),
             jax.ShapeDtypeStruct((count, 128), F32),
+            jax.ShapeDtypeStruct((count, 128), F32),
         ],
-        scratch_shapes=[pltpu.VMEM((rows, vocab), F32)],
+        scratch_shapes=[pltpu.VMEM((count, 128), F32)] * 3,
         compiler_params=params(),
         cost_estimate=pl.CostEstimate(
             flops=2 * count * width * vocab,
@@ -193,42 +224,46 @@
     )(states, targets[:, None], table_low)
 
 
-def states_kernel(raised_ref, scales_ref, targets_ref, table_ref, grads_ref, out_ref, *, tile):
-    vocab = table_ref.shape[1]
-    weight = scales_ref[:, 1:2]
-    factor = scales_ref[:, 0:1]
+def states_kernel(
+    raised_ref, factors_ref, weights_ref, targets_ref, table_ref, grads_ref, out_ref, *, tile, each
+):
+    width, vocab = table_ref.shape
+    weight = weights_ref[...]
     targets = targets_ref[...]
     total = None
     for start in range(0, vocab, tile):
         lanes = lax.broadcasted_iota(jnp.int32, (1, tile), 1) + start
+        factor = factors_ref[:, start // each : start // each + 1]
         chances = raised_ref[:, start : start + tile].astype(F32) * factor
         part = (jnp.where(targets == lanes, chances - weight, chances)).astype(BF16)
         grads_ref[:, start : start + tile] = part
         found = dot(part, table_ref[:, start : start + tile], ((1,), (1,)))
         total = found if total is None else total + found
-    out_ref[...] = total.astype(BF16)
-
-
-def head_states(raised, factors, weights, targets, table_low, rows=256, tile=512):
+    out_ref[:, :width] = total.astype(BF16)
+    out_ref[:, width:] = jnp.zeros((out_ref.shape[0], out_ref.shape[1] - width), BF16)
+
+
+def head_states(raised, factors, weights, targets, table_low, each, rows=256, tile=512):
     count, vocab = raised.shape
     width = table_low.shape[0]
-    scales = jnp.stack([factors * weights, weights], axis=1)
+    padded = width + -width % 128
     return pl.pallas_call(
-        functools.partial(states_kernel, tile=tile),
+        functools.partial(states_kernel, tile=tile, each=each),
         grid=(count // rows,),
         in_specs=[
             pl.BlockSpec((rows, vocab), lambda i: (i, 0)),
-            pl.BlockSpec((rows, 2), lambda i: (i, 0)),
+            pl.BlockSpec((rows, 128), lambda i: (i, 0)),
+            pl.BlockSpec((rows, 1), lambda i: (i, 0)),
             pl.BlockSpec((rows, 1), lambda i: (i, 0)),
             whole((width, vocab)),
         ],
         out_specs=[
             pl.BlockSpec((rows, vocab), lambda i: (i, 0)),
-            pl.BlockSpec((rows, width), lambda i: (i, 0)),
+            pl.BlockSpec((rows, padded), lambda i: (i, 0)),
         ],
         out_shape=[
             jax.ShapeDtypeStruct((count, vocab), BF16),
-            jax.ShapeDtypeStruct((count, width), BF16),
+            jax.ShapeDtypeStruct((count, padded), BF16),
         ],
         compiler_params=params(),
         cost_estimate=pl.CostEstimate(
@@ -236,7 +271,7 @@
             bytes_accessed=2 * vocab * (width + 2 * count),
             transcendentals=0,
         ),
-    )(raised, scales, targets[:, None], table_low)
+    )(raised, factors, weights[:, None], targets[:, None], table_low)
 
 
 def table_kernel(
@@ -337,6 +372,76 @@
     )
 
 
+def attend_kernel(queries_ref, kv_ref, bias_ref, out_ref):
+    queries = queries_ref[0]
+    kv = kv_ref[:, 0].reshape(-1, queries.shape[1])
+    scores = dot(queries, kv, ((1,), (1,))) * HEAD_DIM ** (-0.5) + bias_ref[...]
+    highest = jnp.max(scores, axis=-1, keepdims=True)
+    weights = jnp.exp(scores - highest)
+    totals = jnp.sum(weights, axis=-1, keepdims=True)
+    output = dot((weights / totals).astype(BF16), kv)
+    lanes = lax.broadcasted_iota(jnp.int32, output.shape, 1)
+    out_ref[0] = jnp.where(lanes < HEAD_DIM, highest + jnp.log(totals), output)
+
+
+def attend_back_kernel(queries_ref, kv_ref, bias_ref, out_ref, grads_ref, grad_rows_ref, grad_kv_ref):
+    queries, output, grads = queries_ref[0], out_ref[0], grads_ref[0]
+    kv = kv_ref[:, 0].reshape(-1, queries.shape[1])
+    scale = HEAD_DIM ** (-0.5)
+    scores = dot(queries, kv, ((1,), (1,))) * scale + bias_ref[...]
+    chances = jnp.exp(scores - output[:, :1])
+    delta = jnp.sum(grads.astype(F32) * output, axis=-1, keepdims=True)
+    grad_scores = (chances * (dot(grads, kv, ((1,), (1,))) - delta)).astype(BF16)
+    grad_rows_ref[0] = dot(grad_scores, kv) * scale
+    grad_kv = dot(grad_scores, queries, ((0,), (0,))) * scale
+    grad_kv = grad_kv + dot(chances.astype(BF16), grads, ((0,), (0,)))
+    grad_kv_ref[:, 0] = grad_kv.astype(BF16).reshape(grad_kv_ref[:, 0].shape)
+
+
+def attend_specs(queries, kv):
+    heads, rows, lanes = queries.shape
+    blocks, _, block, _ = kv.shape
+    return (
+        pl.BlockSpec((1, rows, lanes), lambda h: (h, 0, 0)),
+        pl.BlockSpec((blocks, 1, block, lanes), lambda h: (0, h, 0, 0)),
+        whole((1, blocks * block)),
+        pl.CostEstimate(
+            flops=4 * heads * rows * blocks * block * lanes,
+            bytes_accessed=4 * heads * blocks * block * lanes,
+            transcendentals=heads * rows * blocks * block,
+        ),
+    )
+
+
+def attend(queries, kv, bias):
+    rows, pairs, one, cost = attend_specs(queries, kv)
+    return pl.pallas_call(
+        attend_kernel,
+        grid=(queries.shape[0],),
+        in_specs=[rows, pairs, one],
+        out_specs=rows,
+        out_shape=jax.ShapeDtypeStruct(queries.shape, F32),
+        compiler_params=params(),
+        cost_estimate=cost,
+    )(queries, kv, bias)
+
+
+def attend_back(queries, kv, bias, output, grads):
+    rows, pairs, one, cost = attend_specs(queries, kv)
+    return pl.pallas_call(
+        attend_back_kernel,
+        grid=(queries.shape[0],),
+        in_specs=[rows, pairs, one, rows, rows],
+        out_specs=[rows, pairs],
+        out_shape=[
+            jax.ShapeDtypeStruct(queries.shape, F32),
+            jax.ShapeDtypeStruct(kv.shape, BF16),
+        ],
+        compiler_params=params(),
+        cost_estimate=cost,
+    )(queries, kv, bias, output, grads)
+
+
 def place_kernel(
     starts_ref,
     ranks_ref,
@@ -360,7 +465,7 @@
             for source, rows_ref in enumerate(rows_refs):
                 pick = ranks_ref[source * lanes : (source + 1) * lanes, :] == wanted
                 pick = jnp.where(pick, 1.0, 0.0).astype(BF16)
-                part = dot(rows_ref[...], pick, ((0,), (0,)))
+                part = dot(rows_ref[...], pick, ((0,), (0,)))[: sorted_rows.shape[0]]
                 found = part if found is None else found + part
             sorted_rows[:, columns] = found.astype(BF16)
             return carry
@@ -401,7 +506,7 @@
 
 def place_rows(kept, received, rows, ranks, ids, starts, tile, chunk=128, block=256):
     width, columns = kept.shape
-    lanes = rows[0].shape[0]
+    lanes, padded = rows[0].shape
     total = len(rows) * lanes
     block = min(block, total)
     spec = pl.BlockSpec((width, tile), lambda i, starts: (0, i))
@@ -411,7 +516,7 @@
             num_scalar_prefetch=1,
             grid=(columns // tile,),
             in_specs=[whole((total, 1)), whole((total, 1))]
-            + [whole((lanes, width))] * len(rows)
+            + [whole((lanes, padded))] * len(rows)
             + [spec] * 2,
             out_specs=[spec, whole((1, 128))],
             scratch_shapes=[pltpu.VMEM((width, total), BF16), pltpu.VMEM((width, tile), F32)],
@@ -793,26 +898,14 @@
         vals = mixed[:, QUERY + KEY :].astype(BF16).reshape(tok_rows, KV_HEADS, HEAD_DIM)
         kv = jnp.concatenate([rotated[:, HEADS:], vals], 2).transpose(1, 0, 2)
         kv = links.rep_gather(jnp.concatenate([kv[None], links.all_across(kv)]))
-        kv = kv.transpose(2, 0, 1, 3, 4).reshape(KV_HEADS, seq_len, 2 * HEAD_DIM)
-        scale = HEAD_DIM ** (-0.5)
+        kv = kv.reshape(n_rep * wide, KV_HEADS, tok_rows, 2 * HEAD_DIM)
         key_places = (
             (jnp.stack([my_rep ^ other for other in (0, 2, 1, 3)]) * wide)[:, None, None]
             + ((links.w - jnp.arange(wide, dtype=jnp.int32)) % wide)[None, :, None]
         ) * tok_rows + jnp.arange(tok_rows, dtype=jnp.int32)
         key_blocks = key_places.reshape(-1) // BLOCK
-        query_blocks = jnp.tile(positions // BLOCK, group_size)
-        allowed = (key_blocks[None, :] <= query_blocks[:, None])[None]
-
-        def batched(spec, a, b):
-            return jnp.einsum(spec, a, b, preferred_element_type=F32)
-
-        scores = jnp.where(allowed, batched("htd,hsd->hts", queries, kv) * scale, -1e30)
-        highest = jnp.max(scores, axis=-1, keepdims=True)
-        weights = jnp.exp(scores - highest)
-        totals = jnp.sum(weights, axis=-1, keepdims=True)
-        chances = weights / totals
-        chances_low = chances.astype(BF16)
-        outputs = batched("hts,hsd->htd", chances_low, kv)[:, :, HEAD_DIM:]
+        bias = jnp.where(key_blocks <= positions[0] // BLOCK, 0.0, -1e30).astype(F32)[None]
+        outputs = attend(queries, kv, bias)
 
         def to_rows(heads):
             return (
@@ -821,7 +914,7 @@
                 .reshape(tok_rows, QUERY)
             )
 
-        attended = to_rows(outputs).astype(BF16)
+        attended = to_rows(outputs[:, :, HEAD_DIM:].astype(BF16))
         middle = values + in_order(*times(attended, attn_out))
         normed_two, norm_two_back = jax.vjp(rms_norm, middle, gains[1])
         normed_two = normed_two.astype(BF16)
@@ -837,11 +930,13 @@
         near_targets, far_targets = group_targets[:line_rows], group_targets[line_rows:]
         pair_near = links.chip(near)
         pair_far = links.chip(far)
-        near_raised, near_stats = head_logits(near, near_targets, table_low)
+        head_tile = 1024 if vocab_rows % 1024 == 0 else 512
+        near_raised, near_highs, near_stats = head_logits(
+            near, near_targets, table_low, head_tile
+        )
         far, near_stats = lax.optimization_barrier((far, near_stats))
-        far_raised, far_stats = head_logits(far, far_targets, table_low)
+        far_raised, far_highs, far_stats = head_logits(far, far_targets, table_low, head_tile)
         stats = jnp.concatenate([near_stats, far_stats])[:, :3].T
-        high = stats[0]
         stats = stats.reshape(3, wide, LINE, tok_rows)
         ordered = jnp.stack(
             [lax.dynamic_index_in_dim(stats, turn[step], 1, False) for step in range(wide)], 1
@@ -860,14 +955,28 @@
         log_totals = turned(log_totals)
         group_loss = jnp.sum(turned(losses) * group_mask)
         pair_logs = links.chip(log_totals)
-        factors = jnp.exp(high - log_totals)
+
+        def factors(highs, part):
+            return jnp.exp(highs - log_totals[part, None]) * group_weights[part, None]
+
+        near_rows, far_rows = slice(0, line_rows), slice(line_rows, None)
         far_grads, far_part = head_states(
-            far_raised, factors[line_rows:], group_weights[line_rows:], far_targets, table_low
+            far_raised,
+            factors(far_highs, far_rows),
+            group_weights[far_rows],
+            far_targets,
+            table_low,
+            head_tile,
         )
         far_sent = far_part
         near_raised, far_part = lax.optimization_barrier((near_raised, far_part))
         near_grads, near_part = head_states(
-            near_raised, factors[:line_rows], group_weights[:line_rows], near_targets, table_low
+            near_raised,
+            factors(near_highs, near_rows),
+            group_weights[near_rows],
+            near_targets,
+            table_low,
+            head_tile,
         )
 
         table_operands = (
@@ -885,7 +994,7 @@
         received = links.core(sent)
         sent, near_part = lax.optimization_barrier((sent, near_part))
         grad_states = links.sum_across(near_part, far_sent)
-        grad_final = links.line_sum(grad_states.reshape(LINE, tok_rows, D))
+        grad_final = links.line_sum(grad_states.reshape(LINE, tok_rows, -1))[:, :D]
         kept = head_table(*table_operands, my_rep, vocab_tile)
         kept, grad_final = lax.optimization_barrier((kept, grad_final))
 
@@ -929,17 +1038,13 @@
             .transpose(1, 2, 0, 3)
             .reshape(KV_HEADS, group_size * tok_rows, HEAD_DIM)
         )
-        deltas = jnp.sum(grad_heads.astype(F32) * outputs, axis=-1, keepdims=True)
         grad_heads = jnp.pad(grad_heads, ((0, 0), (0, 0), (HEAD_DIM, 0)))
-        grad_chances = batched("htd,hsd->hts", grad_heads, kv)
-        grad_scores = (chances * (grad_chances - deltas)).astype(BF16)
-        grad_kv = batched("hts,htd->hsd", grad_scores, queries) * scale
-        grad_kv = grad_kv + batched("hts,htd->hsd", chances_low, grad_heads)
-        grad_kv = grad_kv.astype(BF16).reshape(KV_HEADS, n_rep, wide, tok_rows, 2 * HEAD_DIM)
-        grad_kv = links.rep_sum(grad_kv.transpose(1, 2, 0, 3, 4))
+        grad_queries, grad_kv = attend_back(queries, kv, bias, outputs, grad_heads)
+        grad_kv = grad_kv.reshape(n_rep, wide, KV_HEADS, tok_rows, 2 * HEAD_DIM)
+        grad_kv = links.rep_sum(grad_kv)
         far_kv = grad_kv[1:].astype(BF16).reshape(-1, tok_rows, 2 * HEAD_DIM)
         grad_kv = links.sum_across(grad_kv[0], far_kv).transpose(1, 0, 2)
-        grad_queries = batched("hts,hsd->htd", grad_scores, kv)[:, :, :HEAD_DIM] * scale
+        grad_queries = grad_queries[:, :, :HEAD_DIM]
         grad_rotated = jnp.concatenate(
             [
                 to_rows(grad_queries).reshape(tok_rows, HEADS, HEAD_DIM),
@@ -955,14 +1060,16 @@
         grad_gains = jnp.stack([grad_gain_one, grad_gain_two, grad_gain_three], 1)
         grad_gains = grad_gains + links.core(grad_gains)
         grad_gains = pad_blocks((grad_gains + links.chip(grad_gains)).T).T
-        packed = dot(packing, grad_values).astype(BF16).reshape(n_shard, room, D)
+        wide_values = jnp.pad(grad_values, ((0, 0), (0, -D % 128)))
+        packed = dot(packing, wide_values).astype(BF16).reshape(n_shard, room, -1)
         packed = lax.all_to_all(packed, "shard", 0, 0, tiled=True)
         grad_attn_in = weight_grad(pad_blocks(normed_one), mixed_mine, mixed_other)
         grad_attn = jnp.concatenate([grad_attn_out, grad_attn_in, grad_gains.astype(BF16)], 1)
         packed, grad_attn = lax.optimization_barrier((packed, grad_attn))
-        packed = packed.reshape(n_shard * room, D)
+        packed = packed.reshape(n_shard * room, -1)
         across = links.chip(packed)
-        grad_attn = links.scatter(grad_attn)[:in_rows].astype(BF16)
+        grad_attn = grad_attn.reshape((n_shard, -1) + grad_attn.shape[1:])
+        grad_attn = lax.all_to_all(grad_attn, "shard", 0, 0, tiled=True)
         across, grad_mlp = lax.optimization_barrier((across, grad_mlp))
         grad_mlp_in = grad_mlp[:in_rows, : 2 * units]
         grad_mlp_out = grad_mlp[:, 2 * units :].reshape(unit_part, D)
@@ -981,6 +1088,7 @@
         )
 
         table_squares, grad_attn = lax.optimization_barrier((table_squares, grad_attn))
+        grad_attn = jnp.sum(grad_attn.astype(F32), axis=0)[:in_rows].astype(BF16)
         gain_sum = grad_attn[:, -3:].astype(F32).T
         grad_attn = grad_attn[:, :-3]
         table_core = links.core(table_sum)
@@ -992,16 +1100,18 @@
         shared = jnp.concatenate([grad_attn, grad_mlp_out.reshape(in_rows, -1)], 1)[None]
         totals, shared = lax.optimization_barrier((totals, shared))
         totals = totals + links.chip(totals)
+        mlp_in_sum = mlp_in_sum.reshape(n_rep, in_rows, 2, n_shard, unit_part)
+        mlp_in_sum = mlp_in_sum.transpose(1, 2, 3, 0, 4).reshape(in_rows, 2 * FF)
         shared = jnp.concatenate([shared, links.chip(shared)])
-        totals, table_sum, shared = lax.optimization_barrier((totals, table_sum, shared))
+        totals, table_sum, shared, mlp_in_sum = lax.optimization_barrier(
+            (totals, table_sum, shared, mlp_in_sum)
+        )
         table_chip = links.chip(table_sum)
         shared = jnp.concatenate([shared, links.core(shared)])
         shared = jnp.stack(links.in_turn(shared, True))
         loss_sum = totals[1]
         squares = links.spread(jnp.broadcast_to(totals[0], (8, 128)))
         out_cols = D // n_rep
-        mlp_in_sum = mlp_in_sum.reshape(n_rep, in_rows, 2, n_shard, unit_part)
-        mlp_in_sum = mlp_in_sum.transpose(1, 2, 3, 0, 4).reshape(in_rows, 2 * FF)
         attn_cols = out_cols + 2 * in_cols // n_rep
         attn = jnp.stack([shared[r, :, :attn_cols] for r in (0, 2, 1, 3)], 1)
         mlp_out_sum = shared[:, :, attn_cols:].reshape(n_rep * unit_part, D)

time: 747 us -> 728 us (0.975)
  matrix products: 62.4 us -> 39.1 us
  Pallas kernels: 199 us -> 214 us
  waiting for transfers between devices: 148 us -> 139 us
  local copies, waits for them, and re-layouts: 118 us -> 110 us
    pallas_call x4 -> x6, Pallas kernels: 60.6 us -> 75.2 us  [the longest x2 30 us: head_states(): pl.pallas_call(functools.partial(states_kernel, tile=tile, each=each), gr...]
    dot_general x5 -> x0, matrix products: 14.2 us -> none  [batched(): return jnp.einsum(spec, a, b, preferred_element_type=F32)]
    all_to_all x1, waiting for transfers between devices: 11.2 us -> 0.01 us  [local(): grad_attn = lax.all_to_all(grad_attn, 'shard', 0, 0, tiled=True)]
    all_gather x1, waiting for transfers between devices: 0.01 us -> 9.84 us  [local(): mlp_in_sum = lax.all_gather(grad_mlp_in, 'rep')]
    reshape x6 -> x2, local copies, waits for them, and re-layouts: 8.91 us -> 1.32 us  [local(): grad_attn = grad_attn.reshape((n_shard, -1) + grad_attn.shape[1:])]
    sub x1 -> x0, matrix products: 7.51 us -> none  [local(): weights = jnp.exp(scores - highest)]
    unnamed x206 -> x190, local copies, waits for them, and re-layouts: 18.4 us -> 17.8 us
  transfers between devices with their start and end apart: 44 -> 44, of which waited for: 19 -> 16; matrix products, arithmetic and copies ran while one was open for 22% -> 21% of each run, Pallas kernels for 23% -> 25%
where the time goes in v5:
time: 728 us; the launch traced here: 719 us
  Pallas kernels  214 us (29%)
  waiting for transfers between devices  139 us (19%)
  local copies, waits for them, and re-layouts  110 us (15%)
  other arithmetic  78.1 us (11%)
  starting transfers between devices  63.8 us (9%)
  blocking collectives  46.2 us (6%)
  matrix products  39.1 us (5%)
  between operations  21.8 us (3%)
    pallas_call x3, Pallas kernels, adam(): pl.pallas_call(functools.partial(adam_kernel, rate=rate, count=count), gr...  62.3 us
    ppermute x13, waiting for transfers between devices, chip(): return lax.ppermute(value, 'rep', [(r, r ^ 2) for r in range(self.n_rep)])  48.6 us
    dot_general x20, matrix products, dot(): return lax.dot_general(a, b, (dims, ((), ())), preferred_element_type=F32)  38.7 us
    pallas_call x2, Pallas kernels, head_table(): pl.pallas_call(table_kernel, grid_spec=pltpu.PrefetchScalarGridSpec(num_s...  30.5 us
    pallas_call x2, Pallas kernels, head_states(): pl.pallas_call(functools.partial(states_kernel, tile=tile, each=each), gr...  30 us
    pallas_call x2, Pallas kernels, head_logits(): pl.pallas_call(functools.partial(logits_kernel, block=block), grid=(vocab...  28.4 us
    all_to_all x1, waiting for transfers between devices, local(): lax.all_to_all(looked.reshape(n_shard, room, D), 'shard', 0, 0, tiled=True)  22.7 us
    all_gather x1, blocking collectives, line_gather(): lax.all_gather(value, 'shard', axis_index_groups=self.lines, tiled=True)  20.6 us
  transfers between devices with their start and end apart: 44, of which 16 were waited for; matrix products, arithmetic and copies ran while one was open for 21% of the time, Pallas kernels for 25%

profile of v5, /device:TPU:0, one launch (start us, length us, event | category | flops | bytes accessed | tf_op | source)
XLA Modules:
  0.0 718.6 jit_solution(3851571552290967100)
XLA Ops:
  10.7 6.1 all-gather.4
  17.4 6.3 all-to-all-start.1
  33.1 20.0 %shard_map.412 = (bf16[960,6144]{1,0:T(8,128)(2,1)}, bf16[512,960]{1,0:T(8,128)(2,1)}) custom-call(s32[512,1]{1,0:T(8,128)} %broadcast_in_dim_reshape.4.ids_ref, f32[960,6144]{1,0:T(8,128)} %bitcast.311), custom_call_target="tpu_custom_call" | custom-call | flops 6039797760 | bytes 35389440 | tf_op jit(solution)/shard_map/pallas_call | solution.py:120
  60.2 5.9 convert_reduce_fusion.1
  66.0 22.7 %all-to-all-done.2 = bf16[8,64,960]{2,1,0:T(8,128)(2,1)S(1)} async-done(((bf16[8,64,960]{2,1,0:T(8,128)(2,1)}), bf16[8,64,960]{2,1,0:T(8,128)(2,1)S(1)}, u32[]{:S(2)}, u32[]{:S(2)}) %all-to-all-start.2) | async-done | bytes 983072 | tf_op jit(solution)/shard_map/all_to_all | solution.py:844
  89.3 6.9 conditional.2
  116.2 8.9 %collective-permute-done.1 = bf16[5,128,128]{1,2,0:T(8,128)(2,1)S(1)} collective-permute-done((bf16[5,128,128]{1,2,0:T(8,128)(2,1)S(1)}, bf16[5,128,128]{1,2,0:T(8,128)(2,1)S(1)}, u32[]{:S(2)}, u32[]{:S(2)}) %collective-permute-start.1) | collective-permute-done | bytes 163872 | tf_op jit(solution)/shard_map/ppermute | solution.py:662
  126.9 7.4 %collective-permute-done.2 = bf16[1,2,5,128,128]{3,4,2,1,0:T(8,128)(2,1)S(1)} collective-permute-done((bf16[1,2,5,128,128]{3,4,2,1,0:T(8,128)(2,1)S(1)}, bf16[1,2,5,128,128]{3,4,2,1,0:T(8,128)(2,1)S(1)}, u32[]{:S(2)}, u32[]{:S(2)}) %collective-permute-start.2) | collective-permute-done | bytes 327712 | tf_op jit(solution)/shard_map/ppermute | solution.py:718
  136.1 14.7 %all-gather.14.cloned.1.call-done = bf16[960,1920]{1,0:T(8,128)(2,1)} async-done(((bf16[120,1920]{1,0:T(8,128)(2,1)}), bf16[960,1920]{1,0:T(8,128)(2,1)}) %all-gather.14.cloned.1.call-update) | async-done | bytes 3686416 | tf_op jit(solution)/shard_map/all_gather | solution.py:843
  158.6 8.3 %shard_map.413.out_ref = f32[5,384,128]{2,1,0:T(8,128)} custom-call(bf16[5,384,128]{2,1,0:T(8,128)(2,1)} %pad.34.queries_ref, bf16[8,5,128,128]{3,2,1,0:T(8,128)(2,1)} %bitcast.370, f32[1,1024]{1,0:T(1,128)} %compare_select_fusion.1.bias_ref), custom_call_target="tpu_custom_call" | custom-call | flops 1006632960 | bytes 2621440 | tf_op jit(solution)/shard_map/pallas_call | solution.py:418
  173.7 10.1 %all_gather.42 = bf16[512,960]{0,1:T(8,128)(2,1)S(1)} all-gather(bf16[128,960]{0,1:T(8,128)(2,1)S(1)} %multiply_convert_fusion.3), channel_id=1, replica_groups=mesh['rep'=4,'shard'=8] {'rep'}, dimensions={0}, use_global_device_ids=true | all-gather | bytes 1228800 | tf_op jit(solution)/shard_map/all_gather | solution.py:921
  194.0 12.9 %all-to-all-done.4 = bf16[4,128,960]{1,2,0:T(8,128)(2,1)S(1)} async-done(((bf16[4,128,960]{1,2,0:T(8,128)(2,1)}), bf16[4,128,960]{1,2,0:T(8,128)(2,1)S(1)}, u32[]{:S(2)}, u32[]{:S(2)}) %all-to-all-start.4) | async-done | bytes 983072 | tf_op jit(solution)/shard_map/all_to_all | solution.py:709
  208.2 20.6 %all_gather.44 = bf16[512,960]{0,1:T(8,128)(2,1)S(1)} all-gather(bf16[128,960]{0,1:T(8,128)(2,1)S(1)} %multiply_convert_fusion.2), channel_id=1, replica_groups={{0,2,4,6},{1,3,5,7},{8,10,12,14},{9,11,13,15},{16,18,20,22},{17,19,21,2..., dimensions={0}, use_global_device_ids=true | all-gather | bytes 1228800 | tf_op jit(solution)/shard_map/all_gather | solution.py:676
  234.9 14.2 %shard_map.414 = (bf16[512,6144]{1,0:T(8,128)(2,1)}, f32[512,128]{1,0:T(8,128)}, f32[512,128]{1,0:T(8,128)}) custom-call(bf16[512,960]{1,0:T(8,128)(2,1)} %copy.456.states_ref, s32[512,1]{1,0:T(8,128)} %copy.457.targets_ref, bf16[960,6144]{1,0:T(8,128)(2,1)} %get-tuple-element.179.table_ref), custom_call_target="tpu_custom_call" | custom-call | flops 6039797760 | bytes 18087936 | tf_op jit(solution)/shard_map/pallas_call | solution.py:199
  252.6 14.2 %shard_map.415 = (bf16[512,6144]{1,0:T(8,128)(2,1)}, f32[512,128]{1,0:T(8,128)}, f32[512,128]{1,0:T(8,128)}) custom-call(bf16[512,960]{1,0:T(8,128)(2,1)} %copy.458.states_ref, s32[512,1]{1,0:T(8,128)} %copy.459.targets_ref, bf16[960,6144]{1,0:T(8,128)(2,1)} %get-tuple-element.179.table_ref), custom_call_target="tpu_custom_call" | custom-call | flops 6039797760 | bytes 18087936 | tf_op jit(solution)/shard_map/pallas_call | solution.py:199
  288.0 15.0 %shard_map.416 = (bf16[512,6144]{1,0:T(8,128)(2,1)}, bf16[512,1024]{1,0:T(8,128)(2,1)}) custom-call(bf16[512,6144]{1,0:T(8,128)(2,1)} %get-tuple-element.192.raised_ref, f32[512,128]{1,0:T(8,128)} %exponential_multiply_fusion.1.factors_ref, f32[512,1]{1,0:T(8,128)} %copy.465.weights_ref, s32[512,1]{1,0:T(8,128)} %copy.459.targets_ref, ...), custom_call_target="tpu_custom_call" | custom-call | flops 6039797760 | bytes 24379392 | tf_op jit(solution)/shard_map/pallas_call | solution.py:250
  305.9 15.0 %shard_map.417 = (bf16[512,6144]{1,0:T(8,128)(2,1)}, bf16[512,1024]{1,0:T(8,128)(2,1)}) custom-call(bf16[512,6144]{1,0:T(8,128)(2,1)} %get-tuple-element.197.raised_ref, f32[512,128]{1,0:T(8,128)} %exponential_multiply_fusion.factors_ref, f32[512,1]{1,0:T(8,128)} %copy.467.weights_ref, s32[512,1]{1,0:T(8,128)} %copy.457.targets_ref, ...), custom_call_target="tpu_custom_call" | custom-call | flops 6039797760 | bytes 24379392 | tf_op jit(solution)/shard_map/pallas_call | solution.py:250
  324.3 15.7 %shard_map.419 = bf16[960,1536]{1,0:T(8,128)(2,1)} custom-call(s32[1]{0:T(128)} %bitcast.40.part_ref, bf16[960,512]{1,0:T(8,128)(2,1)} %bitcast.325, bf16[960,512]{1,0:T(8,128)(2,1)} %bitcast.329, bf16[960,512]{1,0:T(8,128)(2,1)} %bitcast.331, bf16[960,512]{1,0:T(8,128)(2,1)} %bitcast.61.far_pair_t, bf16[512,6144]{1,0:T(8,128)(2,1)} %get-tuple-element.199.near_grads, ...), custom_call_target="tpu_custom_call" | custom-call | flops 9059696640 | bytes 14942208 | tf_op jit(solution)/shard_map/pallas_call | solution.py:332
  347.6 14.9 %shard_map.418.refs_4_ = bf16[960,1536]{1,0:T(8,128)(2,1)S(1)} custom-call(s32[1]{0:T(128)} %bitcast.13.part_ref, bf16[960,512]{1,0:T(8,128)(2,1)} %bitcast.326, bf16[960,512]{1,0:T(8,128)(2,1)} %bitcast.330, bf16[960,512]{1,0:T(8,128)(2,1)} %bitcast.332, bf16[960,512]{1,0:T(8,128)(2,1)} %bitcast.61.far_pair_t, ...), custom_call_target="tpu_custom_call" | custom-call | flops 9059696640 | bytes 14942208 | tf_op jit(solution)/shard_map/pallas_call | solution.py:332
  362.5 7.8 %all-to-all-done.6 = bf16[4,128,1024]{2,1,0:T(8,128)(2,1)} async-done(((bf16[4,128,1024]{2,1,0:T(8,128)(2,1)}), bf16[4,128,1024]{2,1,0:T(8,128)(2,1)}, u32[]{:S(2)}, u32[]{:S(2)}) %all-to-all-start.6) | async-done | bytes 1048608 | tf_op jit(solution)/shard_map/all_to_all | solution.py:679
  378.2 9.4 %all_gather.45 = bf16[512,960]{0,1:T(8,128)(2,1)S(1)} all-gather(bf16[128,960]{0,1:T(8,128)(2,1)S(1)} %fusion.60), channel_id=1, replica_groups=mesh['rep'=4,'shard'=8] {'rep'}, dimensions={0}, use_global_device_ids=true | all-gather | bytes 1228800 | tf_op jit(solution)/shard_map/all_gather | solution.py:1017
  397.4 6.3 constant_dynamic-slice_fusion.6
  427.3 8.5 %shard_map.420 = (f32[5,384,128]{2,1,0:T(8,128)}, bf16[8,5,128,128]{3,2,1,0:T(8,128)(2,1)}) custom-call(bf16[5,384,128]{2,1,0:T(8,128)(2,1)} %pad.34.queries_ref, bf16[8,5,128,128]{3,2,1,0:T(8,128)(2,1)} %bitcast.371, f32[1,1024]{1,0:T(1,128)} %compare_select_fusion.1.bias_ref, f32[5,384,128]{2,1,0:T(8,128)} %shard_map.413.out_ref, ...), custom_call_target="tpu_custom_call" | custom-call | flops 1006632960 | bytes 2621440 | tf_op jit(solution)/shard_map/pallas_call | solution.py:431
  494.7 18.3 %collective-permute-done.20 = f32[960,3]{0,1:T(4,128)S(1)} collective-permute-done((f32[960,3]{0,1:T(4,128)S(1)}, f32[960,3]{0,1:T(4,128)S(1)}, u32[]{:S(2)}, u32[]{:S(2)}) %collective-permute-start.20) | collective-permute-done | bytes 11552 | tf_op jit(solution)/shard_map/ppermute | solution.py:718
  530.2 14.8 %collective-permute-done.21.refs_1_ = bf16[512,1024]{1,0:T(8,128)(2,1)} collective-permute-done((bf16[512,1024]{1,0:T(8,128)(2,1)}, bf16[512,1024]{1,0:T(8,128)(2,1)}, u32[]{:S(2)}, u32[]{:S(2)}) %collective-permute-start.21) | collective-permute-done | bytes 1048608 | tf_op jit(solution)/shard_map/ppermute | solution.py:718
  555.2 9.8 %all-gather.16.cloned.1.call-done = bf16[480,1280]{1,0:T(8,128)(2,1)} async-done(((bf16[120,1280]{1,0:T(8,128)(2,1)}), bf16[480,1280]{1,0:T(8,128)(2,1)}) %all-gather.16.cloned.1.call-update) | async-done | bytes 1228816 | tf_op jit(solution)/shard_map/all_gather | solution.py:1076
  565.0 10.1 %shard_map.421 = (bf16[960,1536]{1,0:T(8,128)(2,1)}, f32[1,128]{1,0:T(1,128)S(1)}) custom-call(s32[4]{0:T(128)} %convert_reduce_fusion.5.starts_ref, s32[2048,1]{1,0:T(8,128)} %copy.491.ranks_ref, s32[2048,1]{1,0:T(8,128)} %copy.492.ids_ref, bf16[512,1024]{1,0:T(8,128)(2,1)} %bitcast.114.refs_0_, bf16[512,1024]{1,0:T(8,128)(2,1)} %collective-permute-done.21.refs_1_, ...), custom_call_target="tpu_custom_call" | custom-call | flops 503316480 | bytes 12779520 | tf_op jit(solution)/shard_map/pallas_call | solution.py:513
  607.1 6.4 all-to-all-start.9
  629.3 28.5 %shard_map.422 = (f32[960,6144]{1,0:T(8,128)}, f32[960,6144]{1,0:T(8,128)}, f32[960,6144]{1,0:T(8,128)}, bf16[960,6144]{1,0:T(8,128)(2,1)}) custom-call(s32[2]{0:T(128)} %pad_add_fusion.3.quarters_ref, f32[1]{0:T(128)} %bitcast.134.scale_ref, f32[960,6144]{1,0:T(8,128)} %bitcast.312, f32[960,6144]{1,0:T(8,128)} %bitcast.315, f32[960,6144]{1,0:T(8,128)} %bitcast.318, ...), custom_call_target="tpu_custom_call" | custom-call | tf_op jit(solution)/shard_map/pallas_call | solution.py:563
  658.8 16.0 %shard_map.423 = (f32[120,1600]{1,0:T(8,128)}, f32[120,1600]{1,0:T(8,128)}, f32[120,1600]{1,0:T(8,128)}, bf16[120,1600]{1,0:T(8,128)(2,1)}, f32[120,960]{1,0:T(8...) custom-call(f32[1]{0:T(128)} %bitcast.134.scale_ref, ...), custom_call_target="tpu_custom_call" | custom-call | tf_op jit(solution)/shard_map/pallas_call | solution.py:621
  675.2 16.9 %shard_map.424 = (f32[960,6144]{1,0:T(8,128)}, f32[960,6144]{1,0:T(8,128)}, f32[960,6144]{1,0:T(8,128)}, bf16[960,6144]{1,0:T(8,128)(2,1)}) custom-call(s32[1]{0:T(128)} %bitcast.39.quarters_ref, f32[1]{0:T(128)} %bitcast.134.scale_ref, f32[960,6144]{1,0:T(8,128)} %bitcast.313, ...), custom_call_target="tpu_custom_call", output_to_operand_aliasing={{0}: (6, {}), {1}: (7, {}), {2}: (8, {}), {3}: (9, {})} | custom-call | tf_op jit(solution)/shard_map/pallas_call | solution.py:563
  693.6 16.9 %shard_map.425 = (f32[960,6144]{1,0:T(8,128)}, f32[960,6144]{1,0:T(8,128)}, f32[960,6144]{1,0:T(8,128)}, bf16[960,6144]{1,0:T(8,128)(2,1)}) custom-call(s32[1]{0:T(128)} %bitcast.41.quarters_ref, f32[1]{0:T(128)} %bitcast.134.scale_ref, f32[960,6144]{1,0:T(8,128)} %bitcast.314, ...), custom_call_target="tpu_custom_call", output_to_operand_aliasing={{0}: (6, {}), {1}: (7, {}), {2}: (8, {}), {3}: (9, {})} | custom-call | tf_op jit(solution)/shard_map/pallas_call | solution.py:563
  (503 shorter events, 289.2 us)
Async XLA Ops:
  7.2 99.8 %all-gather.12.cloned.1.call-start = ((), (), s32[]{:S(2)}) async-start(), calls=%async_computation.12 | async-start | bytes 2764800 | tf_op jit(solution)/shard_map/all_gather | solution.py:809
  17.4 13.8 %all-to-all-start.1 = ((s32[8,4,3,128]{3,1,2,0:T(4,128)}), s32[8,4,3,128]{3,1,2,0:T(4,128)S(1)}, u32[]{:S(2)}, u32[]{:S(2)}) async-start(s32[8,4,3,128]{3,1,2,0:T(4,128)} %broadcast_in_dim.71), calls=%async_computation.1 | async-start | bytes 98304 | tf_op jit(solution)/shard_map/all_to_all | solution.py:691
  53.1 35.6 %all-to-all-start.2 = ((bf16[8,64,960]{2,1,0:T(8,128)(2,1)}), bf16[8,64,960]{2,1,0:T(8,128)(2,1)S(1)}, u32[]{:S(2)}, u32[]{:S(2)}) async-start(bf16[8,64,960]{2,1,0:T(8,128)(2,1)} %bitcast.375), calls=%async_computation.2 | async-start | bytes 2097152 | tf_op jit(solution)/shard_map/all_to_all | solution.py:844
  56.8 93.9 %all-gather.14.cloned.1.call-start = ((), (), s32[]{:S(2)}) async-start(), calls=%async_computation.13 | async-start | bytes 4147200 | tf_op jit(solution)/shard_map/all_gather | solution.py:843
  96.8 10.1 %all-to-all-start.3 = ((bf16[8,3,120]{2,1,0:T(4,128)(2,1)}), bf16[8,3,120]{2,1,0:T(4,128)(2,1)S(1)}, u32[]{:S(2)}, u32[]{:S(2)}) async-start(bf16[8,3,120]{2,1,0:T(4,128)(2,1)} %broadcast_in_dim.78), calls=%async_computation.3 | async-start | bytes 16384 | tf_op jit(solution)/shard_map/all_to_all | solution.py:691
  114.8 10.3 %collective-permute-start.1 = (bf16[5,128,128]{1,2,0:T(8,128)(2,1)S(1)}, bf16[5,128,128]{1,2,0:T(8,128)(2,1)S(1)}, u32[]{:S(2)}, u32[]{:S(2)}) collective-permute-start(bf16[5,128,128]{1,2,0:T(8,128)(2,1)S(1)} %get-tuple-element.383), channel_id=1, source_target_pairs={{0,1},{1,0},{2,3},{3,2},{4,5},{5,4},{6,7},{7,6},{8,9},{9,8},{10,11... | collective-permute-start | bytes 491528 | tf_op jit(solution)/shard_map/ppermute | solution.py:662
  135.2 20.7 %collective-permute-start.3 = (bf16[2,2,5,128,128]{3,4,2,1,0:T(8,128)(2,1)}, bf16[2,2,5,128,128]{3,4,2,1,0:T(8,128)(2,1)}, u32[]{:S(2)}, u32[]{:S(2)}) collective-permute-start(bf16[2,2,5,128,128]{3,4,2,1,0:T(8,128)(2,1)} %pad_maximum_fusion.9), channel_id=1, source_target_pairs={{0,8},{8,0},{16,24},{24,16},{1,9},{9,1},{17,25},{25,17},{2,10},{10... | collective-permute-start | bytes 1966088 | tf_op jit(solution)/shard_map/ppermute | solution.py:694
  189.7 17.2 %all-to-all-start.4 = ((bf16[4,128,960]{1,2,0:T(8,128)(2,1)}), bf16[4,128,960]{1,2,0:T(8,128)(2,1)S(1)}, u32[]{:S(2)}, u32[]{:S(2)}) async-start(bf16[4,128,960]{1,2,0:T(8,128)(2,1)} %convolution_convert_fusion.5), calls=%async_computation.4 | async-start | bytes 1966080 | tf_op jit(solution)/shard_map/all_to_all | solution.py:709
  228.8 22.5 %collective-permute-start.4 = (bf16[512,960]{0,1:T(8,128)(2,1)S(1)}, bf16[512,960]{0,1:T(8,128)(2,1)S(1)}, u32[]{:S(2)}, u32[]{:S(2)}) collective-permute-start(bf16[512,960]{0,1:T(8,128)(2,1)S(1)} %all_gather.44), channel_id=1, source_target_pairs={{0,1},{1,0},{2,3},{3,2},{4,5},{5,4},{6,7},{7,6},{8,9},{9,8},{10,11... | collective-permute-start | bytes 2949128 | tf_op jit(solution)/shard_map/ppermute | solution.py:662
  233.0 50.9 %collective-permute-start.5 = (bf16[512,960]{0,1:T(8,128)(2,1)S(1)}, bf16[512,960]{0,1:T(8,128)(2,1)S(1)}, u32[]{:S(2)}, u32[]{:S(2)}) collective-permute-start(bf16[512,960]{0,1:T(8,128)(2,1)S(1)} %all_gather.44), channel_id=1, source_target_pairs={{0,16},{8,24},{16,0},{24,8},{1,17},{9,25},{17,1},{25,9},{2,18},{10... | collective-permute-start | bytes 2949128 | tf_op jit(solution)/shard_map/ppermute | solution.py:718
  271.5 13.8 %all-to-all-start.5 = ((f32[8,3,2,4,128]{4,3,2,1,0:T(4,128)}), f32[8,3,2,4,128]{4,3,2,1,0:T(4,128)S(1)}, u32[]{:S(2)}, u32[]{:S(2)}) async-start(f32[8,3,2,4,128]{4,3,2,1,0:T(4,128)} %broadcast_in_dim.88), calls=%async_computation.5 | async-start | bytes 196608 | tf_op jit(solution)/shard_map/all_to_all | solution.py:691
  283.0 39.0 %collective-permute-start.6 = (bf16[512,960]{0,1:T(8,128)(2,1)S(1)}, bf16[512,960]{0,1:T(8,128)(2,1)}, u32[]{:S(2)}, u32[]{:S(2)}) collective-permute-start(bf16[512,960]{0,1:T(8,128)(2,1)S(1)} %collective-permute-done.4), channel_id=1, source_target_pairs={{0,16},{8,24},{16,0},{24,8},{1,17},{9,25},{17,1},{25,9},{2,18},{10... | collective-permute-start | bytes 2949128 | tf_op jit(solution)/shard_map/ppermute | solution.py:718
  285.9 35.0 %collective-permute-start.7 = (f32[1024]{0:T(1024)S(1)}, f32[1024]{0:T(1024)S(1)}, u32[]{:S(2)}, u32[]{:S(2)}) collective-permute-start(f32[1024]{0:T(1024)S(1)} %bitcast.447), channel_id=1, source_target_pairs={{0,16},{8,24},{16,0},{24,8},{1,17},{9,25},{17,1},{25,9},{2,18},{10... | collective-permute-start | bytes 12296 | tf_op jit(solution)/shard_map/ppermute | solution.py:718
  303.0 36.9 %collective-permute-start.8 = (bf16[512,1024]{1,0:T(8,128)(2,1)}, bf16[512,1024]{1,0:T(8,128)(2,1)}, u32[]{:S(2)}, u32[]{:S(2)}) collective-permute-start(bf16[512,1024]{1,0:T(8,128)(2,1)} %get-tuple-element.196), channel_id=1, source_target_pairs={{0,1},{1,0},{2,3},{3,2},{4,5},{5,4},{6,7},{7,6},{8,9},{9,8},{10,11... | collective-permute-start | bytes 3145736 | tf_op jit(solution)/shard_map/ppermute | solution.py:662
  342.5 27.7 %all-to-all-start.6 = ((bf16[4,128,1024]{2,1,0:T(8,128)(2,1)}), bf16[4,128,1024]{2,1,0:T(8,128)(2,1)}, u32[]{:S(2)}, u32[]{:S(2)}) async-start(bf16[4,128,1024]{2,1,0:T(8,128)(2,1)} %bitcast.83), calls=%async_computation.6 | async-start | bytes 2097152 | tf_op jit(solution)/shard_map/all_to_all | solution.py:679
  347.5 197.4 %reduce-scatter.2.cloned.1.call-start = ((), (), s32[]{:S(2)}) async-start(), calls=%async_computation.14 | async-start | bytes 4423680 | tf_op jit(solution)/shard_map/reduce_scatter | solution.py:1031
  451.8 10.4 %collective-permute-start.13 = (bf16[2,5,128,128]{2,3,1,0:T(8,128)(2,1)}, bf16[2,5,128,128]{2,3,1,0:T(8,128)(2,1)}, u32[]{:S(2)}, u32[]{:S(2)}) collective-permute-start(bf16[2,5,128,128]{2,3,1,0:T(8,128)(2,1)} %fusion.50), channel_id=1, source_target_pairs={{0,16},{8,24},{16,0},{24,8},{1,17},{9,25},{17,1},{25,9},{2,18},{10... | collective-permute-start | bytes 983048 | tf_op jit(solution)/shard_map/ppermute | solution.py:718
  473.4 13.7 %collective-permute-start.17 = (bf16[1024,800]{0,1:T(8,128)(2,1)}, bf16[1024,800]{0,1:T(8,128)(2,1)}, u32[]{:S(2)}, u32[]{:S(2)}) collective-permute-start(bf16[1024,800]{0,1:T(8,128)(2,1)} %convolution_convert_fusion.1), channel_id=1, source_target_pairs={{0,8},{8,0},{16,24},{24,16},{1,9},{9,1},{17,25},{25,17},{2,10},{10... | collective-permute-start | bytes 4915208 | tf_op jit(solution)/shard_map/ppermute | solution.py:694
  476.0 37.8 %collective-permute-start.16 = (bf16[1024,240]{0,1:T(8,128)(2,1)}, bf16[1024,240]{0,1:T(8,128)(2,1)}, u32[]{:S(2)}, u32[]{:S(2)}) collective-permute-start(bf16[1024,240]{0,1:T(8,128)(2,1)} %select_convert_fusion.1), channel_id=1, source_target_pairs={{0,16},{8,24},{16,0},{24,8},{1,17},{9,25},{17,1},{25,9},{2,18},{10... | collective-permute-start | bytes 1474568 | tf_op jit(solution)/shard_map/ppermute | solution.py:718
  480.2 13.1 %collective-permute-start.19 = (f32[960,3]{0,1:T(4,128)}, f32[960,3]{0,1:T(4,128)}, u32[]{:S(2)}, u32[]{:S(2)}) collective-permute-start(f32[960,3]{0,1:T(4,128)} %pad_maximum_fusion.20), channel_id=1, source_target_pairs={{0,8},{8,0},{16,24},{24,16},{1,9},{9,1},{17,25},{25,17},{2,10},{10... | collective-permute-start | bytes 34568 | tf_op jit(solution)/shard_map/ppermute | solution.py:694
  482.8 37.1 %all-to-all-start.7 = ((bf16[8,64,1024]{2,1,0:T(8,128)(2,1)}), bf16[8,64,1024]{2,1,0:T(8,128)(2,1)}, u32[]{:S(2)}, u32[]{:S(2)}) async-start(bf16[8,64,1024]{2,1,0:T(8,128)(2,1)} %bitcast.339), calls=%async_computation.7 | async-start | bytes 2097152 | tf_op jit(solution)/shard_map/all_to_all | solution.py:1065
  491.8 23.9 %collective-permute-start.18 = (bf16[1024,400]{0,1:T(8,128)(2,1)}, bf16[1024,400]{0,1:T(8,128)(2,1)}, u32[]{:S(2)}, u32[]{:S(2)}) collective-permute-start(bf16[1024,400]{0,1:T(8,128)(2,1)} %select_convert_fusion), channel_id=1, source_target_pairs={{0,16},{8,24},{16,0},{24,8},{1,17},{9,25},{17,1},{25,9},{2,18},{10... | collective-permute-start | bytes 2457608 | tf_op jit(solution)/shard_map/ppermute | solution.py:718
  494.0 18.9 %collective-permute-start.20 = (f32[960,3]{0,1:T(4,128)S(1)}, f32[960,3]{0,1:T(4,128)S(1)}, u32[]{:S(2)}, u32[]{:S(2)}) collective-permute-start(f32[960,3]{0,1:T(4,128)S(1)} %fusion.109), channel_id=1, source_target_pairs={{0,16},{8,24},{16,0},{24,8},{1,17},{9,25},{17,1},{25,9},{2,18},{10... | collective-permute-start | bytes 34568 | tf_op jit(solution)/shard_map/ppermute | solution.py:718
  494.7 56.0 %collective-permute-start.9 = (bf16[960,1536]{1,0:T(8,128)(2,1)}, bf16[960,1536]{1,0:T(8,128)(2,1)}, u32[]{:S(2)}, u32[]{:S(2)}) collective-permute-start(bf16[960,1536]{1,0:T(8,128)(2,1)} %shard_map.419), channel_id=1, source_target_pairs={{0,8},{8,0},{16,24},{24,16},{1,9},{9,1},{17,25},{25,17},{2,10},{10... | collective-permute-start | bytes 8847368 | tf_op jit(solution)/shard_map/ppermute | solution.py:694
  519.9 25.1 %collective-permute-start.21 = (bf16[512,1024]{1,0:T(8,128)(2,1)}, bf16[512,1024]{1,0:T(8,128)(2,1)}, u32[]{:S(2)}, u32[]{:S(2)}) collective-permute-start(bf16[512,1024]{1,0:T(8,128)(2,1)} %bitcast.114.refs_0_), channel_id=1, source_target_pairs={{0,16},{8,24},{16,0},{24,8},{1,17},{9,25},{17,1},{25,9},{2,18},{10... | collective-permute-start | bytes 3145736 | tf_op jit(solution)/shard_map/ppermute | solution.py:718
  524.4 52.6 %all-to-all-start.8 = ((bf16[8,128,643]{1,2,0:T(8,128)(2,1)}), bf16[8,128,643]{1,2,0:T(8,128)(2,1)}, u32[]{:S(2)}, u32[]{:S(2)}) async-start(bf16[8,128,643]{1,2,0:T(8,128)(2,1)} %copy.494), calls=%async_computation.9 | async-start | bytes 2654208 | tf_op jit(solution)/shard_map/all_to_all | solution.py:1072
  530.1 34.9 %all-gather.16.cloned.1.call-start = ((), (), s32[]{:S(2)}) async-start(), calls=%async_computation.15 | async-start | bytes 1536000 | tf_op jit(solution)/shard_map/all_gather | solution.py:1076
  587.1 11.4 %collective-permute-start.26 = (bf16[1,120,1280]{1,2,0:T(8,128)(2,1)S(1)}, bf16[1,120,1280]{1,2,0:T(8,128)(2,1)}, u32[]{:S(2)}, u32[]{:S(2)}) collective-permute-start(bf16[1,120,1280]{1,2,0:T(8,128)(2,1)S(1)} %maximum_bitcast_fusion.1), channel_id=1, source_target_pairs={{0,16},{8,24},{16,0},{24,8},{1,17},{9,25},{17,1},{25,9},{2,18},{10... | collective-permute-start | bytes 921608 | tf_op jit(solution)/shard_map/ppermute | solution.py:718
  594.7 34.6 %collective-permute-start.28 = (bf16[960,1536]{1,0:T(8,128)(2,1)S(1)}, bf16[960,1536]{1,0:T(8,128)(2,1)}, u32[]{:S(2)}, u32[]{:S(2)}) collective-permute-start(bf16[960,1536]{1,0:T(8,128)(2,1)S(1)} %get-tuple-element.230.refs_0_), channel_id=1, source_target_pairs={{0,8},{8,0},{16,24},{24,16},{1,9},{9,1},{17,25},{25,17},{2,10},{10... | collective-permute-start | bytes 8847368 | tf_op jit(solution)/shard_map/ppermute | solution.py:694
  600.4 74.5 %collective-permute-start.29 = (bf16[960,1536]{1,0:T(8,128)(2,1)S(1)}, bf16[960,1536]{1,0:T(8,128)(2,1)}, u32[]{:S(2)}, u32[]{:S(2)}) collective-permute-start(bf16[960,1536]{1,0:T(8,128)(2,1)S(1)} %get-tuple-element.230.refs_0_), channel_id=1, source_target_pairs={{0,16},{8,24},{16,0},{24,8},{1,17},{9,25},{17,1},{25,9},{2,18},{10... | collective-permute-start | bytes 8847368 | tf_op jit(solution)/shard_map/ppermute | solution.py:718
  607.1 17.6 %all-to-all-start.9 = ((f32[8,8,128]{2,1,0:T(8,128)}), f32[8,8,128]{2,1,0:T(8,128)S(1)}, u32[]{:S(2)}, u32[]{:S(2)}) async-start(f32[8,8,128]{2,1,0:T(8,128)} %broadcast_in_dim_broadcast_in_dim_broadcast_in_dim.3), calls=%async_computation.10 | async-start | bytes 65536 | tf_op jit(solution)/shard_map/all_to_all | solution.py:691
  674.9 17.2 %collective-permute-start.30 = (bf16[960,1536]{1,0:T(8,128)(2,1)}, bf16[960,1536]{1,0:T(8,128)(2,1)S(1)}, u32[]{:S(2)}, u32[]{:S(2)}) collective-permute-start(bf16[960,1536]{1,0:T(8,128)(2,1)} %collective-permute-done.29.refs_0_), channel_id=1, source_target_pairs={{0,8},{8,0},{16,24},{24,16},{1,9},{9,1},{17,25},{25,17},{2,10},{10... | collective-permute-start | bytes 8847368 | tf_op jit(solution)/shard_map/ppermute | solution.py:694
  (107 other events, 1196.3 us)
Sparse Core Ops, SparseCore 0:
  10.8 63.1 all-gather.11
  76.8 73.9 all-gather.13
  446.1 90.7 reduce-scatter.1
  546.9 18.1 all-gather.15

commit v6 on v5

--- a/solution.py
+++ b/solution.py
@@ -414,7 +414,7 @@
 
 
 def attend(queries, kv, bias):
-    rows, pairs, one, cost = attend_specs(queries, kv)
+    rows, pairs, one, _ = attend_specs(queries, kv)
     return pl.pallas_call(
         attend_kernel,
         grid=(queries.shape[0],),
@@ -422,7 +422,7 @@
         out_specs=rows,
         out_shape=jax.ShapeDtypeStruct(queries.shape, F32),
         compiler_params=params(),
-        cost_estimate=cost,
+        cost_estimate=pl.CostEstimate(flops=0, bytes_accessed=0, transcendentals=0),
     )(queries, kv, bias)
 
 
@@ -877,8 +877,6 @@
         attn_other = links.core(attn_mine)
         attn_in = (attn_mine[:, :in_cols], attn_other[:, :in_cols])
         attn_out = (attn_mine[:, in_cols:], attn_other[:, in_cols:])
-        mlp_in = mlp_all[:, : 2 * units]
-        mlp_out = mlp_all[:, 2 * units :].reshape(n_shard * unit_part, D)
         def times(value, pair):
             return dot(value, pair[0]), dot(value, pair[1])
 
@@ -906,6 +904,9 @@
         key_blocks = key_places.reshape(-1) // BLOCK
         bias = jnp.where(key_blocks <= positions[0] // BLOCK, 0.0, -1e30).astype(F32)[None]
         outputs = attend(queries, kv, bias)
+        outputs, mlp_all = lax.optimization_barrier((outputs, mlp_all))
+        mlp_in = mlp_all[:, : 2 * units]
+        mlp_out = mlp_all[:, 2 * units :].reshape(n_shard * unit_part, D)
 
         def to_rows(heads):
             return (

time: 728 us -> 717 us (0.985)
  waiting for transfers between devices: 139 us -> 128 us
    all_gather x1, waiting for transfers between devices: 14.7 us -> 3.68 us  [local(): mlp_all = lax.all_gather(mlp_part, 'shard', tiled=True)]
    unnamed x190 -> x186, local copies, waits for them, and re-layouts: 17.8 us -> 17.8 us
  transfers between devices with their start and end apart: 44 -> 44, of which waited for: 16 -> 17; matrix products, arithmetic and copies ran while one was open for 21% -> 21% of each run, Pallas kernels for 25% -> 27%
where the time goes in v6:
time: 717 us; the launch traced here: 706 us
  Pallas kernels  214 us (30%)
  waiting for transfers between devices  128 us (18%)
  local copies, waits for them, and re-layouts  109 us (15%)
  other arithmetic  77.2 us (11%)
  starting transfers between devices  62.6 us (9%)
  blocking collectives  46.8 us (7%)
  matrix products  41.1 us (6%)
  between operations  21.8 us (3%)
    pallas_call x3, Pallas kernels, adam(): pl.pallas_call(functools.partial(adam_kernel, rate=rate, count=count), gr...  62.3 us
    ppermute x13, waiting for transfers between devices, chip(): return lax.ppermute(value, 'rep', [(r, r ^ 2) for r in range(self.n_rep)])  49 us
    dot_general x20, matrix products, dot(): return lax.dot_general(a, b, (dims, ((), ())), preferred_element_type=F32)  40.7 us
    pallas_call x2, Pallas kernels, head_table(): pl.pallas_call(table_kernel, grid_spec=pltpu.PrefetchScalarGridSpec(num_s...  30.5 us
    pallas_call x2, Pallas kernels, head_states(): pl.pallas_call(functools.partial(states_kernel, tile=tile, each=each), gr...  30 us
    pallas_call x2, Pallas kernels, head_logits(): pl.pallas_call(functools.partial(logits_kernel, block=block), grid=(vocab...  28.4 us
    all_to_all x1, waiting for transfers between devices, local(): lax.all_to_all(looked.reshape(n_shard, room, D), 'shard', 0, 0, tiled=True)  22.7 us
    all_gather x1, blocking collectives, line_gather(): lax.all_gather(value, 'shard', axis_index_groups=self.lines, tiled=True)  20.6 us
  transfers between devices with their start and end apart: 44, of which 17 were waited for; matrix products, arithmetic and copies ran while one was open for 21% of the time, Pallas kernels for 27%

profile of v6, /device:TPU:0, one launch (start us, length us, event | category | flops | bytes accessed | tf_op | source)
XLA Modules:
  0.0 706.4 jit_solution(9895639331299869323)
XLA Ops:
  10.7 6.1 all-gather.4
  17.4 6.3 all-to-all-start.1
  33.1 20.0 %shard_map.412 = (bf16[960,6144]{1,0:T(8,128)(2,1)}, bf16[512,960]{1,0:T(8,128)(2,1)}) custom-call(s32[512,1]{1,0:T(8,128)} %broadcast_in_dim_reshape.4.ids_ref, f32[960,6144]{1,0:T(8,128)} %bitcast.311), custom_call_target="tpu_custom_call" | custom-call | flops 6039797760 | bytes 35389440 | tf_op jit(solution)/shard_map/pallas_call | solution.py:120
  60.2 5.8 convert_reduce_fusion.1
  66.0 22.7 %all-to-all-done.2 = bf16[8,64,960]{2,1,0:T(8,128)(2,1)S(1)} async-done(((bf16[8,64,960]{2,1,0:T(8,128)(2,1)}), bf16[8,64,960]{2,1,0:T(8,128)(2,1)S(1)}, u32[]{:S(2)}, u32[]{:S(2)}) %all-to-all-start.2) | async-done | bytes 983072 | tf_op jit(solution)/shard_map/all_to_all | solution.py:844
  89.3 6.3 conditional.2
  115.7 9.0 %collective-permute-done.1 = bf16[5,128,128]{1,2,0:T(8,128)(2,1)S(1)} collective-permute-done((bf16[5,128,128]{1,2,0:T(8,128)(2,1)S(1)}, bf16[5,128,128]{1,2,0:T(8,128)(2,1)S(1)}, u32[]{:S(2)}, u32[]{:S(2)}) %collective-permute-start.1) | collective-permute-done | bytes 163872 | tf_op jit(solution)/shard_map/ppermute | solution.py:662
  126.5 7.4 %collective-permute-done.2 = bf16[1,2,5,128,128]{3,4,2,1,0:T(8,128)(2,1)S(1)} collective-permute-done((bf16[1,2,5,128,128]{3,4,2,1,0:T(8,128)(2,1)S(1)}, bf16[1,2,5,128,128]{3,4,2,1,0:T(8,128)(2,1)S(1)}, u32[]{:S(2)}, u32[]{:S(2)}) %collective-permute-start.2) | collective-permute-done | bytes 327712 | tf_op jit(solution)/shard_map/ppermute | solution.py:718
  139.0 8.3 %shard_map.413.out_ref = f32[5,384,128]{2,1,0:T(8,128)} custom-call(bf16[5,384,128]{2,1,0:T(8,128)(2,1)} %pad.34.queries_ref, bf16[8,5,128,128]{3,2,1,0:T(8,128)(2,1)} %bitcast.337, f32[1,1024]{1,0:T(1,128)} %compare_select_fusion.1.bias_ref), custom_call_target="tpu_custom_call" | custom-call | tf_op jit(solution)/shard_map/pallas_call | solution.py:418
  157.6 10.7 %all_gather.43 = bf16[512,960]{0,1:T(8,128)(2,1)} all-gather(bf16[128,960]{0,1:T(8,128)(2,1)S(1)} %multiply_convert_fusion.3), channel_id=1, replica_groups=mesh['rep'=4,'shard'=8] {'rep'}, dimensions={0}, use_global_device_ids=true | all-gather | bytes 1228800 | tf_op jit(solution)/shard_map/all_gather | solution.py:922
  183.2 12.9 %all-to-all-done.4 = bf16[4,128,960]{1,2,0:T(8,128)(2,1)S(1)} async-done(((bf16[4,128,960]{1,2,0:T(8,128)(2,1)}), bf16[4,128,960]{1,2,0:T(8,128)(2,1)S(1)}, u32[]{:S(2)}, u32[]{:S(2)}) %all-to-all-start.4) | async-done | bytes 983072 | tf_op jit(solution)/shard_map/all_to_all | solution.py:709
  197.4 20.6 %all_gather.44 = bf16[512,960]{0,1:T(8,128)(2,1)S(1)} all-gather(bf16[128,960]{0,1:T(8,128)(2,1)S(1)} %multiply_convert_fusion.2), channel_id=1, replica_groups={{0,2,4,6},{1,3,5,7},{8,10,12,14},{9,11,13,15},{16,18,20,22},{17,19,21,2..., dimensions={0}, use_global_device_ids=true | all-gather | bytes 1228800 | tf_op jit(solution)/shard_map/all_gather | solution.py:676
  224.0 14.2 %shard_map.414 = (bf16[512,6144]{1,0:T(8,128)(2,1)}, f32[512,128]{1,0:T(8,128)}, f32[512,128]{1,0:T(8,128)}) custom-call(bf16[512,960]{1,0:T(8,128)(2,1)} %copy.456.states_ref, s32[512,1]{1,0:T(8,128)} %copy.457.targets_ref, bf16[960,6144]{1,0:T(8,128)(2,1)} %get-tuple-element.181.table_ref), custom_call_target="tpu_custom_call" | custom-call | flops 6039797760 | bytes 18087936 | tf_op jit(solution)/shard_map/pallas_call | solution.py:199
  241.8 14.2 %shard_map.415 = (bf16[512,6144]{1,0:T(8,128)(2,1)}, f32[512,128]{1,0:T(8,128)}, f32[512,128]{1,0:T(8,128)}) custom-call(bf16[512,960]{1,0:T(8,128)(2,1)} %copy.458.states_ref, s32[512,1]{1,0:T(8,128)} %copy.459.targets_ref, bf16[960,6144]{1,0:T(8,128)(2,1)} %get-tuple-element.181.table_ref), custom_call_target="tpu_custom_call" | custom-call | flops 6039797760 | bytes 18087936 | tf_op jit(solution)/shard_map/pallas_call | solution.py:199
  277.1 15.0 %shard_map.416 = (bf16[512,6144]{1,0:T(8,128)(2,1)}, bf16[512,1024]{1,0:T(8,128)(2,1)}) custom-call(bf16[512,6144]{1,0:T(8,128)(2,1)} %get-tuple-element.196.raised_ref, f32[512,128]{1,0:T(8,128)} %exponential_multiply_fusion.1.factors_ref, f32[512,1]{1,0:T(8,128)} %copy.465.weights_ref, s32[512,1]{1,0:T(8,128)} %copy.459.targets_ref, ...), custom_call_target="tpu_custom_call" | custom-call | flops 6039797760 | bytes 24379392 | tf_op jit(solution)/shard_map/pallas_call | solution.py:250
  295.1 15.0 %shard_map.417 = (bf16[512,6144]{1,0:T(8,128)(2,1)}, bf16[512,1024]{1,0:T(8,128)(2,1)}) custom-call(bf16[512,6144]{1,0:T(8,128)(2,1)} %get-tuple-element.201.raised_ref, f32[512,128]{1,0:T(8,128)} %exponential_multiply_fusion.factors_ref, f32[512,1]{1,0:T(8,128)} %copy.467.weights_ref, s32[512,1]{1,0:T(8,128)} %copy.457.targets_ref, ...), custom_call_target="tpu_custom_call" | custom-call | flops 6039797760 | bytes 24379392 | tf_op jit(solution)/shard_map/pallas_call | solution.py:250
  313.4 15.7 %shard_map.419 = bf16[960,1536]{1,0:T(8,128)(2,1)} custom-call(s32[1]{0:T(128)} %bitcast.40.part_ref, bf16[960,512]{1,0:T(8,128)(2,1)} %bitcast.325, bf16[960,512]{1,0:T(8,128)(2,1)} %bitcast.329, bf16[960,512]{1,0:T(8,128)(2,1)} %bitcast.331, bf16[960,512]{1,0:T(8,128)(2,1)} %bitcast.61.far_pair_t, bf16[512,6144]{1,0:T(8,128)(2,1)} %get-tuple-element.203.near_grads, ...), custom_call_target="tpu_custom_call" | custom-call | flops 9059696640 | bytes 14942208 | tf_op jit(solution)/shard_map/pallas_call | solution.py:332
  336.7 14.9 %shard_map.418.refs_4_ = bf16[960,1536]{1,0:T(8,128)(2,1)S(1)} custom-call(s32[1]{0:T(128)} %bitcast.13.part_ref, bf16[960,512]{1,0:T(8,128)(2,1)} %bitcast.326, bf16[960,512]{1,0:T(8,128)(2,1)} %bitcast.330, bf16[960,512]{1,0:T(8,128)(2,1)} %bitcast.332, bf16[960,512]{1,0:T(8,128)(2,1)} %bitcast.61.far_pair_t, ...), custom_call_target="tpu_custom_call" | custom-call | flops 9059696640 | bytes 14942208 | tf_op jit(solution)/shard_map/pallas_call | solution.py:332
  351.6 7.8 %all-to-all-done.6 = bf16[4,128,1024]{2,1,0:T(8,128)(2,1)} async-done(((bf16[4,128,1024]{2,1,0:T(8,128)(2,1)}), bf16[4,128,1024]{2,1,0:T(8,128)(2,1)}, u32[]{:S(2)}, u32[]{:S(2)}) %all-to-all-start.6) | async-done | bytes 1048608 | tf_op jit(solution)/shard_map/all_to_all | solution.py:679
  367.3 9.4 %all_gather.45 = bf16[512,960]{0,1:T(8,128)(2,1)S(1)} all-gather(bf16[128,960]{0,1:T(8,128)(2,1)S(1)} %fusion.60), channel_id=1, replica_groups=mesh['rep'=4,'shard'=8] {'rep'}, dimensions={0}, use_global_device_ids=true | all-gather | bytes 1228800 | tf_op jit(solution)/shard_map/all_gather | solution.py:1018
  386.6 6.3 constant_dynamic-slice_fusion.6
  416.4 8.5 %shard_map.420 = (f32[5,384,128]{2,1,0:T(8,128)}, bf16[8,5,128,128]{3,2,1,0:T(8,128)(2,1)}) custom-call(bf16[5,384,128]{2,1,0:T(8,128)(2,1)} %pad.34.queries_ref, bf16[8,5,128,128]{3,2,1,0:T(8,128)(2,1)} %bitcast.338, f32[1,1024]{1,0:T(1,128)} %compare_select_fusion.1.bias_ref, f32[5,384,128]{2,1,0:T(8,128)} %shard_map.413.out_ref, ...), custom_call_target="tpu_custom_call" | custom-call | flops 1006632960 | bytes 2621440 | tf_op jit(solution)/shard_map/pallas_call | solution.py:431
  454.8 5.5 collective-permute-done.14
  484.0 18.3 %collective-permute-done.20 = f32[960,3]{0,1:T(4,128)S(1)} collective-permute-done((f32[960,3]{0,1:T(4,128)S(1)}, f32[960,3]{0,1:T(4,128)S(1)}, u32[]{:S(2)}, u32[]{:S(2)}) %collective-permute-start.20) | collective-permute-done | bytes 11552 | tf_op jit(solution)/shard_map/ppermute | solution.py:718
  513.4 5.7 all-to-all-start.8
  519.2 15.2 %collective-permute-done.21.refs_1_ = bf16[512,1024]{1,0:T(8,128)(2,1)} collective-permute-done((bf16[512,1024]{1,0:T(8,128)(2,1)}, bf16[512,1024]{1,0:T(8,128)(2,1)}, u32[]{:S(2)}, u32[]{:S(2)}) %collective-permute-start.21) | collective-permute-done | bytes 1048608 | tf_op jit(solution)/shard_map/ppermute | solution.py:718
  544.6 9.5 %all-gather.16.cloned.1.call-done = bf16[480,1280]{1,0:T(8,128)(2,1)} async-done(((bf16[120,1280]{1,0:T(8,128)(2,1)}), bf16[480,1280]{1,0:T(8,128)(2,1)}) %all-gather.16.cloned.1.call-update) | async-done | bytes 1228816 | tf_op jit(solution)/shard_map/all_gather | solution.py:1077
  554.1 10.1 %shard_map.421 = (bf16[960,1536]{1,0:T(8,128)(2,1)}, f32[1,128]{1,0:T(1,128)S(1)}) custom-call(s32[4]{0:T(128)} %convert_reduce_fusion.5.starts_ref, s32[2048,1]{1,0:T(8,128)} %copy.491.ranks_ref, s32[2048,1]{1,0:T(8,128)} %copy.492.ids_ref, bf16[512,1024]{1,0:T(8,128)(2,1)} %bitcast.114.refs_0_, bf16[512,1024]{1,0:T(8,128)(2,1)} %collective-permute-done.21.refs_1_, ...), custom_call_target="tpu_custom_call" | custom-call | flops 503316480 | bytes 12779520 | tf_op jit(solution)/shard_map/pallas_call | solution.py:513
  617.1 28.5 %shard_map.422 = (f32[960,6144]{1,0:T(8,128)}, f32[960,6144]{1,0:T(8,128)}, f32[960,6144]{1,0:T(8,128)}, bf16[960,6144]{1,0:T(8,128)(2,1)}) custom-call(s32[2]{0:T(128)} %pad_add_fusion.3.quarters_ref, f32[1]{0:T(128)} %bitcast.134.scale_ref, f32[960,6144]{1,0:T(8,128)} %bitcast.312, f32[960,6144]{1,0:T(8,128)} %bitcast.315, f32[960,6144]{1,0:T(8,128)} %bitcast.318, ...), custom_call_target="tpu_custom_call" | custom-call | tf_op jit(solution)/shard_map/pallas_call | solution.py:563
  646.6 16.0 %shard_map.423 = (f32[120,1600]{1,0:T(8,128)}, f32[120,1600]{1,0:T(8,128)}, f32[120,1600]{1,0:T(8,128)}, bf16[120,1600]{1,0:T(8,128)(2,1)}, f32[120,960]{1,0:T(8...) custom-call(f32[1]{0:T(128)} %bitcast.134.scale_ref, ...), custom_call_target="tpu_custom_call" | custom-call | tf_op jit(solution)/shard_map/pallas_call | solution.py:621
  663.0 16.9 %shard_map.424 = (f32[960,6144]{1,0:T(8,128)}, f32[960,6144]{1,0:T(8,128)}, f32[960,6144]{1,0:T(8,128)}, bf16[960,6144]{1,0:T(8,128)(2,1)}) custom-call(s32[1]{0:T(128)} %bitcast.39.quarters_ref, f32[1]{0:T(128)} %bitcast.134.scale_ref, f32[960,6144]{1,0:T(8,128)} %bitcast.313, ...), custom_call_target="tpu_custom_call", output_to_operand_aliasing={{0}: (6, {}), {1}: (7, {}), {2}: (8, {}), {3}: (9, {})} | custom-call | tf_op jit(solution)/shard_map/pallas_call | solution.py:563
  681.4 16.9 %shard_map.425 = (f32[960,6144]{1,0:T(8,128)}, f32[960,6144]{1,0:T(8,128)}, f32[960,6144]{1,0:T(8,128)}, bf16[960,6144]{1,0:T(8,128)(2,1)}) custom-call(s32[1]{0:T(128)} %bitcast.41.quarters_ref, f32[1]{0:T(128)} %bitcast.134.scale_ref, f32[960,6144]{1,0:T(8,128)} %bitcast.314, ...), custom_call_target="tpu_custom_call", output_to_operand_aliasing={{0}: (6, {}), {1}: (7, {}), {2}: (8, {}), {3}: (9, {})} | custom-call | tf_op jit(solution)/shard_map/pallas_call | solution.py:563
  (499 shorter events, 286.6 us)
Async XLA Ops:
  7.2 99.2 %all-gather.12.cloned.1.call-start = ((), (), s32[]{:S(2)}) async-start(), calls=%async_computation.12 | async-start | bytes 2764800 | tf_op jit(solution)/shard_map/all_gather | solution.py:809
  17.4 13.8 %all-to-all-start.1 = ((s32[8,4,3,128]{3,1,2,0:T(4,128)}), s32[8,4,3,128]{3,1,2,0:T(4,128)S(1)}, u32[]{:S(2)}, u32[]{:S(2)}) async-start(s32[8,4,3,128]{3,1,2,0:T(4,128)} %broadcast_in_dim.71), calls=%async_computation.1 | async-start | bytes 98304 | tf_op jit(solution)/shard_map/all_to_all | solution.py:691
  53.1 35.6 %all-to-all-start.2 = ((bf16[8,64,960]{2,1,0:T(8,128)(2,1)}), bf16[8,64,960]{2,1,0:T(8,128)(2,1)S(1)}, u32[]{:S(2)}, u32[]{:S(2)}) async-start(bf16[8,64,960]{2,1,0:T(8,128)(2,1)} %bitcast.375), calls=%async_computation.2 | async-start | bytes 2097152 | tf_op jit(solution)/shard_map/all_to_all | solution.py:844
  56.8 94.1 %all-gather.14.cloned.1.call-start = ((), (), s32[]{:S(2)}) async-start(), calls=%async_computation.13 | async-start | bytes 4147200 | tf_op jit(solution)/shard_map/all_gather | solution.py:843
  96.2 10.1 %all-to-all-start.3 = ((bf16[8,3,120]{2,1,0:T(4,128)(2,1)}), bf16[8,3,120]{2,1,0:T(4,128)(2,1)S(1)}, u32[]{:S(2)}, u32[]{:S(2)}) async-start(bf16[8,3,120]{2,1,0:T(4,128)(2,1)} %broadcast_in_dim.78), calls=%async_computation.3 | async-start | bytes 16384 | tf_op jit(solution)/shard_map/all_to_all | solution.py:691
  114.4 10.4 %collective-permute-start.1 = (bf16[5,128,128]{1,2,0:T(8,128)(2,1)S(1)}, bf16[5,128,128]{1,2,0:T(8,128)(2,1)S(1)}, u32[]{:S(2)}, u32[]{:S(2)}) collective-permute-start(bf16[5,128,128]{1,2,0:T(8,128)(2,1)S(1)} %get-tuple-element.387), channel_id=1, source_target_pairs={{0,1},{1,0},{2,3},{3,2},{4,5},{5,4},{6,7},{7,6},{8,9},{9,8},{10,11... | collective-permute-start | bytes 491528 | tf_op jit(solution)/shard_map/ppermute | solution.py:662
  178.8 17.2 %all-to-all-start.4 = ((bf16[4,128,960]{1,2,0:T(8,128)(2,1)}), bf16[4,128,960]{1,2,0:T(8,128)(2,1)S(1)}, u32[]{:S(2)}, u32[]{:S(2)}) async-start(bf16[4,128,960]{1,2,0:T(8,128)(2,1)} %convolution_convert_fusion.5), calls=%async_computation.4 | async-start | bytes 1966080 | tf_op jit(solution)/shard_map/all_to_all | solution.py:709
  217.9 22.5 %collective-permute-start.4 = (bf16[512,960]{0,1:T(8,128)(2,1)S(1)}, bf16[512,960]{0,1:T(8,128)(2,1)S(1)}, u32[]{:S(2)}, u32[]{:S(2)}) collective-permute-start(bf16[512,960]{0,1:T(8,128)(2,1)S(1)} %all_gather.44), channel_id=1, source_target_pairs={{0,1},{1,0},{2,3},{3,2},{4,5},{5,4},{6,7},{7,6},{8,9},{9,8},{10,11... | collective-permute-start | bytes 2949128 | tf_op jit(solution)/shard_map/ppermute | solution.py:662
  222.1 50.9 %collective-permute-start.5 = (bf16[512,960]{0,1:T(8,128)(2,1)S(1)}, bf16[512,960]{0,1:T(8,128)(2,1)S(1)}, u32[]{:S(2)}, u32[]{:S(2)}) collective-permute-start(bf16[512,960]{0,1:T(8,128)(2,1)S(1)} %all_gather.44), channel_id=1, source_target_pairs={{0,16},{8,24},{16,0},{24,8},{1,17},{9,25},{17,1},{25,9},{2,18},{10... | collective-permute-start | bytes 2949128 | tf_op jit(solution)/shard_map/ppermute | solution.py:718
  260.6 13.8 %all-to-all-start.5 = ((f32[8,3,2,4,128]{4,3,2,1,0:T(4,128)}), f32[8,3,2,4,128]{4,3,2,1,0:T(4,128)S(1)}, u32[]{:S(2)}, u32[]{:S(2)}) async-start(f32[8,3,2,4,128]{4,3,2,1,0:T(4,128)} %broadcast_in_dim.88), calls=%async_computation.5 | async-start | bytes 196608 | tf_op jit(solution)/shard_map/all_to_all | solution.py:691
  272.2 39.0 %collective-permute-start.6 = (bf16[512,960]{0,1:T(8,128)(2,1)S(1)}, bf16[512,960]{0,1:T(8,128)(2,1)}, u32[]{:S(2)}, u32[]{:S(2)}) collective-permute-start(bf16[512,960]{0,1:T(8,128)(2,1)S(1)} %collective-permute-done.4), channel_id=1, source_target_pairs={{0,16},{8,24},{16,0},{24,8},{1,17},{9,25},{17,1},{25,9},{2,18},{10... | collective-permute-start | bytes 2949128 | tf_op jit(solution)/shard_map/ppermute | solution.py:718
  275.1 35.0 %collective-permute-start.7 = (f32[1024]{0:T(1024)S(1)}, f32[1024]{0:T(1024)S(1)}, u32[]{:S(2)}, u32[]{:S(2)}) collective-permute-start(f32[1024]{0:T(1024)S(1)} %bitcast.447), channel_id=1, source_target_pairs={{0,16},{8,24},{16,0},{24,8},{1,17},{9,25},{17,1},{25,9},{2,18},{10... | collective-permute-start | bytes 12296 | tf_op jit(solution)/shard_map/ppermute | solution.py:718
  292.2 36.9 %collective-permute-start.8 = (bf16[512,1024]{1,0:T(8,128)(2,1)}, bf16[512,1024]{1,0:T(8,128)(2,1)}, u32[]{:S(2)}, u32[]{:S(2)}) collective-permute-start(bf16[512,1024]{1,0:T(8,128)(2,1)} %get-tuple-element.200), channel_id=1, source_target_pairs={{0,1},{1,0},{2,3},{3,2},{4,5},{5,4},{6,7},{7,6},{8,9},{9,8},{10,11... | collective-permute-start | bytes 3145736 | tf_op jit(solution)/shard_map/ppermute | solution.py:662
  331.7 27.7 %all-to-all-start.6 = ((bf16[4,128,1024]{2,1,0:T(8,128)(2,1)}), bf16[4,128,1024]{2,1,0:T(8,128)(2,1)}, u32[]{:S(2)}, u32[]{:S(2)}) async-start(bf16[4,128,1024]{2,1,0:T(8,128)(2,1)} %bitcast.83), calls=%async_computation.6 | async-start | bytes 2097152 | tf_op jit(solution)/shard_map/all_to_all | solution.py:679
  336.7 197.7 %reduce-scatter.2.cloned.1.call-start = ((), (), s32[]{:S(2)}) async-start(), calls=%async_computation.14 | async-start | bytes 4423680 | tf_op jit(solution)/shard_map/reduce_scatter | solution.py:1032
  396.9 9.6 %collective-permute-start.11 = (bf16[128,960]{0,1:T(8,128)(2,1)}, bf16[128,960]{0,1:T(8,128)(2,1)}, u32[]{:S(2)}, u32[]{:S(2)}) collective-permute-start(bf16[128,960]{0,1:T(8,128)(2,1)} %fusion.59), channel_id=1, source_target_pairs={{0,16},{8,24},{16,0},{24,8},{1,17},{9,25},{17,1},{25,9},{2,18},{10... | collective-permute-start | bytes 737288 | tf_op jit(solution)/shard_map/ppermute | solution.py:718
  441.0 10.4 %collective-permute-start.13 = (bf16[2,5,128,128]{2,3,1,0:T(8,128)(2,1)}, bf16[2,5,128,128]{2,3,1,0:T(8,128)(2,1)}, u32[]{:S(2)}, u32[]{:S(2)}) collective-permute-start(bf16[2,5,128,128]{2,3,1,0:T(8,128)(2,1)} %fusion.50), channel_id=1, source_target_pairs={{0,16},{8,24},{16,0},{24,8},{1,17},{9,25},{17,1},{25,9},{2,18},{10... | collective-permute-start | bytes 983048 | tf_op jit(solution)/shard_map/ppermute | solution.py:718
  462.4 14.0 %collective-permute-start.17 = (bf16[1024,800]{0,1:T(8,128)(2,1)}, bf16[1024,800]{0,1:T(8,128)(2,1)}, u32[]{:S(2)}, u32[]{:S(2)}) collective-permute-start(bf16[1024,800]{0,1:T(8,128)(2,1)} %convolution_convert_fusion.1), channel_id=1, source_target_pairs={{0,8},{8,0},{16,24},{24,16},{1,9},{9,1},{17,25},{25,17},{2,10},{10... | collective-permute-start | bytes 4915208 | tf_op jit(solution)/shard_map/ppermute | solution.py:694
  465.0 38.2 %collective-permute-start.16 = (bf16[1024,240]{0,1:T(8,128)(2,1)}, bf16[1024,240]{0,1:T(8,128)(2,1)}, u32[]{:S(2)}, u32[]{:S(2)}) collective-permute-start(bf16[1024,240]{0,1:T(8,128)(2,1)} %select_convert_fusion.1), channel_id=1, source_target_pairs={{0,16},{8,24},{16,0},{24,8},{1,17},{9,25},{17,1},{25,9},{2,18},{10... | collective-permute-start | bytes 1474568 | tf_op jit(solution)/shard_map/ppermute | solution.py:718
  469.6 12.8 %collective-permute-start.19 = (f32[960,3]{0,1:T(4,128)}, f32[960,3]{0,1:T(4,128)}, u32[]{:S(2)}, u32[]{:S(2)}) collective-permute-start(f32[960,3]{0,1:T(4,128)} %pad_maximum_fusion.20), channel_id=1, source_target_pairs={{0,8},{8,0},{16,24},{24,16},{1,9},{9,1},{17,25},{25,17},{2,10},{10... | collective-permute-start | bytes 34568 | tf_op jit(solution)/shard_map/ppermute | solution.py:694
  472.1 37.0 %all-to-all-start.7 = ((bf16[8,64,1024]{2,1,0:T(8,128)(2,1)}), bf16[8,64,1024]{2,1,0:T(8,128)(2,1)}, u32[]{:S(2)}, u32[]{:S(2)}) async-start(bf16[8,64,1024]{2,1,0:T(8,128)(2,1)} %bitcast.341), calls=%async_computation.7 | async-start | bytes 2097152 | tf_op jit(solution)/shard_map/all_to_all | solution.py:1066
  481.2 23.9 %collective-permute-start.18 = (bf16[1024,400]{0,1:T(8,128)(2,1)}, bf16[1024,400]{0,1:T(8,128)(2,1)}, u32[]{:S(2)}, u32[]{:S(2)}) collective-permute-start(bf16[1024,400]{0,1:T(8,128)(2,1)} %select_convert_fusion), channel_id=1, source_target_pairs={{0,16},{8,24},{16,0},{24,8},{1,17},{9,25},{17,1},{25,9},{2,18},{10... | collective-permute-start | bytes 2457608 | tf_op jit(solution)/shard_map/ppermute | solution.py:718
  483.1 19.2 %collective-permute-start.20 = (f32[960,3]{0,1:T(4,128)S(1)}, f32[960,3]{0,1:T(4,128)S(1)}, u32[]{:S(2)}, u32[]{:S(2)}) collective-permute-start(f32[960,3]{0,1:T(4,128)S(1)} %fusion.109), channel_id=1, source_target_pairs={{0,16},{8,24},{16,0},{24,8},{1,17},{9,25},{17,1},{25,9},{2,18},{10... | collective-permute-start | bytes 34568 | tf_op jit(solution)/shard_map/ppermute | solution.py:718
  484.0 56.0 %collective-permute-start.9 = (bf16[960,1536]{1,0:T(8,128)(2,1)}, bf16[960,1536]{1,0:T(8,128)(2,1)}, u32[]{:S(2)}, u32[]{:S(2)}) collective-permute-start(bf16[960,1536]{1,0:T(8,128)(2,1)} %shard_map.419), channel_id=1, source_target_pairs={{0,8},{8,0},{16,24},{24,16},{1,9},{9,1},{17,25},{25,17},{2,10},{10... | collective-permute-start | bytes 8847368 | tf_op jit(solution)/shard_map/ppermute | solution.py:694
  509.2 25.2 %collective-permute-start.21 = (bf16[512,1024]{1,0:T(8,128)(2,1)}, bf16[512,1024]{1,0:T(8,128)(2,1)}, u32[]{:S(2)}, u32[]{:S(2)}) collective-permute-start(bf16[512,1024]{1,0:T(8,128)(2,1)} %bitcast.114.refs_0_), channel_id=1, source_target_pairs={{0,16},{8,24},{16,0},{24,8},{1,17},{9,25},{17,1},{25,9},{2,18},{10... | collective-permute-start | bytes 3145736 | tf_op jit(solution)/shard_map/ppermute | solution.py:718
  513.4 52.6 %all-to-all-start.8 = ((bf16[8,128,643]{1,2,0:T(8,128)(2,1)}), bf16[8,128,643]{1,2,0:T(8,128)(2,1)}, u32[]{:S(2)}, u32[]{:S(2)}) async-start(bf16[8,128,643]{1,2,0:T(8,128)(2,1)} %copy.494), calls=%async_computation.9 | async-start | bytes 2654208 | tf_op jit(solution)/shard_map/all_to_all | solution.py:1073
  519.2 34.9 %all-gather.16.cloned.1.call-start = ((), (), s32[]{:S(2)}) async-start(), calls=%async_computation.15 | async-start | bytes 1536000 | tf_op jit(solution)/shard_map/all_gather | solution.py:1077
  576.1 11.8 %collective-permute-start.26 = (bf16[1,120,1280]{1,2,0:T(8,128)(2,1)S(1)}, bf16[1,120,1280]{1,2,0:T(8,128)(2,1)}, u32[]{:S(2)}, u32[]{:S(2)}) collective-permute-start(bf16[1,120,1280]{1,2,0:T(8,128)(2,1)S(1)} %maximum_bitcast_fusion.1), channel_id=1, source_target_pairs={{0,16},{8,24},{16,0},{24,8},{1,17},{9,25},{17,1},{25,9},{2,18},{10... | collective-permute-start | bytes 921608 | tf_op jit(solution)/shard_map/ppermute | solution.py:718
  584.2 32.9 %collective-permute-start.28 = (bf16[960,1536]{1,0:T(8,128)(2,1)S(1)}, bf16[960,1536]{1,0:T(8,128)(2,1)}, u32[]{:S(2)}, u32[]{:S(2)}) collective-permute-start(bf16[960,1536]{1,0:T(8,128)(2,1)S(1)} %get-tuple-element.234.refs_0_), channel_id=1, source_target_pairs={{0,8},{8,0},{16,24},{24,16},{1,9},{9,1},{17,25},{25,17},{2,10},{10... | collective-permute-start | bytes 8847368 | tf_op jit(solution)/shard_map/ppermute | solution.py:694
  589.9 72.7 %collective-permute-start.29 = (bf16[960,1536]{1,0:T(8,128)(2,1)S(1)}, bf16[960,1536]{1,0:T(8,128)(2,1)}, u32[]{:S(2)}, u32[]{:S(2)}) collective-permute-start(bf16[960,1536]{1,0:T(8,128)(2,1)S(1)} %get-tuple-element.234.refs_0_), channel_id=1, source_target_pairs={{0,16},{8,24},{16,0},{24,8},{1,17},{9,25},{17,1},{25,9},{2,18},{10... | collective-permute-start | bytes 8847368 | tf_op jit(solution)/shard_map/ppermute | solution.py:718
  596.6 15.8 %all-to-all-start.9 = ((f32[8,8,128]{2,1,0:T(8,128)}), f32[8,8,128]{2,1,0:T(8,128)S(1)}, u32[]{:S(2)}, u32[]{:S(2)}) async-start(f32[8,8,128]{2,1,0:T(8,128)} %broadcast_in_dim_broadcast_in_dim_broadcast_in_dim.3), calls=%async_computation.10 | async-start | bytes 65536 | tf_op jit(solution)/shard_map/all_to_all | solution.py:691
  662.7 17.2 %collective-permute-start.30 = (bf16[960,1536]{1,0:T(8,128)(2,1)}, bf16[960,1536]{1,0:T(8,128)(2,1)S(1)}, u32[]{:S(2)}, u32[]{:S(2)}) collective-permute-start(bf16[960,1536]{1,0:T(8,128)(2,1)} %collective-permute-done.29.refs_0_), channel_id=1, source_target_pairs={{0,8},{8,0},{16,24},{24,16},{1,9},{9,1},{17,25},{25,17},{2,10},{10... | collective-permute-start | bytes 8847368 | tf_op jit(solution)/shard_map/ppermute | solution.py:694
  (105 other events, 1141.4 us)
Sparse Core Ops, SparseCore 0:
  10.8 63.1 all-gather.11
  76.8 74.0 all-gather.13
  435.2 90.6 reduce-scatter.1
  536.3 17.7 all-gather.15
